TPU v7x, 32 devices: a whole 2x2x4 slice. The times are simulated.
32 devices in a mesh: leaf: 8 (over z, y), probe: 4 (over x, core).
Axes of the slice: x: 2, y: 2, z: 4, core: 2. Of those that a mesh axis runs over, the one named last changes fastest.
Arguments:
- coords: float32 [3, 32768], P(None, 'leaf'), may hold values from 0 to 1
- weights: float32 [32768], P('leaf'), may hold values from 0.01 to 0.1
- omega: bfloat16 [256, 32768], P('probe', 'leaf'), may hold values from -6 to 6
- near_local: int32 [256, 24], P('leaf'), may hold values from 0 to 255, as said below
- far_pairs: int32 [2, 512], P(None, 'leaf'), may hold values from 0 to 255, as said below
- skel_rows: int32 [256, 32], P('leaf'), may hold values from 0 to 127, as said below
- parent_interp: bfloat16 [32, 256, 64], P('leaf'), may hold values from -0.375 to 0.375
Outputs:
- near_sample: float32 [256, 32768], P('probe', 'leaf')
- parent_sample: float32 [256, 2048], P('probe', 'leaf')
Inputs may be any that keep to these rules, and one draw needn't show every extreme that they name: `near_local`: entry 0 of leaf t's row is t itself; every other entry names a leaf of the same device as t (equal index // 32); repeats may occur. `far_pairs`: column c belongs to device c // 64: its source leaf lies on that device and its target leaf on another device. Of one device's 64 columns at most 16 have targets on any one other device, and one device receives exactly 16 from every other device. `skel_rows`: the 32 numbers of one leaf are distinct.
All inputs are finite; a program needn't handle non-finite values.
Results may differ from a plain program's by a relative error of at most 0.008.
Values may be sent and summed in bfloat16 or wider, within the bound.
No kernel may reach another device: no remote copies, remote signals or barrier semaphores. Data moves between devices by JAX's collectives and lax.ppermute only.
A program may use at most 64 MiB of HBM per device.

v0:
```python
import jax
import jax.numpy as jnp
from jax import lax
from jax.sharding import PartitionSpec as P

LEAF_PTS = 128
SK = 32
SK2 = 64
CHILD = 8
CAP = 16


DELTA_SQ = 0.0001
INV_FOUR_PI = 0.07957747154594767


def kernel_block(target_points, source_points, source_weights):
    delta_x = target_points[..., 0, :, None] - source_points[..., 0, None, :]
    delta_y = target_points[..., 1, :, None] - source_points[..., 1, None, :]
    delta_z = target_points[..., 2, :, None] - source_points[..., 2, None, :]
    dist_sq = delta_x * delta_x + delta_y * delta_y + delta_z * delta_z
    values = source_weights[..., None, :] * INV_FOUR_PI * lax.rsqrt(dist_sq + DELTA_SQ)
    return values.astype(jnp.bfloat16)


def per_device(coords, weights, omega, near_local, far_pairs, skel_rows, parent_interp):
    n_leaf = lax.axis_size("leaf")
    leaf_dev = coords.shape[1] // LEAF_PTS
    probe_dev = omega.shape[0]
    offset = lax.axis_index("leaf") * leaf_dev
    leaf_node_coords = coords.reshape(3, leaf_dev, LEAF_PTS).transpose(1, 0, 2)
    leaf_weights = weights.reshape(leaf_dev, LEAF_PTS)
    leaf_probes = omega.reshape(probe_dev, leaf_dev, LEAF_PTS).transpose(1, 0, 2)
    flat_probes = leaf_probes.reshape(leaf_dev, probe_dev * LEAF_PTS)
    probes_wide = leaf_probes.astype(jnp.float32)
    leaf_iota = jnp.arange(leaf_dev, dtype=jnp.int32)
    local_ids = near_local - offset
    counts = jnp.sum(
        (local_ids[:, :, None] == leaf_iota[None, None, :]).astype(jnp.float32), axis=1
    )
    block_size = max(1, min(leaf_dev, 128 // leaf_dev))

    def local_block(first_leaf):
        targets = lax.dynamic_slice_in_dim(leaf_node_coords, first_leaf, block_size, 0)
        count_rows = lax.dynamic_slice_in_dim(counts, first_leaf, block_size, 0)
        kernel = kernel_block(targets[:, None], leaf_node_coords[None], leaf_weights[None])
        scaled = kernel.astype(jnp.float32) * count_rows[:, :, None, None]
        return jnp.einsum("bjts,jps->bpt", scaled, probes_wide, precision=lax.Precision.HIGHEST)

    firsts = jnp.arange(0, leaf_dev, block_size, dtype=jnp.int32)
    local_sum = lax.map(local_block, firsts).reshape(leaf_dev, probe_dev, LEAF_PTS)
    source = far_pairs[0] - offset
    target = far_pairs[1]
    owner = target // leaf_dev
    indicator_matrix = (owner[:, None] == jnp.arange(n_leaf, dtype=jnp.int32)[None, :]).astype(
        jnp.int32
    )
    ranks = jnp.sum((jnp.cumsum(indicator_matrix, axis=0) - 1) * indicator_matrix, axis=1)
    slots = owner * CAP + ranks
    slot_count = n_leaf * CAP
    slot_hit = (slots[None, :] == jnp.arange(slot_count, dtype=jnp.int32)[:, None]).astype(
        jnp.int32
    )
    slot_valid = jnp.sum(slot_hit, axis=1)
    slot_source = jnp.sum(slot_hit * source[None, :], axis=1)
    slot_target = jnp.sum(slot_hit * target[None, :], axis=1)
    slot_owner = jnp.arange(slot_count, dtype=jnp.int32) // CAP
    requests = jnp.where(slot_valid > 0, slot_target - slot_owner * leaf_dev, -1).reshape(
        n_leaf, CAP
    )
    source_pick = (slot_source[:, None] == leaf_iota[None, :]).astype(jnp.bfloat16)
    slot_probes = jnp.dot(source_pick, flat_probes, preferred_element_type=jnp.float32)
    slot_probes = slot_probes.astype(jnp.bfloat16).reshape(slot_count, probe_dev, LEAF_PTS)
    slot_points = leaf_node_coords[slot_source]
    slot_weights = leaf_weights[slot_source]
    arrived = lax.all_to_all(requests, "leaf", split_axis=0, concat_axis=0, tiled=True)
    send_points = jnp.concatenate([slot_points, slot_weights[:, None, :]], axis=1)
    got_points = lax.all_to_all(
        send_points.reshape(n_leaf, CAP, 4, LEAF_PTS),
        "leaf",
        split_axis=0,
        concat_axis=0,
        tiled=True,
    )
    got_points = got_points.reshape(slot_count, 4, LEAF_PTS)
    got_probes = lax.all_to_all(
        slot_probes.reshape(n_leaf, CAP, probe_dev, LEAF_PTS),
        "leaf",
        split_axis=0,
        concat_axis=0,
        tiled=True,
    )
    got_probes = got_probes.reshape(slot_count, probe_dev, LEAF_PTS)
    own_points = leaf_node_coords[jnp.maximum(arrived, 0).reshape(-1)]
    kernel = kernel_block(own_points, got_points[:, :3], got_points[:, 3])
    partial_rows = jnp.einsum(
        "nts,nps->npt", kernel, got_probes, preferred_element_type=jnp.float32
    )
    incoming = lax.optimization_barrier(partial_rows.astype(jnp.bfloat16)).astype(jnp.float32)
    incoming = incoming.reshape(slot_count, probe_dev * LEAF_PTS)
    collect = (arrived.reshape(-1)[None, :] == leaf_iota[:, None]).astype(jnp.float32)
    far_sum = jnp.dot(
        collect, incoming, precision=lax.Precision.HIGHEST, preferred_element_type=jnp.float32
    )
    sampled_block = local_sum + far_sum.reshape(leaf_dev, probe_dev, LEAF_PTS)
    near_sample = sampled_block.transpose(1, 0, 2).reshape(probe_dev, leaf_dev * LEAF_PTS)
    selected_row_index = (
        jnp.arange(LEAF_PTS, dtype=jnp.int32)[None, :, None] == skel_rows[:, None, :]
    ).astype(jnp.float32)
    selected_entries = jnp.einsum(
        "yie,yea->yia", sampled_block, selected_row_index, precision=lax.Precision.HIGHEST
    ).astype(jnp.bfloat16)
    parent_dev = leaf_dev // CHILD
    stacked = selected_entries.reshape(parent_dev, CHILD, probe_dev, SK).transpose(0, 2, 1, 3)
    stacked = stacked.reshape(parent_dev, probe_dev, CHILD * SK)
    merged = jnp.einsum("pqc,pck->pqk", stacked, parent_interp, preferred_element_type=jnp.float32)
    energy = lax.psum(jnp.sum(merged * merged, axis=(1, 2)), "probe")
    factor = lax.rsqrt(energy / (SK2 * probe_dev * lax.axis_size("probe")) + 1e-06)
    parent_sample = (
        (merged * factor[:, None, None]).transpose(1, 0, 2).reshape(probe_dev, parent_dev * SK2)
    )
    return (near_sample, parent_sample)


def solution(mesh):
    return jax.shard_map(
        per_device,
        mesh=mesh,
        in_specs=(
            P(None, "leaf"),
            P("leaf"),
            P("probe", "leaf"),
            P("leaf", None),
            P(None, "leaf"),
            P("leaf", None),
            P("leaf", None, None),
        ),
        out_specs=(P("probe", "leaf"), P("probe", "leaf")),
        check_vma=False,
    )
```

profile of v0, /device:TPU:0, one launch (start us, length us, event | category | flops | bytes accessed | tf_op | source)
XLA Modules:
  0.0 182.9 jit_solution(12693781195605716126)
XLA Ops:
  3.4 7.3 %all-to-all-start = ((s32[8,1,16]{2,1,0:T(1,128)}), s32[8,1,16]{2,1,0:T(1,128)S(1)}, u32[]{:S(2)}, u32[]{:S(2)}) async-start(s32[8,1,16]{2,1,0:T(1,128)} %bitcast.22), calls=%async_computation | async-start | bytes 8192 | tf_op jit(solution)/shard_map/all_to_all | solution.py:76
  10.7 1.6 gather_fusion
  12.3 1.4 gather_fusion.1
  14.8 1.2 bitcast_convert_fusion
  17.1 5.7 %all-to-all-start.2 = ((f32[8,16,4,128]{3,2,1,0:T(4,128)}), f32[8,16,4,128]{3,2,1,0:T(4,128)S(1)}, u32[]{:S(2)}, u32[]{:S(2)}) async-start(f32[8,16,4,128]{3,2,1,0:T(4,128)} %pad_maximum_fusion), calls=%async_computation.2 | async-start | bytes 524288 | tf_op jit(solution)/shard_map/all_to_all | solution.py:78
  23.6 1.9 %copy.85 = bf16[16,8,64,128]{3,2,1,0:T(8,128)(2,1)} copy(bf16[16,8,64,128]{3,1,2,0:T(8,128)(2,1)S(1)} %fusion.27) | data formatting | bytes 4194304
  26.6 4.8 %all-to-all-done.2 = f32[8,16,4,128]{3,2,1,0:T(4,128)S(1)} async-done(((f32[8,16,4,128]{3,2,1,0:T(4,128)}), f32[8,16,4,128]{3,2,1,0:T(4,128)S(1)}, u32[]{:S(2)}, u32[]{:S(2)}) %all-to-all-start.2) | async-done | bytes 262176 | tf_op jit(solution)/shard_map/all_to_all | solution.py:78
  31.3 4.7 %all-to-all-start.1 = ((bf16[8,16,64,128]{3,2,1,0:T(8,128)(2,1)}), bf16[8,16,64,128]{3,2,1,0:T(8,128)(2,1)}, u32[]{:S(2)}, u32[]{:S(2)}) async-start(bf16[8,16,64,128]{3,2,1,0:T(8,128)(2,1)} %bitcast.67), calls=%async_computation.1 | async-start | bytes 4194304 | tf_op jit(solution)/shard_map/all_to_all | solution.py:86
  36.0 116.7 %while.10 = (s32[]{:T(128)}, f32[8,4,64,128]{3,1,0,2:T(4,128)}, f32[4096]{0:T(1024)S(1)}, s32[8]{0:T(128)S(1)}, f32[32,3,128]{2,0,1:T(8,128)S(1)}, /*index=5*/f3...) while((s32[]{:T(128)}, f32[8,4,64,128]{3,1,0,2:T(4,128)}, ...), condition=%wide.region_2.3_spmd, body=%wide.region_1.2_spmd.sunk | while | flops 1637879808 | bytes 1671323 | solution.py:51
  38.6 11.3 %fusion.57 = f32[1,4,64,128]{3,2,1,0:T(8,128)S(1)} fusion(f32[4,32]{1,0:T(4,128)S(1)} %constant_dynamic-slice_fusion.2, f32[32,128]{1,0:T(8,128)S(1)} %get-tuple-element.152, f32[4,128]{1,0:T(4,128)S(1)} %get-tuple-element.153, f32[32,128]{1,0:T(8,128)S(1)} %get-tuple-element.154, f32[4,128]{1,0:T(4,128)S(1)} %get-tuple-element.155, ...), kind=kOutput, calls=%fused_computation.16.clone.1 | convolution fusion | flops 1637875712 | bytes 1251840 | tf_op jit(solution)/shard_map/while/body/eval_jaxpr/bjts,jps->bpt/dot_general | solution.py:48
  53.2 11.3 %fusion.57 = f32[1,4,64,128]{3,2,1,0:T(8,128)S(1)} fusion(f32[4,32]{1,0:T(4,128)S(1)} %constant_dynamic-slice_fusion.2, f32[32,128]{1,0:T(8,128)S(1)} %get-tuple-element.152, f32[4,128]{1,0:T(4,128)S(1)} %get-tuple-element.153, f32[32,128]{1,0:T(8,128)S(1)} %get-tuple-element.154, f32[4,128]{1,0:T(4,128)S(1)} %get-tuple-element.155, ...), kind=kOutput, calls=%fused_computation.16.clone.1 | convolution fusion | flops 1637875712 | bytes 1251840 | tf_op jit(solution)/shard_map/while/body/eval_jaxpr/bjts,jps->bpt/dot_general | solution.py:48
  67.7 11.3 %fusion.57 = f32[1,4,64,128]{3,2,1,0:T(8,128)S(1)} fusion(f32[4,32]{1,0:T(4,128)S(1)} %constant_dynamic-slice_fusion.2, f32[32,128]{1,0:T(8,128)S(1)} %get-tuple-element.152, f32[4,128]{1,0:T(4,128)S(1)} %get-tuple-element.153, f32[32,128]{1,0:T(8,128)S(1)} %get-tuple-element.154, f32[4,128]{1,0:T(4,128)S(1)} %get-tuple-element.155, ...), kind=kOutput, calls=%fused_computation.16.clone.1 | convolution fusion | flops 1637875712 | bytes 1251840 | tf_op jit(solution)/shard_map/while/body/eval_jaxpr/bjts,jps->bpt/dot_general | solution.py:48
  82.3 11.3 %fusion.57 = f32[1,4,64,128]{3,2,1,0:T(8,128)S(1)} fusion(f32[4,32]{1,0:T(4,128)S(1)} %constant_dynamic-slice_fusion.2, f32[32,128]{1,0:T(8,128)S(1)} %get-tuple-element.152, f32[4,128]{1,0:T(4,128)S(1)} %get-tuple-element.153, f32[32,128]{1,0:T(8,128)S(1)} %get-tuple-element.154, f32[4,128]{1,0:T(4,128)S(1)} %get-tuple-element.155, ...), kind=kOutput, calls=%fused_computation.16.clone.1 | convolution fusion | flops 1637875712 | bytes 1251840 | tf_op jit(solution)/shard_map/while/body/eval_jaxpr/bjts,jps->bpt/dot_general | solution.py:48
  96.9 11.3 %fusion.57 = f32[1,4,64,128]{3,2,1,0:T(8,128)S(1)} fusion(f32[4,32]{1,0:T(4,128)S(1)} %constant_dynamic-slice_fusion.2, f32[32,128]{1,0:T(8,128)S(1)} %get-tuple-element.152, f32[4,128]{1,0:T(4,128)S(1)} %get-tuple-element.153, f32[32,128]{1,0:T(8,128)S(1)} %get-tuple-element.154, f32[4,128]{1,0:T(4,128)S(1)} %get-tuple-element.155, ...), kind=kOutput, calls=%fused_computation.16.clone.1 | convolution fusion | flops 1637875712 | bytes 1251840 | tf_op jit(solution)/shard_map/while/body/eval_jaxpr/bjts,jps->bpt/dot_general | solution.py:48
  111.5 11.3 %fusion.57 = f32[1,4,64,128]{3,2,1,0:T(8,128)S(1)} fusion(f32[4,32]{1,0:T(4,128)S(1)} %constant_dynamic-slice_fusion.2, f32[32,128]{1,0:T(8,128)S(1)} %get-tuple-element.152, f32[4,128]{1,0:T(4,128)S(1)} %get-tuple-element.153, f32[32,128]{1,0:T(8,128)S(1)} %get-tuple-element.154, f32[4,128]{1,0:T(4,128)S(1)} %get-tuple-element.155, ...), kind=kOutput, calls=%fused_computation.16.clone.1 | convolution fusion | flops 1637875712 | bytes 1251840 | tf_op jit(solution)/shard_map/while/body/eval_jaxpr/bjts,jps->bpt/dot_general | solution.py:48
  126.1 11.3 %fusion.57 = f32[1,4,64,128]{3,2,1,0:T(8,128)S(1)} fusion(f32[4,32]{1,0:T(4,128)S(1)} %constant_dynamic-slice_fusion.2, f32[32,128]{1,0:T(8,128)S(1)} %get-tuple-element.152, f32[4,128]{1,0:T(4,128)S(1)} %get-tuple-element.153, f32[32,128]{1,0:T(8,128)S(1)} %get-tuple-element.154, f32[4,128]{1,0:T(4,128)S(1)} %get-tuple-element.155, ...), kind=kOutput, calls=%fused_computation.16.clone.1 | convolution fusion | flops 1637875712 | bytes 1251840 | tf_op jit(solution)/shard_map/while/body/eval_jaxpr/bjts,jps->bpt/dot_general | solution.py:48
  140.7 11.3 %fusion.57 = f32[1,4,64,128]{3,2,1,0:T(8,128)S(1)} fusion(f32[4,32]{1,0:T(4,128)S(1)} %constant_dynamic-slice_fusion.2, f32[32,128]{1,0:T(8,128)S(1)} %get-tuple-element.152, f32[4,128]{1,0:T(4,128)S(1)} %get-tuple-element.153, f32[32,128]{1,0:T(8,128)S(1)} %get-tuple-element.154, f32[4,128]{1,0:T(4,128)S(1)} %get-tuple-element.155, ...), kind=kOutput, calls=%fused_computation.16.clone.1 | convolution fusion | flops 1637875712 | bytes 1251840 | tf_op jit(solution)/shard_map/while/body/eval_jaxpr/bjts,jps->bpt/dot_general | solution.py:48
  155.2 9.3 %fusion.26 = bf16[128,64,128]{2,1,0:T(8,128)(2,1)S(1)} fusion(bf16[128,64,128]{2,1,0:T(8,128)(2,1)} %bitcast.25, f32[128,128]{1,0:T(8,128)S(1)} %bitcast.154, f32[128,128]{1,0:T(8,128)S(1)} %bitcast.151, f32[128,128]{1,0:T(8,128)S(1)} %bitcast.152, f32[128,128]{1,0:T(8,128)S(1)} %bitcast.150, f32[128,128]{1,0:T(8,128)S(1)} %bitcast.153, ...), kind=kOutput, calls=%fused_computation.41 | convolution fusion | flops 292552704 | bytes 4653056 | tf_op jit(solution)/shard_map/nts,nps->npt/dot_general | solution.py:96
  164.5 3.2 %copy.97 = bf16[16,8,64,128]{3,1,2,0:T(8,128)(2,1)} copy(bf16[16,8,64,128]{3,2,1,0:T(8,128)(2,1)S(1)} %bitcast.140) | data formatting | bytes 4194304
  167.7 3.2 %copy.69 = bf16[8192,128]{1,0:T(8,128)(2,1)S(1)} copy(bf16[8192,128]{0,1:T(8,128)(2,1)} %bitcast.134) | data formatting | bytes 4194304 | tf_op jit(solution)/shard_map/dot_general | solution.py:102
  170.9 2.0 %convolution_add_fusion = f32[32,64,128]{2,0,1:T(8,128)S(1)} fusion(f32[32,64,128]{2,0,1:T(8,128)} %bitcast.141, bf16[64,128,128]{2,1,0:T(8,128)(2,1)S(1)} %bitcast.133, s32[128]{0:T(128)S(1)} %eq.92), kind=kOutput, calls=%fused_computation.43 | convolution fusion | flops 67375104 | bytes 4194816 | tf_op jit(solution)/shard_map/dot_general | solution.py:102
  172.9 1.5 convolution_convert_fusion.1
  174.7 5.7 %psum.7 = f32[4]{0:T(128)S(1)} all-reduce(f32[4]{0:T(128)S(1)} %get-tuple-element.101), channel_id=1, replica_groups=mesh['leaf'=8,'probe'=4] {'probe'}, use_global_device_ids=true, to_apply=%region_9.10 | all-reduce | flops 4 | bytes 32 | tf_op jit(solution)/shard_map/psum | solution.py:117
  181.3 1.6 copy.98
  (107 shorter events, 21.4 us)
Async XLA Ops:
  0.6 173.8 %copy-start = (bf16[4,256,64]{1,2,0:T(8,128)(2,1)S(1)}, bf16[4,256,64]{1,2,0:T(8,128)(2,1)}, u32[]{:S(2)}) copy-start(bf16[4,256,64]{1,2,0:T(8,128)(2,1)} %param.15) | copy-start | bytes 393220
  3.4 13.7 %all-to-all-start = ((s32[8,1,16]{2,1,0:T(1,128)}), s32[8,1,16]{2,1,0:T(1,128)S(1)}, u32[]{:S(2)}, u32[]{:S(2)}) async-start(s32[8,1,16]{2,1,0:T(1,128)} %bitcast.22), calls=%async_computation | async-start | bytes 8192 | tf_op jit(solution)/shard_map/all_to_all | solution.py:76
  16.0 7.6 %copy-start.2 = (f32[3,4096]{1,0:T(4,128)S(1)}, f32[3,4096]{1,0:T(4,128)}, u32[]{:S(2)}) copy-start(f32[3,4096]{1,0:T(4,128)} %param.9) | copy-start | bytes 147460
  17.1 14.2 %all-to-all-start.2 = ((f32[8,16,4,128]{3,2,1,0:T(4,128)}), f32[8,16,4,128]{3,2,1,0:T(4,128)S(1)}, u32[]{:S(2)}, u32[]{:S(2)}) async-start(f32[8,16,4,128]{3,2,1,0:T(4,128)} %pad_maximum_fusion), calls=%async_computation.2 | async-start | bytes 524288 | tf_op jit(solution)/shard_map/all_to_all | solution.py:78
  23.6 2.0 %copy-start.3 = (f32[32,64,128]{2,0,1:T(8,128)S(1)}, f32[32,64,128]{2,0,1:T(8,128)}, u32[]{:S(2)}) copy-start(f32[32,64,128]{2,0,1:T(8,128)} %bitcast_convert_fusion) | copy-start | bytes 3145732
  25.6 0.7 copy-start.5
  31.3 4.7 %copy-start.1 = (f32[4096]{0:T(1024)S(1)}, f32[4096]{0:T(1024)}, u32[]{:S(2)}) copy-start(f32[4096]{0:T(1024)} %param.10) | copy-start | bytes 49156
  31.3 123.9 %all-to-all-start.1 = ((bf16[8,16,64,128]{3,2,1,0:T(8,128)(2,1)}), bf16[8,16,64,128]{3,2,1,0:T(8,128)(2,1)}, u32[]{:S(2)}, u32[]{:S(2)}) async-start(bf16[8,16,64,128]{3,2,1,0:T(8,128)(2,1)} %bitcast.67), calls=%async_computation.1 | async-start | bytes 4194304 | tf_op jit(solution)/shard_map/all_to_all | solution.py:86
  170.9 2.0 %copy-start.4 = (s32[32,32]{1,0:T(8,128)S(1)}, s32[32,32]{1,0:T(8,128)}, u32[]{:S(2)}) copy-start(s32[32,32]{1,0:T(8,128)} %param.14) | copy-start | bytes 12292
where the time goes:
time: 184 us; the launch traced here: 183 us
  matrix products  104 us (57%)
  local copies, waits for them, and re-layouts  28.5 us (15%)
  starting transfers between devices  17.7 us (10%)
  loops' own time  15.2 us (8%)
  blocking collectives  5.65 us (3%)
  other arithmetic  5.58 us (3%)
  waiting for transfers between devices  5.03 us (3%)
    dot_general x8, matrix products, local_block(): jnp.einsum('bjts,jps->bpt', scaled, probes_wide, precision=lax.Precision....  90.5 us
    another operation x1, loops' own time, per_device(): lax.map(local_block, firsts).reshape(leaf_dev, probe_dev, LEAF_PTS)  15.2 us
    dot_general x1, matrix products, per_device(): jnp.einsum('nts,nps->npt', kernel, got_probes, preferred_element_type=jnp...  9.29 us
    unnamed x16, local copies, waits for them, and re-layouts  7.94 us
    all_to_all x1, starting transfers between devices, per_device(): lax.all_to_all(requests, 'leaf', split_axis=0, concat_axis=0, tiled=True)  7.28 us
    dynamic_update_slice x8, local copies, waits for them, and re-layouts, per_device(): lax.map(local_block, firsts).reshape(leaf_dev, probe_dev, LEAF_PTS)  5.96 us
    all_to_all x1, starting transfers between devices, per_device(): lax.all_to_all(send_points.reshape(n_leaf, CAP, 4, LEAF_PTS), 'leaf', spl...  5.74 us
    psum x1, blocking collectives, per_device(): energy = lax.psum(jnp.sum(merged * merged, axis=(1, 2)), 'probe')  5.65 us
  transfers between devices with their start and end apart: 3, of which 2 were waited for; matrix products, arithmetic and copies ran while one was open for 62% of the time, Pallas kernels for 0%

commit v1 on v0

v1 whole, which is shorter than its diff:
```python
import functools

import jax
import jax.numpy as jnp
from jax import lax
from jax.experimental import pallas as pl
from jax.experimental.pallas import tpu as pltpu
from jax.sharding import PartitionSpec as P

LEAF_PTS = 128
SK = 32
SK2 = 64
CHILD = 8

DELTA_SQ = 0.0001
INV_FOUR_PI = 0.07957747154594767

VMEM_LIMIT = 48 * 1024 * 1024
GROUP = 4

SMEM = pl.BlockSpec(memory_space=pltpu.SMEM)
VMEM = pl.BlockSpec(memory_space=pltpu.VMEM)


def leaf_lanes(leaf):
    return pl.ds(pl.multiple_of(leaf * LEAF_PTS, LEAF_PTS), LEAF_PTS)


def column_of(row):
    return jnp.transpose(jnp.broadcast_to(row, (LEAF_PTS, LEAF_PTS)))


def kernel_block(columns, source, scale):
    delta_x = columns[0] - source[0:1]
    delta_y = columns[1] - source[1:2]
    delta_z = columns[2] - source[2:3]
    dist_sq = delta_x * delta_x + delta_y * delta_y + delta_z * delta_z
    values = source[3:4] * scale * lax.rsqrt(dist_sq + DELTA_SQ)
    return values.astype(jnp.bfloat16)


def times_block(probes, block):
    return lax.dot_general(
        probes, block, (((1,), (1,)), ((), ())), preferred_element_type=jnp.float32
    )


def local_body(index_ref, count_ref, groups_ref, points_ref, omega_ref, out_ref, cols_ref):
    leaf_dev = groups_ref.shape[0]

    def target_step(t, carry):
        for c in range(3):
            cols_ref[c] = column_of(points_ref[c : c + 1, leaf_lanes(t)])

        def group_step(g, total):
            for u in range(GROUP):
                s = index_ref[t, g * GROUP + u]
                scale = count_ref[t, g * GROUP + u] * INV_FOUR_PI
                source = points_ref[:, leaf_lanes(s)]
                block = kernel_block([cols_ref[c] for c in range(3)], source, scale)
                total = total + times_block(omega_ref[:, leaf_lanes(s)], block)
            return total

        zero = jnp.zeros((omega_ref.shape[0], LEAF_PTS), jnp.float32)
        out_ref[:, leaf_lanes(t)] = lax.fori_loop(0, groups_ref[t], group_step, zero)
        return carry

    lax.fori_loop(0, leaf_dev, target_step, 0)


def far_body(dests, *refs):
    source_ref, target_ref = refs[:2]
    target_points = refs[2 : 2 + dests]
    source_points = refs[2 + dests : 6 + dests]
    omegas = refs[6 + dests : 10 + dests]
    own_ref = refs[10 + dests]
    rest_ref = refs[11 + dests]
    total_ref, cols_ref = refs[12 + dests :]
    leaf_dev = own_ref.shape[1] // LEAF_PTS
    pairs = source_ref.shape[1]
    total_ref[...] = jnp.zeros_like(total_ref)
    for k in range(4):

        def pair_step(p, carry, k=k):
            target = target_ref[k, p]

            @pl.when(target >= 0)
            def _():
                s = source_ref[k, p]
                leaf = lax.rem(target, leaf_dev)
                dest = lax.div(target, leaf_dev)
                for r in range(dests):

                    @pl.when(dest == r)
                    def _(r=r):
                        for c in range(3):
                            cols_ref[c] = column_of(target_points[r][c : c + 1, leaf_lanes(leaf)])

                source = source_points[k][:, leaf_lanes(s)]
                block = kernel_block([cols_ref[c] for c in range(3)], source, INV_FOUR_PI)
                total_ref[dest, :, leaf_lanes(leaf)] += times_block(
                    omegas[k][:, leaf_lanes(s)], block
                )

            return carry

        lax.fori_loop(0, pairs, pair_step, 0)
    own_ref[...] = total_ref[0]
    for r in range(1, dests):
        rest_ref[r - 1] = total_ref[r].astype(jnp.bfloat16)


def merge_body(local_ref, own_ref, arrived_ref, pick_ref, near_ref, merged_ref, energy_ref):
    near = local_ref[...] + own_ref[...] + arrived_ref[...].astype(jnp.float32)
    near_ref[...] = near
    rounded = near.astype(jnp.bfloat16)
    parents, width, _ = pick_ref.shape
    for p in range(parents):
        merged = jnp.dot(
            rounded[:, p * width : (p + 1) * width], pick_ref[p], preferred_element_type=jnp.float32
        )
        merged_ref[:, p * SK2 : (p + 1) * SK2] = merged
        energy_ref[p : p + 1, :] = jnp.broadcast_to(
            jnp.sum(jnp.sum(merged * merged, axis=0, keepdims=True), axis=1, keepdims=True),
            (1, LEAF_PTS),
        )


def scale_body(count, merged_ref, energy_ref, out_ref):
    parents = energy_ref.shape[0]
    for p in range(parents):
        factor = lax.rsqrt(energy_ref[p : p + 1, 0:SK2] / count + 1e-06)
        out_ref[:, p * SK2 : (p + 1) * SK2] = merged_ref[:, p * SK2 : (p + 1) * SK2] * factor


def call(body, out_shape, in_specs, scratch=()):
    many = isinstance(out_shape, (tuple, list))
    return pl.pallas_call(
        body,
        out_shape=out_shape,
        in_specs=in_specs,
        out_specs=[VMEM] * len(out_shape) if many else VMEM,
        scratch_shapes=list(scratch),
        compiler_params=pltpu.CompilerParams(vmem_limit_bytes=VMEM_LIMIT),
    )


def exchange(array, axis, bit):
    size = lax.axis_size(axis)
    return lax.ppermute(array, axis, [(i, i ^ bit) for i in range(size)])


def local_tables(near_local, offset, leaf_dev):
    leaf_iota = jnp.arange(leaf_dev, dtype=jnp.int32)
    ids = near_local - offset
    counts = jnp.sum((ids[:, :, None] == leaf_iota).astype(jnp.int32), axis=1)
    present = (counts > 0).astype(jnp.int32)
    before = (leaf_iota[:, None] < leaf_iota[None, :]).astype(jnp.int32)
    place = jnp.sum(present[:, :, None] * before[None], axis=1)
    hit = (place[:, :, None] == leaf_iota).astype(jnp.int32) * present[:, :, None]
    index = jnp.sum(hit * leaf_iota[None, :, None], axis=1)
    count = jnp.sum(hit * counts[:, :, None], axis=1).astype(jnp.float32)
    groups = (jnp.sum(present, axis=1) + GROUP - 1) // GROUP
    return index, count, groups


def per_device(coords, weights, omega, near_local, far_pairs, skel_rows, parent_interp):
    n_leaf = lax.axis_size("leaf")
    points = coords.shape[1]
    leaf_dev = points // LEAF_PTS
    probe_dev = omega.shape[0]
    parent_dev = leaf_dev // CHILD
    me = lax.axis_index("leaf")
    top, low = n_leaf // 2, 1
    dests = n_leaf // 4
    pair_dev = far_pairs.shape[1]

    bundle = jnp.concatenate([coords, weights[None]], axis=0)
    pair_columns = 2 * pair_dev // 4
    sent = jnp.concatenate(
        [bundle, far_pairs.reshape(4, pair_columns).astype(jnp.float32)], axis=1
    )
    across = exchange(sent, "leaf", top)
    beside = exchange(sent, "leaf", low)
    target_bundles = [bundle] + [
        exchange(bundle, "leaf", 2 * r) for r in range(1, dests)
    ]
    both = exchange(across, "leaf", low)
    omega_across = exchange(omega, "leaf", top)
    omega_beside = exchange(omega, "leaf", low)
    omega_both = exchange(omega_across, "leaf", low)

    index, count, groups = local_tables(near_local, me * leaf_dev, leaf_dev)
    local = call(
        local_body,
        jax.ShapeDtypeStruct((probe_dev, points), jnp.float32),
        [SMEM, SMEM, SMEM, VMEM, VMEM],
        [pltpu.VMEM((3, LEAF_PTS, LEAF_PTS), jnp.float32)],
    )(index, count, groups, bundle, omega)

    bundles = [sent, across, beside, both]
    pairs = jnp.stack([b[:, points:].astype(jnp.int32).reshape(2, pair_dev) for b in bundles])
    owners = me ^ jnp.array([0, top, low, top | low], jnp.int32)
    sources = pairs[:, 0] - owners[:, None] * leaf_dev
    relation = (pairs[:, 1] // leaf_dev) ^ me
    inside = (relation & (top | low)) == 0
    targets = jnp.where(inside, (relation // 2) * leaf_dev + pairs[:, 1] % leaf_dev, -1)
    own, rest = call(
        functools.partial(far_body, dests),
        [
            jax.ShapeDtypeStruct((probe_dev, points), jnp.float32),
            jax.ShapeDtypeStruct((dests - 1, probe_dev, points), jnp.bfloat16),
        ],
        [SMEM, SMEM] + [VMEM] * (dests + 8),
        [
            pltpu.VMEM((dests, probe_dev, points), jnp.float32),
            pltpu.VMEM((3, LEAF_PTS, LEAF_PTS), jnp.float32),
        ],
    )(
        sources,
        targets,
        *target_bundles,
        *bundles,
        omega,
        omega_across,
        omega_beside,
        omega_both,
    )
    half = dests // 2
    while half > 1:
        got = exchange(rest[half - 1 :], "leaf", 2 * half)
        own = own + got[0].astype(jnp.float32)
        rest = rest[: half - 1] + got[1:]
        half //= 2
    arrived = exchange(rest[0], "leaf", 2)

    rows = (
        jnp.arange(LEAF_PTS, dtype=jnp.int32)[None, :, None] == skel_rows[:, None, :]
    ).astype(jnp.bfloat16)
    weights_of = parent_interp.reshape(leaf_dev, SK, SK2)
    pick = jnp.einsum("lir,lrk->lik", rows, weights_of, preferred_element_type=jnp.float32)
    pick = pick.astype(jnp.bfloat16).reshape(parent_dev, CHILD * LEAF_PTS, SK2)
    near, merged, energy = call(
        merge_body,
        [
            jax.ShapeDtypeStruct((probe_dev, points), jnp.float32),
            jax.ShapeDtypeStruct((probe_dev, parent_dev * SK2), jnp.float32),
            jax.ShapeDtypeStruct((parent_dev, LEAF_PTS), jnp.float32),
        ],
        [VMEM] * 4,
    )(local, own, arrived, pick)
    energy = lax.psum(energy, "probe")
    parent = call(
        functools.partial(scale_body, float(SK2 * probe_dev * lax.axis_size("probe"))),
        jax.ShapeDtypeStruct((probe_dev, parent_dev * SK2), jnp.float32),
        [VMEM] * 2,
    )(merged, energy)
    return near, parent


def solution(mesh):
    return jax.shard_map(
        per_device,
        mesh=mesh,
        in_specs=(
            P(None, "leaf"),
            P("leaf"),
            P("probe", "leaf"),
            P("leaf", None),
            P(None, "leaf"),
            P("leaf", None),
            P("leaf", None, None),
        ),
        out_specs=(P("probe", "leaf"), P("probe", "leaf")),
        check_vma=False,
    )
```

time: 184 us -> 127 us (0.69)
  matrix products: 104 us -> 1.32 us
  Pallas kernels: 0 us -> 69.9 us
  waiting for transfers between devices: 5.03 us -> 31.2 us
  local copies, waits for them, and re-layouts: 28.5 us -> 5.16 us
  loops' own time: 15.2 us -> 0 us
  starting transfers between devices: 17.7 us -> 10.1 us
  other arithmetic: 5.58 us -> 2.89 us
    dot_general x13 -> x1, matrix products: 104 us -> 1.32 us  [per_device(): jnp.einsum('lir,lrk->lik', rows, weights_of, preferred_element_type=jnp.f...]
    pallas_call x0 -> x4, Pallas kernels: none -> 69.9 us  [the longest x1 39.4 us: per_device(): call(local_body, jax.ShapeDtypeStruct((probe_dev, points), jnp.float32),...]
    ppermute x0 -> x8, waiting for transfers between devices: none -> 31.2 us  [exchange(): return lax.ppermute(array, axis, [(i, i ^ bit) for i in range(size)])]
    all_to_all x3 -> x0, starting transfers between devices: 17.7 us -> none  [the longest x1 7.28 us: per_device(): lax.all_to_all(requests, 'leaf', split_axis=0, concat_axis=0, tiled=True)]
    another operation x1 -> x0, loops' own time: 15.2 us -> none  [per_device(): lax.map(local_block, firsts).reshape(leaf_dev, probe_dev, LEAF_PTS)]
    ppermute x0 -> x8, starting transfers between devices: none -> 10.1 us  [exchange(): return lax.ppermute(array, axis, [(i, i ^ bit) for i in range(size)])]
    dynamic_update_slice x8 -> x0, local copies, waits for them, and re-layouts: 5.96 us -> none  [per_device(): lax.map(local_block, firsts).reshape(leaf_dev, probe_dev, LEAF_PTS)]
    all_to_all x3 -> x0, waiting for transfers between devices: 5.03 us -> none  [the longest x1 4.77 us: per_device(): lax.all_to_all(send_points.reshape(n_leaf, CAP, 4, LEAF_PTS), 'leaf', spl...]
  transfers between devices with their start and end apart: 3 -> 8, of which waited for: 2 -> 2; matrix products, arithmetic and copies ran while one was open for 62% -> 5% of each run, Pallas kernels for 0% -> 31%
where the time goes in v1:
time: 127 us
  Pallas kernels  69.9 us (55%)
  waiting for transfers between devices  31.2 us (25%)
  starting transfers between devices  10.1 us (8%)
  blocking collectives  5.63 us (4%)
  local copies, waits for them, and re-layouts  5.16 us (4%)
  other arithmetic  2.89 us (2%)
  matrix products  1.32 us (1%)
    pallas_call x1, Pallas kernels, per_device(): call(local_body, jax.ShapeDtypeStruct((probe_dev, points), jnp.float32),...  39.4 us
    ppermute x8, waiting for transfers between devices, exchange(): return lax.ppermute(array, axis, [(i, i ^ bit) for i in range(size)])  31.2 us
    pallas_call x1, Pallas kernels, per_device(): call(functools.partial(far_body, dests), [jax.ShapeDtypeStruct((probe_dev...  28.5 us
    ppermute x8, starting transfers between devices, exchange(): return lax.ppermute(array, axis, [(i, i ^ bit) for i in range(size)])  10.1 us
    psum x1, blocking collectives, per_device(): energy = lax.psum(energy, 'probe')  5.63 us
    unnamed x19, local copies, waits for them, and re-layouts  3.24 us
  transfers between devices with their start and end apart: 8, of which 2 were waited for; matrix products, arithmetic and copies ran while one was open for 5% of the time, Pallas kernels for 31%

profile of v1, /device:TPU:0, one launch (start us, length us, event | category | flops | bytes accessed | tf_op | source)
XLA Modules:
  0.0 127.0 jit_solution(8430772767122459611)
XLA Ops:
  0.6 0.7 convert_convert_fusion
  1.4 1.0 pad_maximum_fusion.refs_4_
  2.4 3.0 %collective-permute-start.1 = (f32[4,4128]{1,0:T(4,128)S(1)}, f32[4,4128]{1,0:T(4,128)S(1)}, u32[]{:S(2)}, u32[]{:S(2)}) collective-permute-start(f32[4,4128]{1,0:T(4,128)S(1)} %pad_maximum_fusion.refs_4_), channel_id=1, source_target_pairs={{0,4},{4,0},{8,12},{12,8},{16,20},{20,16},{24,28},{28,24},{1,5},{5... | collective-permute-start | bytes 198152 | tf_op jit(solution)/shard_map/ppermute | solution.py:150
  5.4 2.6 %collective-permute-start = (f32[4,4128]{1,0:T(4,128)S(1)}, f32[4,4128]{1,0:T(4,128)S(1)}, u32[]{:S(2)}, u32[]{:S(2)}) collective-permute-start(f32[4,4128]{1,0:T(4,128)S(1)} %pad_maximum_fusion.refs_4_), channel_id=1, source_target_pairs={{0,16},{4,20},{8,24},{12,28},{16,0},{20,4},{24,8},{28,12},{1,17},{... | collective-permute-start | bytes 198152 | tf_op jit(solution)/shard_map/ppermute | solution.py:150
  8.0 0.3 collective-permute-start.4
  8.3 0.2 collective-permute-start.5
  8.6 1.9 %collective-permute-start.3 = (f32[4,4096]{1,0:T(4,128)S(1)}, f32[4,4096]{1,0:T(4,128)S(1)}, u32[]{:S(2)}, u32[]{:S(2)}) collective-permute-start(f32[4,4096]{1,0:T(4,128)S(1)} %pad_maximum_fusion.1.points_ref.refs_2_), channel_id=1, source_target_pairs={{0,8},{4,12},{8,0},{12,4},{16,24},{20,28},{24,16},{28,20},{1,9},{5... | collective-permute-start | bytes 196616 | tf_op jit(solution)/shard_map/ppermute | solution.py:150
  10.6 0.2 convert_reduce_fusion
  10.8 0.2 multiply_reduce_fusion
  11.0 0.6 fusion.1
  11.6 1.7 %copy.28 = bf16[4,256,64]{2,1,0:T(8,128)(2,1)} copy(bf16[4,256,64]{1,2,0:T(8,128)(2,1)} %param.14) | data formatting | bytes 262144 | tf_op args[6]
  13.4 1.5 %collective-permute-start.2 = (f32[4,4128]{1,0:T(4,128)S(1)}, f32[4,4128]{1,0:T(4,128)S(1)}, u32[]{:S(2)}, u32[]{:S(2)}) collective-permute-start(f32[4,4128]{1,0:T(4,128)S(1)} %collective-permute-done.refs_5_), channel_id=1, source_target_pairs={{0,4},{4,0},{8,12},{12,8},{16,20},{20,16},{24,28},{28,24},{1,5},{5... | collective-permute-start | bytes 198152 | tf_op jit(solution)/shard_map/ppermute | solution.py:150
  15.1 19.0 %collective-permute-done.4.refs_9_ = bf16[64,4096]{1,0:T(8,128)(2,1)S(1)} collective-permute-done((bf16[64,4096]{1,0:T(8,128)(2,1)}, bf16[64,4096]{1,0:T(8,128)(2,1)S(1)}, u32[]{:S(2)}, u32[]{:S(2)}) %collective-permute-start.4) | collective-permute-done | bytes 524320 | tf_op jit(solution)/shard_map/ppermute | solution.py:150
  34.1 0.5 collective-permute-start.6
  34.8 0.6 copy-done.1
  35.4 12.2 %collective-permute-done.6.refs_11_ = bf16[64,4096]{1,0:T(8,128)(2,1)S(1)} collective-permute-done((bf16[64,4096]{1,0:T(8,128)(2,1)S(1)}, bf16[64,4096]{1,0:T(8,128)(2,1)S(1)}, u32[]{:S(2)}, u32[]{:S(2)}) %collective-permute-start.6) | collective-permute-done | bytes 524320 | tf_op jit(solution)/shard_map/ppermute | solution.py:150
  47.6 0.8 copy-done.2
  48.5 28.5 %shard_map.96 = (f32[64,4096]{1,0:T(8,128)S(1)}, bf16[1,64,4096]{2,1,0:T(8,128)(2,1)}) custom-call(s32[4,64]{1,0:T(4,128)S(1)} %get-tuple-element.15.refs_0_, s32[4,64]{1,0:T(4,128)S(1)} %get-tuple-element.14.refs_1_, f32[4,4096]{1,0:T(4,128)S(1)} %pad_maximum_fusion.1.points_ref.refs_2_, f32[4,4096]{1,0:T(4,128)S(1)} %copy-done.2, ...), custom_call_target="tpu_custom_call" | custom-call | tf_op jit(solution)/shard_map/pallas_call | solution.py:208
  77.0 1.3 %convolution_convert_fusion = bf16[32,128,64]{1,2,0:T(8,128)(2,1)} fusion(bf16[32,32,64]{2,1,0:T(8,128)(2,1)S(1)} %bitcast.20, s32[32,32]{1,0:T(8,128)S(1)} %copy-done.6), kind=kOutput, calls=%fused_computation | convolution fusion | flops 17170432 | bytes 659456 | tf_op jit(solution)/shard_map/lir,lrk->lik/dot_general | solution.py:241
  78.3 1.5 %copy.29 = bf16[32,128,64]{2,1,0:T(8,128)(2,1)S(1)} copy(bf16[32,128,64]{1,2,0:T(8,128)(2,1)} %convolution_convert_fusion) | data formatting | bytes 1048576 | tf_op jit(solution)/shard_map/convert_element_type | solution.py:242
  79.9 39.4 %shard_map.95.local_ref = f32[64,4096]{1,0:T(8,128)S(1)} custom-call(s32[32,32]{1,0:T(8,128)S(1)} %get-tuple-element.13.index_ref, f32[32,32]{1,0:T(8,128)S(1)} %convert_element_type.52.count_ref, s32[32]{0:T(128)S(1)} %and_select_fusion.groups_ref, f32[4,4096]{1,0:T(4,128)S(1)} %pad_maximum_fusion.1.points_ref.refs_2_, bf16[64,4096]{1,0:T(8,128)(2,1)S(1)} %copy-done), custom_call_target="tpu_custom_call" | custom-call | tf_op jit(solution)/shard_map/pallas_call | solution.py:194
  119.4 1.2 shard_map.97
  120.6 5.6 %psum.7.energy_ref = f32[4,128]{1,0:T(4,128)S(1)} all-reduce(f32[4,128]{1,0:T(4,128)S(1)} %get-tuple-element.11), channel_id=1, replica_groups=mesh['leaf'=8,'probe'=4] {'probe'}, use_global_device_ids=true, to_apply=%region_5.6 | all-reduce | flops 512 | bytes 4096 | tf_op jit(solution)/shard_map/psum | solution.py:252
  126.3 0.7 shard_map.98
  (40 shorter events, 0.7 us)
Async XLA Ops:
  1.3 9.2 %copy-start.8 = (s32[4]{0:T(128)S(1)}, s32[4]{0:T(128)}, u32[]{:S(2)}) copy-start(s32[4]{0:T(128)} %constant.70.clone) | copy-start | bytes 52
  1.3 9.2 %copy-start.7 = (s32[32,24]{0,1:T(8,128)S(1)}, s32[32,24]{0,1:T(8,128)}, u32[]{:S(2)}) copy-start(s32[32,24]{0,1:T(8,128)} %param.11) | copy-start | bytes 9220
  1.4 7.1 %copy-start.4 = (f32[3,4096]{1,0:T(4,128)S(1)}, f32[3,4096]{1,0:T(4,128)}, u32[]{:S(2)}) copy-start(f32[3,4096]{1,0:T(4,128)} %param.8) | copy-start | bytes 147460
  1.4 7.1 %copy-start.5 = (f32[4096]{0:T(1024)S(1)}, f32[4096]{0:T(1024)}, u32[]{:S(2)}) copy-start(f32[4096]{0:T(1024)} %param.9) | copy-start | bytes 49156
  1.4 46.2 %copy-start = (bf16[64,4096]{1,0:T(8,128)(2,1)S(1)}, bf16[64,4096]{1,0:T(8,128)(2,1)}, u32[]{:S(2)}) copy-start(bf16[64,4096]{1,0:T(8,128)(2,1)} %refs_8_.1) | copy-start | bytes 1572868
  2.4 12.6 %collective-permute-start.1 = (f32[4,4128]{1,0:T(4,128)S(1)}, f32[4,4128]{1,0:T(4,128)S(1)}, u32[]{:S(2)}, u32[]{:S(2)}) collective-permute-start(f32[4,4128]{1,0:T(4,128)S(1)} %pad_maximum_fusion.refs_4_), channel_id=1, source_target_pairs={{0,4},{4,0},{8,12},{12,8},{16,20},{20,16},{24,28},{28,24},{1,5},{5... | collective-permute-start | bytes 198152 | tf_op jit(solution)/shard_map/ppermute | solution.py:150
  5.4 8.0 %collective-permute-start = (f32[4,4128]{1,0:T(4,128)S(1)}, f32[4,4128]{1,0:T(4,128)S(1)}, u32[]{:S(2)}, u32[]{:S(2)}) collective-permute-start(f32[4,4128]{1,0:T(4,128)S(1)} %pad_maximum_fusion.refs_4_), channel_id=1, source_target_pairs={{0,16},{4,20},{8,24},{12,28},{16,0},{20,4},{24,8},{28,12},{1,17},{... | collective-permute-start | bytes 198152 | tf_op jit(solution)/shard_map/ppermute | solution.py:150
  8.0 26.1 %collective-permute-start.4 = (bf16[64,4096]{1,0:T(8,128)(2,1)}, bf16[64,4096]{1,0:T(8,128)(2,1)S(1)}, u32[]{:S(2)}, u32[]{:S(2)}) collective-permute-start(bf16[64,4096]{1,0:T(8,128)(2,1)} %refs_8_.1), channel_id=1, source_target_pairs={{0,16},{4,20},{8,24},{12,28},{16,0},{20,4},{24,8},{28,12},{1,17},{... | collective-permute-start | bytes 1572872 | tf_op jit(solution)/shard_map/ppermute | solution.py:150
  8.3 27.1 %collective-permute-start.5 = (bf16[64,4096]{1,0:T(8,128)(2,1)}, bf16[64,4096]{1,0:T(8,128)(2,1)S(1)}, u32[]{:S(2)}, u32[]{:S(2)}) collective-permute-start(bf16[64,4096]{1,0:T(8,128)(2,1)} %refs_8_.1), channel_id=1, source_target_pairs={{0,4},{4,0},{8,12},{12,8},{16,20},{20,16},{24,28},{28,24},{1,5},{5... | collective-permute-start | bytes 1572872 | tf_op jit(solution)/shard_map/ppermute | solution.py:150
  8.6 26.2 %collective-permute-start.3 = (f32[4,4096]{1,0:T(4,128)S(1)}, f32[4,4096]{1,0:T(4,128)S(1)}, u32[]{:S(2)}, u32[]{:S(2)}) collective-permute-start(f32[4,4096]{1,0:T(4,128)S(1)} %pad_maximum_fusion.1.points_ref.refs_2_), channel_id=1, source_target_pairs={{0,8},{4,12},{8,0},{12,4},{16,24},{20,28},{24,16},{28,20},{1,9},{5... | collective-permute-start | bytes 196616 | tf_op jit(solution)/shard_map/ppermute | solution.py:150
  13.4 21.2 %collective-permute-start.2 = (f32[4,4128]{1,0:T(4,128)S(1)}, f32[4,4128]{1,0:T(4,128)S(1)}, u32[]{:S(2)}, u32[]{:S(2)}) collective-permute-start(f32[4,4128]{1,0:T(4,128)S(1)} %collective-permute-done.refs_5_), channel_id=1, source_target_pairs={{0,4},{4,0},{8,12},{12,8},{16,20},{20,16},{24,28},{28,24},{1,5},{5... | collective-permute-start | bytes 198152 | tf_op jit(solution)/shard_map/ppermute | solution.py:150
  34.1 13.5 %collective-permute-start.6 = (bf16[64,4096]{1,0:T(8,128)(2,1)S(1)}, bf16[64,4096]{1,0:T(8,128)(2,1)S(1)}, u32[]{:S(2)}, u32[]{:S(2)}) collective-permute-start(bf16[64,4096]{1,0:T(8,128)(2,1)S(1)} %collective-permute-done.4.refs_9_), channel_id=1, source_target_pairs={{0,4},{4,0},{8,12},{12,8},{16,20},{20,16},{24,28},{28,24},{1,5},{5... | collective-permute-start | bytes 1572872 | tf_op jit(solution)/shard_map/ppermute | solution.py:150
  34.8 0.6 copy-start.1
  47.6 0.8 copy-start.2
  48.5 28.5 %copy-start.3 = (bf16[4,256,64]{2,1,0:T(8,128)(2,1)S(1)}, bf16[4,256,64]{2,1,0:T(8,128)(2,1)}, u32[]{:S(2)}) copy-start(bf16[4,256,64]{2,1,0:T(8,128)(2,1)} %copy.28) | copy-start | bytes 393220
  48.5 28.5 %copy-start.6 = (s32[32,32]{1,0:T(8,128)S(1)}, s32[32,32]{1,0:T(8,128)}, u32[]{:S(2)}) copy-start(s32[32,32]{1,0:T(8,128)} %param.13) | copy-start | bytes 12292
  77.0 42.4 %collective-permute-start.7 = (bf16[64,4096]{1,0:T(8,128)(2,1)}, bf16[64,4096]{1,0:T(8,128)(2,1)S(1)}, u32[]{:S(2)}, u32[]{:S(2)}) collective-permute-start(bf16[64,4096]{1,0:T(8,128)(2,1)} %bitcast.8), channel_id=1, source_target_pairs={{0,8},{4,12},{8,0},{12,4},{16,24},{20,28},{24,16},{28,20},{1,9},{5... | collective-permute-start | bytes 1572872 | tf_op jit(solution)/shard_map/ppermute | solution.py:150

commit v2 on v1

v2 whole, which is shorter than its diff:
```python
import functools

import jax
import jax.numpy as jnp
from jax import lax
from jax.experimental import pallas as pl
from jax.experimental.pallas import tpu as pltpu
from jax.sharding import PartitionSpec as P

LEAF_PTS = 128
SK = 32
SK2 = 64
CHILD = 8
CAP = 16

DELTA_SQ = 0.0001
INV_FOUR_PI = 0.07957747154594767

VMEM_LIMIT = 12 * 1024 * 1024
BATCH = 8
FEATURES = 32
CHUNKS = (1, 1)
LOCAL_PARTS = 1

SMEM = pl.BlockSpec(memory_space=pltpu.SMEM)
VMEM = pl.BlockSpec(memory_space=pltpu.VMEM)


def leaf_range(leaf):
    return pl.ds(pl.multiple_of(leaf * LEAF_PTS, LEAF_PTS), LEAF_PTS)


def split_three(values):
    first = values.astype(jnp.bfloat16).astype(jnp.float32)
    rest = values - first
    second = rest.astype(jnp.bfloat16).astype(jnp.float32)
    return first, second, rest - second


def six_products(left, right):
    a, b, c = split_three(left)
    p, q, r = split_three(right)
    return (a, a, b, b, a, c), (p, q, p, q, r, p)


def feature_body(n_source, n_target, *refs):
    source_ref, target_ref, rows = refs[n_source + n_target :]
    points = rows.shape[1]
    rows[27:FEATURES, :] = jnp.zeros((FEATURES - 27, points), jnp.float32)
    for i in range(n_source + n_target):
        points_ref = refs[i]
        centred = points_ref[0:3, :points] - 0.5
        square = centred * centred
        norm = square[0:1] + square[1:2] + square[2:3]
        if i < n_source:
            root = 1.0 / (points_ref[3:4, :points] * INV_FOUR_PI)
            scale = root * root
            side, shared, last = 1, (centred * scale, scale), scale * (norm + DELTA_SQ)
            out = source_ref.at[:, i * points : (i + 1) * points]
        else:
            side, shared, last = 0, (-2.0 * centred, norm), None
            out = target_ref.at[:, (i - n_source) * points : (i - n_source + 1) * points]
        first = 0
        for values in shared:
            for part in six_products(values, values)[side]:
                rows[first : first + values.shape[0], :] = part
                first += values.shape[0]
        parts = [jnp.ones_like(norm)] * 3 if last is None else split_three(last)
        for part in parts:
            rows[first : first + 1, :] = part
            first += 1
        out[...] = rows[...].astype(jnp.bfloat16)


def turned_block(source, target):
    scaled = lax.dot_general(
        source, target, (((0,), (0,)), ((), ())), preferred_element_type=jnp.float32
    )
    return lax.rsqrt(scaled).astype(jnp.bfloat16)


def local_body(
    first, offset_ref, near_ref, target_ref, source_ref, omega_ref, out_ref, even_ref, odd_ref
):
    entries = near_ref.shape[1]
    leaves = out_ref.shape[1] // LEAF_PTS
    offset = offset_ref[0]

    def source_of(t, e):
        return leaf_range(near_ref[first + t, e] - offset)

    def make(t, block_ref):
        target = target_ref[:, leaf_range(first + t)]
        for e in range(entries):
            block_ref[e * LEAF_PTS : (e + 1) * LEAF_PTS, :] = turned_block(
                source_ref[:, source_of(t, e)], target
            )

    def use(t, block_ref):
        probes = jnp.concatenate([omega_ref[:, source_of(t, e)] for e in range(entries)], axis=1)
        out_ref[:, leaf_range(t)] = jnp.dot(
            probes, block_ref[...], preferred_element_type=jnp.float32
        )

    make(0, even_ref)

    def step(k, carry):
        make(2 * k + 1, odd_ref)
        use(2 * k, even_ref)
        make(jnp.minimum(2 * k + 2, leaves - 1), even_ref)
        use(2 * k + 1, odd_ref)
        return carry

    lax.fori_loop(0, leaves // 2, step, 0)


def far_body(first, count_ref, table_ref, source_ref, target_ref, *refs):
    omegas = refs[:4]
    own_ref, rest_ref, even_ref, odd_ref, total_ref, omega_ref = refs[4:]
    size, points = own_ref.shape
    count = count_ref[0]
    total_ref[...] = jnp.zeros_like(total_ref)
    for k in range(4):
        cut = slice(k * points, (k + 1) * points)
        rows = slice(first, first + size) if k < 3 else slice(0, size)
        omega_ref[:, cut] = omegas[k][rows, :]

    def make(base, block_ref):
        for u in range(BATCH):
            block_ref[u] = turned_block(
                source_ref[:, leaf_range(table_ref[0, base + u])],
                target_ref[:, leaf_range(table_ref[1, base + u])],
            )

    def use(base, block_ref):
        for u in range(BATCH):
            product = jnp.dot(
                omega_ref[:, leaf_range(table_ref[0, base + u])],
                block_ref[u],
                preferred_element_type=jnp.float32,
            )
            total_ref[:, leaf_range(table_ref[1, base + u])] += jnp.where(
                base + u < count, product, 0.0
            )

    make(0, even_ref)

    def step(k, carry):
        make((2 * k + 1) * BATCH, odd_ref)
        use(2 * k * BATCH, even_ref)
        make((2 * k + 2) * BATCH, even_ref)
        use((2 * k + 1) * BATCH, odd_ref)
        return carry

    lax.fori_loop(0, lax.div(count + 2 * BATCH - 1, 2 * BATCH), step, 0)
    own_ref[...] = total_ref[:, :points]
    for r in range(1, rest_ref.shape[0] + 1):
        rest_ref[r - 1] = total_ref[:, r * points : (r + 1) * points].astype(jnp.bfloat16)


def pick_body(skel_ref, interp_ref, out_ref):
    turned = jnp.transpose(skel_ref[...].astype(jnp.float32)).astype(jnp.int32)
    lane = lax.broadcasted_iota(jnp.int32, (SK, LEAF_PTS), 1)
    for leaf in range(skel_ref.shape[0]):
        parent, child = divmod(leaf, CHILD)
        chosen = (turned[:, leaf : leaf + 1] == lane).astype(jnp.float32).astype(jnp.bfloat16)
        out_ref[parent, :, child * LEAF_PTS : (child + 1) * LEAF_PTS] = jnp.dot(
            interp_ref[parent, :, child * SK : (child + 1) * SK],
            chosen,
            preferred_element_type=jnp.float32,
        ).astype(jnp.bfloat16)


def merge_body(n_local, n_chunk, *refs):
    locals_ = refs[:n_local]
    owns = refs[n_local : n_local + n_chunk]
    arrived = refs[n_local + n_chunk : n_local + 2 * n_chunk]
    pick_ref, near_ref, merged_ref, energy_ref = refs[n_local + 2 * n_chunk :]
    width = locals_[0].shape[1]
    for i in range(n_local):
        columns = slice(i * width, (i + 1) * width)
        first = 0
        for own_ref, arrived_ref in zip(owns, arrived):
            rows = slice(first, first + own_ref.shape[0])
            first += own_ref.shape[0]
            near_ref[rows, columns] = (
                locals_[i][rows, :]
                + own_ref[:, columns]
                + arrived_ref[:, columns].astype(jnp.float32)
            )
    parents, _, width = pick_ref.shape
    for p in range(parents):
        merged = lax.dot_general(
            near_ref[:, p * width : (p + 1) * width].astype(jnp.bfloat16),
            pick_ref[p],
            (((1,), (1,)), ((), ())),
            preferred_element_type=jnp.float32,
        )
        merged_ref[:, p * SK2 : (p + 1) * SK2] = merged
        energy_ref[p : p + 1, :] = jnp.broadcast_to(
            jnp.sum(jnp.sum(merged * merged, axis=0, keepdims=True), axis=1, keepdims=True),
            (1, LEAF_PTS),
        )


def scale_body(count, merged_ref, energy_ref, out_ref):
    parents = energy_ref.shape[0]
    for p in range(parents):
        factor = lax.rsqrt(energy_ref[p : p + 1, 0:SK2] / count + 1e-06)
        out_ref[:, p * SK2 : (p + 1) * SK2] = merged_ref[:, p * SK2 : (p + 1) * SK2] * factor


def call(body, out_shape, in_specs, scratch=(), micros=1.0):
    many = isinstance(out_shape, (tuple, list))
    return pl.pallas_call(
        body,
        out_shape=out_shape,
        in_specs=in_specs,
        out_specs=[VMEM] * len(out_shape) if many else VMEM,
        scratch_shapes=list(scratch),
        compiler_params=pltpu.CompilerParams(vmem_limit_bytes=VMEM_LIMIT),
        cost_estimate=pl.CostEstimate(
            flops=int(micros * 1e7), bytes_accessed=int(micros * 3e4), transcendentals=0
        ),
    )


def features_of(points, sources, targets):
    return call(
        functools.partial(feature_body, len(sources), len(targets)),
        [
            jax.ShapeDtypeStruct((FEATURES, len(sources) * points), jnp.bfloat16),
            jax.ShapeDtypeStruct((FEATURES, len(targets) * points), jnp.bfloat16),
        ],
        [VMEM] * (len(sources) + len(targets)),
        [pltpu.VMEM((FEATURES, points), jnp.float32)],
    )(*sources, *targets)


def exchange(array, axis, bit):
    size = lax.axis_size(axis)
    return lax.ppermute(array, axis, [(i, i ^ bit) for i in range(size)])


def after(array, *others):
    return lax.optimization_barrier((array, *others))[0]


def far_table(pairs, me, masks, outer, leaf_dev, length):
    owners = me ^ jnp.array(masks, jnp.int32)
    source = pairs[:, 0] - owners[:, None] * leaf_dev
    source += jnp.arange(4, dtype=jnp.int32)[:, None] * leaf_dev
    relation = (pairs[:, 1] // leaf_dev) ^ me
    inside = ((relation & outer) == 0).reshape(-1)
    target = (relation // 2) * leaf_dev + pairs[:, 1] % leaf_dev
    iota = jnp.arange(inside.shape[0], dtype=jnp.int32)
    place = jnp.sum(
        (inside[:, None] & (iota[:, None] < iota[None, :])).astype(jnp.int32), axis=0
    )
    place = jnp.where(inside, place, -1)
    hit = place[None, None, :] == jnp.arange(length, dtype=jnp.int32)[None, :, None]
    codes = jnp.stack([source.reshape(-1), target.reshape(-1)])
    return (
        jnp.sum(inside.astype(jnp.int32)).reshape(1),
        jnp.sum(jnp.where(hit, codes[:, None, :], 0), axis=2),
    )


def per_device(coords, weights, omega, near_local, far_pairs, skel_rows, parent_interp):
    n_leaf = lax.axis_size("leaf")
    points = coords.shape[1]
    leaf_dev = points // LEAF_PTS
    probe_dev = omega.shape[0]
    parent_dev = leaf_dev // CHILD
    me = lax.axis_index("leaf")
    top, low = n_leaf // 2, 1
    dests = n_leaf // 4
    pair_dev = far_pairs.shape[1]
    unit = probe_dev // sum(CHUNKS)
    chunks = [(unit * sum(CHUNKS[:i]), unit * c) for i, c in enumerate(CHUNKS)]

    omega_across = exchange(omega, "leaf", top)
    pair_columns = 2 * pair_dev // 4
    sent = jnp.concatenate(
        [
            jnp.concatenate([coords, weights[None]], axis=0),
            far_pairs.reshape(4, pair_columns).astype(jnp.float32),
        ],
        axis=1,
    )
    across = exchange(sent, "leaf", top)

    source, target = features_of(points, [sent], [sent])
    part_points = points // LOCAL_PARTS
    entries = near_local.shape[1]

    def local_part(i, table):
        return call(
            functools.partial(local_body, i * part_points // LEAF_PTS),
            jax.ShapeDtypeStruct((probe_dev, part_points), jnp.float32),
            [SMEM, SMEM, VMEM, VMEM, VMEM],
            [pltpu.VMEM((entries * LEAF_PTS, LEAF_PTS), jnp.bfloat16)] * 2,
            micros=16.0 / LOCAL_PARTS,
        )((me * leaf_dev).reshape(1), table, target, source, omega)

    omega_beside = exchange(omega, "leaf", low)
    beside = exchange(sent, "leaf", low)
    partners = [exchange(sent, "leaf", 2 * r) for r in range(1, dests)]
    both = exchange(across, "leaf", low)
    local = [local_part(i, near_local) for i in range(LOCAL_PARTS)]
    omega_across = after(omega_across, *local)
    relayed = []
    for first, size in chunks:
        part = omega_across[first : first + size]
        if relayed:
            part = after(omega_across, relayed[-1])[first : first + size]
        relayed.append(exchange(part, "leaf", low))

    bundles = [sent, across, beside, both]
    pairs = jnp.stack([b[:, points:].astype(jnp.int32).reshape(2, pair_dev) for b in bundles])
    pairs = after(pairs, omega_across)
    rounds = (dests * 4 * CAP + 2 * BATCH - 1) // (2 * BATCH)
    far_count, codes = far_table(
        pairs, me, [0, top, low, top | low], top | low, leaf_dev, (2 * rounds + 1) * BATCH
    )
    far_source, far_target = features_of(points, bundles, [sent, *partners])
    owns, arrived = [], []
    for (first, size), omega_both in zip(chunks, relayed):
        own, rest = call(
            functools.partial(far_body, first),
            [
                jax.ShapeDtypeStruct((size, points), jnp.float32),
                jax.ShapeDtypeStruct((dests - 1, size, points), jnp.bfloat16),
            ],
            [SMEM, SMEM] + [VMEM] * 6,
            [
                pltpu.VMEM((BATCH, LEAF_PTS, LEAF_PTS), jnp.bfloat16),
                pltpu.VMEM((BATCH, LEAF_PTS, LEAF_PTS), jnp.bfloat16),
                pltpu.VMEM((size, dests * points), jnp.float32),
                pltpu.VMEM((size, 4 * points), jnp.bfloat16),
            ],
            micros=4.0,
        )(
            far_count, codes, far_source, far_target, omega, omega_across, omega_beside, omega_both
        )
        half = dests // 2
        while half > 1:
            got = exchange(rest[half - 1 :], "leaf", 2 * half)
            own = own + got[0].astype(jnp.float32)
            rest = rest[: half - 1] + got[1:]
            half //= 2
        owns.append(own)
        arrived.append(exchange(rest[0], "leaf", 2))
    pick = call(
        pick_body,
        jax.ShapeDtypeStruct((parent_dev, SK2, CHILD * LEAF_PTS), jnp.bfloat16),
        [VMEM] * 2,
    )(skel_rows, parent_interp.transpose(0, 2, 1))
    near, merged, energy = call(
        functools.partial(merge_body, LOCAL_PARTS, len(chunks)),
        [
            jax.ShapeDtypeStruct((probe_dev, points), jnp.float32),
            jax.ShapeDtypeStruct((probe_dev, parent_dev * SK2), jnp.float32),
            jax.ShapeDtypeStruct((parent_dev, LEAF_PTS), jnp.float32),
        ],
        [VMEM] * (LOCAL_PARTS + 2 * len(chunks) + 1),
        micros=2.0,
    )(*local, *owns, *arrived, pick)
    energy = lax.psum(energy, "probe")
    parent = call(
        functools.partial(scale_body, float(SK2 * probe_dev * lax.axis_size("probe"))),
        jax.ShapeDtypeStruct((probe_dev, parent_dev * SK2), jnp.float32),
        [VMEM] * 2,
    )(merged, energy)
    return near, parent


def solution(mesh):
    return jax.shard_map(
        per_device,
        mesh=mesh,
        in_specs=(
            P(None, "leaf"),
            P("leaf"),
            P("probe", "leaf"),
            P("leaf", None),
            P(None, "leaf"),
            P("leaf", None),
            P("leaf", None, None),
        ),
        out_specs=(P("probe", "leaf"), P("probe", "leaf")),
        check_vma=False,
    )
```

time: 127 us -> 70.7 us (0.56)
  Pallas kernels: 69.9 us -> 28.4 us
  waiting for transfers between devices: 31.2 us -> 16.4 us
  starting transfers between devices: 10.1 us -> 12.3 us
  local copies, waits for them, and re-layouts: 5.16 us -> 3.55 us
  matrix products: 1.32 us -> 0 us
    pallas_call x3 -> x7, Pallas kernels: 69.2 us -> 27.7 us  [the longest x1 16.1 us: local_part(): call(functools.partial(local_body, i * part_points // LEAF_PTS), jax.Shap...]
    ppermute x8 -> x10, waiting for transfers between devices: 31.2 us -> 16.4 us  [exchange(): return lax.ppermute(array, axis, [(i, i ^ bit) for i in range(size)])]
    ppermute x8 -> x10, starting transfers between devices: 10.1 us -> 12.3 us  [exchange(): return lax.ppermute(array, axis, [(i, i ^ bit) for i in range(size)])]
    convert_element_type x1 -> x0, local copies, waits for them, and re-layouts: 1.52 us -> none  [per_device(): pick = pick.astype(jnp.bfloat16).reshape(parent_dev, CHILD * LEAF_PTS, SK2)]
    dot_general x1 -> x0, matrix products: 1.32 us -> none  [per_device(): jnp.einsum('lir,lrk->lik', rows, weights_of, preferred_element_type=jnp.f...]
    unnamed x19 -> x17, local copies, waits for them, and re-layouts: 3.24 us -> 1.93 us
  transfers between devices with their start and end apart: 8 -> 10, of which waited for: 2 -> 4; matrix products, arithmetic and copies ran while one was open for 5% -> 4% of each run, Pallas kernels for 31% -> 38%
where the time goes in v2:
time: 70.7 us; the launch traced here: 69.8 us
  Pallas kernels  28.4 us (40%)
  waiting for transfers between devices  16.4 us (23%)
  starting transfers between devices  12.3 us (17%)
  blocking collectives  5.63 us (8%)
  local copies, waits for them, and re-layouts  3.55 us (5%)
  other arithmetic  2.62 us (4%)
  between operations  0.82 us (1%)
    ppermute x10, waiting for transfers between devices, exchange(): return lax.ppermute(array, axis, [(i, i ^ bit) for i in range(size)])  16.4 us
    pallas_call x1, Pallas kernels, local_part(): call(functools.partial(local_body, i * part_points // LEAF_PTS), jax.Shap...  16.1 us
    ppermute x10, starting transfers between devices, exchange(): return lax.ppermute(array, axis, [(i, i ^ bit) for i in range(size)])  12.3 us
    pallas_call x2, Pallas kernels, per_device(): call(functools.partial(far_body, first), [jax.ShapeDtypeStruct((size, poi...  8.09 us
    psum x1, blocking collectives, per_device(): energy = lax.psum(energy, 'probe')  5.63 us
    unnamed x17, local copies, waits for them, and re-layouts  1.93 us
    pallas_call x2, Pallas kernels, features_of(): call(functools.partial(feature_body, len(sources), len(targets)), [jax.Sh...  1.72 us
  transfers between devices with their start and end apart: 10, of which 4 were waited for; matrix products, arithmetic and copies ran while one was open for 4% of the time, Pallas kernels for 38%

profile of v2, /device:TPU:0, one launch (start us, length us, event | category | flops | bytes accessed | tf_op | source)
XLA Modules:
  0.0 69.8 jit_solution(15072052650034355126)
XLA Ops:
  0.6 0.7 convert_bitcast_fusion
  1.4 0.9 %pad_maximum_fusion.refs_0_.refs_1_.refs_4_ = f32[4,4128]{1,0:T(4,128)S(1)} fusion(f32[4,32]{1,0:T(4,128)S(1)} %convert_element_type.32, f32[1,4096]{1,0:T(1,128)} %bitcast.12, f32[3,4096]{1,0:T(4,128)} %param.8), kind=kLoop, calls=%fused_computation.5 | loop fusion | flops 33024 | bytes 132096 | tf_op jit(solution)/shard_map/concatenate | solution.py:284
  2.3 4.1 %collective-permute-start = (f32[4,4128]{1,0:T(4,128)S(1)}, f32[4,4128]{1,0:T(4,128)S(1)}, u32[]{:S(2)}, u32[]{:S(2)}) collective-permute-start(f32[4,4128]{1,0:T(4,128)S(1)} %pad_maximum_fusion.refs_0_.refs_1_.refs_4_), channel_id=1, source_target_pairs={{0,16},{4,20},{8,24},{12,28},{16,0},{20,4},{24,8},{28,12},{1,17},{... | collective-permute-start | bytes 198152 | tf_op jit(solution)/shard_map/ppermute | solution.py:242
  6.4 1.5 %collective-permute-start.1 = (f32[4,4128]{1,0:T(4,128)S(1)}, f32[4,4128]{1,0:T(4,128)S(1)}, u32[]{:S(2)}, u32[]{:S(2)}) collective-permute-start(f32[4,4128]{1,0:T(4,128)S(1)} %pad_maximum_fusion.refs_0_.refs_1_.refs_4_), channel_id=1, source_target_pairs={{0,4},{4,0},{8,12},{12,8},{16,20},{20,16},{24,28},{28,24},{1,5},{5... | collective-permute-start | bytes 198152 | tf_op jit(solution)/shard_map/ppermute | solution.py:242
  7.9 1.6 %collective-permute-start.4 = (f32[4,4128]{1,0:T(4,128)S(1)}, f32[4,4128]{1,0:T(4,128)S(1)}, u32[]{:S(2)}, u32[]{:S(2)}) collective-permute-start(f32[4,4128]{1,0:T(4,128)S(1)} %pad_maximum_fusion.refs_0_.refs_1_.refs_4_), channel_id=1, source_target_pairs={{0,8},{4,12},{8,0},{12,4},{16,24},{20,28},{24,16},{28,20},{1,9},{5... | collective-permute-start | bytes 198152 | tf_op jit(solution)/shard_map/ppermute | solution.py:242
  11.2 1.0 %copy-done = bf16[64,4096]{1,0:T(8,128)(2,1)S(1)} copy-done((bf16[64,4096]{1,0:T(8,128)(2,1)S(1)}, bf16[64,4096]{1,0:T(8,128)(2,1)}, u32[]{:S(2)}) %copy-start) | copy-done | bytes 524312
  12.2 16.1 %shard_map.96.refs_0_ = f32[64,4096]{1,0:T(8,128)S(1)} custom-call(s32[1]{0:T(128)} %bitcast.offset_ref, s32[32,24]{1,0:T(8,128)S(1)} %copy.11.near_ref, bf16[32,4096]{1,0:T(8,128)(2,1)S(1)} %get-tuple-element.16.target_ref, bf16[32,4096]{1,0:T(8,128)(2,1)S(1)} %get-tuple-element.17.source_ref, bf16[64,4096]{1,0:T(8,128)(2,1)S(1)} %copy-done), custom_call_target="tpu_custom_call" | custom-call | flops 160000000 | bytes 480000 | tf_op jit(solution)/shard_map/pallas_call | solution.py:298
  28.3 1.5 %collective-permute-start.2 = (f32[4,4128]{1,0:T(4,128)S(1)}, f32[4,4128]{1,0:T(4,128)S(1)}, u32[]{:S(2)}, u32[]{:S(2)}) collective-permute-start(f32[4,4128]{1,0:T(4,128)S(1)} %collective-permute-done.refs_1_), channel_id=1, source_target_pairs={{0,4},{4,0},{8,12},{12,8},{16,20},{20,16},{24,28},{28,24},{1,5},{5... | collective-permute-start | bytes 198152 | tf_op jit(solution)/shard_map/ppermute | solution.py:242
  30.0 2.6 %collective-permute-done.2.refs_3_ = f32[4,4128]{1,0:T(4,128)S(1)} collective-permute-done((f32[4,4128]{1,0:T(4,128)S(1)}, f32[4,4128]{1,0:T(4,128)S(1)}, u32[]{:S(2)}, u32[]{:S(2)}) %collective-permute-start.2) | collective-permute-done | bytes 66080 | tf_op jit(solution)/shard_map/ppermute | solution.py:242
  32.8 1.3 %shard_map.97 = (bf16[32,16384]{1,0:T(8,128)(2,1)S(1)}, bf16[32,8192]{1,0:T(8,128)(2,1)S(1)}) custom-call(f32[4,4128]{1,0:T(4,128)S(1)} %pad_maximum_fusion.refs_0_.refs_1_.refs_4_, f32[4,4128]{1,0:T(4,128)S(1)} %collective-permute-done.refs_1_, f32[4,4128]{1,0:T(4,128)S(1)} %collective-permute-done.1.refs_2_, f32[4,4128]{1,0:T(4,128)S(1)} %collective-permute-done.2.refs_3_, ...), custom_call_target="tpu_custom_call" | custom-call | flops 10000000 | bytes 30000 | tf_op jit(solution)/shard_map/pallas_call | solution.py:229
  34.1 0.8 %copy-done.2 = bf16[32,8192]{1,0:T(8,128)(2,1)} copy-done((bf16[32,8192]{1,0:T(8,128)(2,1)}, bf16[32,8192]{1,0:T(8,128)(2,1)S(1)}, u32[]{:S(2)}) %copy-start.2) | copy-done | bytes 524312
  34.9 0.7 %slice.27 = bf16[32,4096]{1,0:T(8,128)(2,1)} slice(bf16[64,4096]{1,0:T(8,128)(2,1)S(1)} %collective-permute-done.3.refs_1_), slice={[0:32], [0:4096]} | slice | bytes 524288 | tf_op jit(solution)/shard_map/slice | solution.py:314
  35.6 0.6 slice_reduce_fusion.1
  36.5 1.5 %collective-permute-start.6 = (bf16[32,4096]{1,0:T(8,128)(2,1)}, bf16[32,4096]{1,0:T(8,128)(2,1)S(1)}, u32[]{:S(2)}, u32[]{:S(2)}) collective-permute-start(bf16[32,4096]{1,0:T(8,128)(2,1)} %slice.27), channel_id=1, source_target_pairs={{0,4},{4,0},{8,12},{12,8},{16,20},{20,16},{24,28},{28,24},{1,5},{5... | collective-permute-start | bytes 786440 | tf_op jit(solution)/shard_map/ppermute | solution.py:242
  38.2 6.5 %collective-permute-done.6.refs_3_ = bf16[32,4096]{1,0:T(8,128)(2,1)S(1)} collective-permute-done((bf16[32,4096]{1,0:T(8,128)(2,1)}, bf16[32,4096]{1,0:T(8,128)(2,1)S(1)}, u32[]{:S(2)}, u32[]{:S(2)}) %collective-permute-start.6) | collective-permute-done | bytes 262176 | tf_op jit(solution)/shard_map/ppermute | solution.py:242
  45.5 4.0 %shard_map.98 = (f32[32,4096]{1,0:T(8,128)S(1)}, bf16[1,32,4096]{2,1,0:T(8,128)(2,1)S(1)}) custom-call(s32[1]{0:T(128)} %bitcast.3.count_ref, s32[2,136]{1,0:T(2,128)S(1)} %select_reduce_fusion.table_ref, bf16[32,16384]{1,0:T(8,128)(2,1)S(1)} %get-tuple-element.20.source_ref, bf16[32,8192]{1,0:T(8,128)(2,1)S(1)} %copy-done.3, ...), custom_call_target="tpu_custom_call" | custom-call | flops 40000000 | bytes 120000 | tf_op jit(solution)/shard_map/pallas_call | solution.py:329
  49.5 0.6 collective-permute-start.8
  50.2 1.6 %collective-permute-done.7.refs_3_ = bf16[32,4096]{1,0:T(8,128)(2,1)S(1)} collective-permute-done((bf16[32,4096]{1,0:T(8,128)(2,1)S(1)}, bf16[32,4096]{1,0:T(8,128)(2,1)S(1)}, u32[]{:S(2)}, u32[]{:S(2)}) %collective-permute-start.7) | collective-permute-done | bytes 262176 | tf_op jit(solution)/shard_map/ppermute | solution.py:242
  51.8 4.0 %shard_map.99 = (f32[32,4096]{1,0:T(8,128)S(1)}, bf16[1,32,4096]{2,1,0:T(8,128)(2,1)S(1)}) custom-call(s32[1]{0:T(128)} %bitcast.3.count_ref, s32[2,136]{1,0:T(2,128)S(1)} %select_reduce_fusion.table_ref, bf16[32,16384]{1,0:T(8,128)(2,1)S(1)} %get-tuple-element.20.source_ref, bf16[32,8192]{1,0:T(8,128)(2,1)S(1)} %copy-done.3, ...), custom_call_target="tpu_custom_call" | custom-call | flops 40000000 | bytes 120000 | tf_op jit(solution)/shard_map/pallas_call | solution.py:329
  55.9 0.6 shard_map.100.refs_5_
  56.6 5.7 %collective-permute-done.9.refs_4_ = bf16[32,4096]{1,0:T(8,128)(2,1)S(1)} collective-permute-done((bf16[32,4096]{1,0:T(8,128)(2,1)S(1)}, bf16[32,4096]{1,0:T(8,128)(2,1)S(1)}, u32[]{:S(2)}, u32[]{:S(2)}) %collective-permute-start.9) | collective-permute-done | bytes 262176 | tf_op jit(solution)/shard_map/ppermute | solution.py:242
  62.3 1.2 %shard_map.101 = (f32[64,4096]{1,0:T(8,128)}, f32[64,256]{1,0:T(8,128)S(1)}, f32[4,128]{1,0:T(4,128)S(1)}) custom-call(f32[64,4096]{1,0:T(8,128)S(1)} %shard_map.96.refs_0_, f32[32,4096]{1,0:T(8,128)S(1)} %get-tuple-element.22.refs_1_, f32[32,4096]{1,0:T(8,128)S(1)} %get-tuple-element.24.refs_2_, bf16[32,4096]{1,0:T(8,128)(2,1)S(1)} %collective-permute-done.8.refs_3_, ...), custom_call_target="tpu_custom_call" | custom-call | flops 20000000 | bytes 60000 | tf_op jit(solution)/shard_map/pallas_call | solution.py:359
  63.5 5.6 %psum.7.energy_ref = f32[4,128]{1,0:T(4,128)S(1)} all-reduce(f32[4,128]{1,0:T(4,128)S(1)} %get-tuple-element.29), channel_id=1, replica_groups=mesh['leaf'=8,'probe'=4] {'probe'}, use_global_device_ids=true, to_apply=%region_3.4 | all-reduce | flops 512 | bytes 4096 | tf_op jit(solution)/shard_map/psum | solution.py:369
  69.1 0.7 %shard_map.102 = f32[64,256]{1,0:T(8,128)} custom-call(f32[64,256]{1,0:T(8,128)S(1)} %get-tuple-element.28.merged_ref, f32[4,128]{1,0:T(4,128)S(1)} %psum.7.energy_ref), custom_call_target="tpu_custom_call" | custom-call | flops 10000000 | bytes 30000 | tf_op jit(solution)/shard_map/pallas_call | solution.py:370
  (51 shorter events, 3.3 us)
Async XLA Ops:
  1.4 9.0 %copy-start.7 = (s32[4]{0:T(128)S(1)}, s32[4]{0:T(128)}, u32[]{:S(2)}) copy-start(s32[4]{0:T(128)} %constant.51.clone) | copy-start | bytes 52
  2.3 8.1 %copy-start.6 = (s32[32,24]{0,1:T(8,128)S(1)}, s32[32,24]{0,1:T(8,128)}, u32[]{:S(2)}) copy-start(s32[32,24]{0,1:T(8,128)} %param.11) | copy-start | bytes 9220
  2.3 26.0 %collective-permute-start = (f32[4,4128]{1,0:T(4,128)S(1)}, f32[4,4128]{1,0:T(4,128)S(1)}, u32[]{:S(2)}, u32[]{:S(2)}) collective-permute-start(f32[4,4128]{1,0:T(4,128)S(1)} %pad_maximum_fusion.refs_0_.refs_1_.refs_4_), channel_id=1, source_target_pairs={{0,16},{4,20},{8,24},{12,28},{16,0},{20,4},{24,8},{28,12},{1,17},{... | collective-permute-start | bytes 198152 | tf_op jit(solution)/shard_map/ppermute | solution.py:242
  6.4 23.4 %collective-permute-start.1 = (f32[4,4128]{1,0:T(4,128)S(1)}, f32[4,4128]{1,0:T(4,128)S(1)}, u32[]{:S(2)}, u32[]{:S(2)}) collective-permute-start(f32[4,4128]{1,0:T(4,128)S(1)} %pad_maximum_fusion.refs_0_.refs_1_.refs_4_), channel_id=1, source_target_pairs={{0,4},{4,0},{8,12},{12,8},{16,20},{20,16},{24,28},{28,24},{1,5},{5... | collective-permute-start | bytes 198152 | tf_op jit(solution)/shard_map/ppermute | solution.py:242
  7.9 24.8 %collective-permute-start.4 = (f32[4,4128]{1,0:T(4,128)S(1)}, f32[4,4128]{1,0:T(4,128)S(1)}, u32[]{:S(2)}, u32[]{:S(2)}) collective-permute-start(f32[4,4128]{1,0:T(4,128)S(1)} %pad_maximum_fusion.refs_0_.refs_1_.refs_4_), channel_id=1, source_target_pairs={{0,8},{4,12},{8,0},{12,4},{16,24},{20,28},{24,16},{28,20},{1,9},{5... | collective-permute-start | bytes 198152 | tf_op jit(solution)/shard_map/ppermute | solution.py:242
  9.5 25.4 %collective-permute-start.3 = (bf16[64,4096]{1,0:T(8,128)(2,1)}, bf16[64,4096]{1,0:T(8,128)(2,1)S(1)}, u32[]{:S(2)}, u32[]{:S(2)}) collective-permute-start(bf16[64,4096]{1,0:T(8,128)(2,1)} %refs_0_.3), channel_id=1, source_target_pairs={{0,16},{4,20},{8,24},{12,28},{16,0},{20,4},{24,8},{28,12},{1,17},{... | collective-permute-start | bytes 1572872 | tf_op jit(solution)/shard_map/ppermute | solution.py:242
  9.9 35.6 %collective-permute-start.5 = (bf16[64,4096]{1,0:T(8,128)(2,1)}, bf16[64,4096]{1,0:T(8,128)(2,1)}, u32[]{:S(2)}, u32[]{:S(2)}) collective-permute-start(bf16[64,4096]{1,0:T(8,128)(2,1)} %refs_0_.3), channel_id=1, source_target_pairs={{0,4},{4,0},{8,12},{12,8},{16,20},{20,16},{24,28},{28,24},{1,5},{5... | collective-permute-start | bytes 1572872 | tf_op jit(solution)/shard_map/ppermute | solution.py:242
  11.2 1.0 %copy-start = (bf16[64,4096]{1,0:T(8,128)(2,1)S(1)}, bf16[64,4096]{1,0:T(8,128)(2,1)}, u32[]{:S(2)}) copy-start(bf16[64,4096]{1,0:T(8,128)(2,1)} %refs_0_.3) | copy-start | bytes 1572868
  28.3 4.4 %collective-permute-start.2 = (f32[4,4128]{1,0:T(4,128)S(1)}, f32[4,4128]{1,0:T(4,128)S(1)}, u32[]{:S(2)}, u32[]{:S(2)}) collective-permute-start(f32[4,4128]{1,0:T(4,128)S(1)} %collective-permute-done.refs_1_), channel_id=1, source_target_pairs={{0,4},{4,0},{8,12},{12,8},{16,20},{20,16},{24,28},{28,24},{1,5},{5... | collective-permute-start | bytes 198152 | tf_op jit(solution)/shard_map/ppermute | solution.py:242
  34.1 0.8 %copy-start.2 = (bf16[32,8192]{1,0:T(8,128)(2,1)}, bf16[32,8192]{1,0:T(8,128)(2,1)S(1)}, u32[]{:S(2)}) copy-start(bf16[32,8192]{1,0:T(8,128)(2,1)S(1)} %get-tuple-element.21.target_ref) | copy-start | bytes 1572868
  34.9 10.6 %copy-start.1 = (bf16[64,4096]{1,0:T(8,128)(2,1)S(1)}, bf16[64,4096]{1,0:T(8,128)(2,1)}, u32[]{:S(2)}) copy-start(bf16[64,4096]{1,0:T(8,128)(2,1)} %refs_0_.3) | copy-start | bytes 1572868
  36.5 8.2 %collective-permute-start.6 = (bf16[32,4096]{1,0:T(8,128)(2,1)}, bf16[32,4096]{1,0:T(8,128)(2,1)S(1)}, u32[]{:S(2)}, u32[]{:S(2)}) collective-permute-start(bf16[32,4096]{1,0:T(8,128)(2,1)} %slice.27), channel_id=1, source_target_pairs={{0,4},{4,0},{8,12},{12,8},{16,20},{20,16},{24,28},{28,24},{1,5},{5... | collective-permute-start | bytes 786440 | tf_op jit(solution)/shard_map/ppermute | solution.py:242
  38.2 7.3 %copy-start.3 = (bf16[32,8192]{1,0:T(8,128)(2,1)S(1)}, bf16[32,8192]{1,0:T(8,128)(2,1)}, u32[]{:S(2)}) copy-start(bf16[32,8192]{1,0:T(8,128)(2,1)} %copy-done.2) | copy-start | bytes 1572868
  44.7 7.1 %collective-permute-start.7 = (bf16[32,4096]{1,0:T(8,128)(2,1)S(1)}, bf16[32,4096]{1,0:T(8,128)(2,1)S(1)}, u32[]{:S(2)}, u32[]{:S(2)}) collective-permute-start(bf16[32,4096]{1,0:T(8,128)(2,1)S(1)} %slice.28), channel_id=1, source_target_pairs={{0,4},{4,0},{8,12},{12,8},{16,20},{20,16},{24,28},{28,24},{1,5},{5... | collective-permute-start | bytes 786440 | tf_op jit(solution)/shard_map/ppermute | solution.py:242
  49.5 6.4 %copy-start.4 = (bf16[4,256,64]{1,2,0:T(8,128)(2,1)S(1)}, bf16[4,256,64]{1,2,0:T(8,128)(2,1)}, u32[]{:S(2)}) copy-start(bf16[4,256,64]{1,2,0:T(8,128)(2,1)} %param.14) | copy-start | bytes 393220
  49.5 7.0 %collective-permute-start.8 = (bf16[32,4096]{1,0:T(8,128)(2,1)S(1)}, bf16[32,4096]{1,0:T(8,128)(2,1)S(1)}, u32[]{:S(2)}, u32[]{:S(2)}) collective-permute-start(bf16[32,4096]{1,0:T(8,128)(2,1)S(1)} %bitcast.10), channel_id=1, source_target_pairs={{0,8},{4,12},{8,0},{12,4},{16,24},{20,28},{24,16},{28,20},{1,9},{5... | collective-permute-start | bytes 786440 | tf_op jit(solution)/shard_map/ppermute | solution.py:242
  51.8 4.1 %copy-start.5 = (s32[32,32]{1,0:T(8,128)S(1)}, s32[32,32]{1,0:T(8,128)}, u32[]{:S(2)}) copy-start(s32[32,32]{1,0:T(8,128)} %skel_ref.1) | copy-start | bytes 12292
  55.8 6.4 %collective-permute-start.9 = (bf16[32,4096]{1,0:T(8,128)(2,1)S(1)}, bf16[32,4096]{1,0:T(8,128)(2,1)S(1)}, u32[]{:S(2)}, u32[]{:S(2)}) collective-permute-start(bf16[32,4096]{1,0:T(8,128)(2,1)S(1)} %bitcast.11), channel_id=1, source_target_pairs={{0,8},{4,12},{8,0},{12,4},{16,24},{20,28},{24,16},{28,20},{1,9},{5... | collective-permute-start | bytes 786440 | tf_op jit(solution)/shard_map/ppermute | solution.py:242

commit v3 on v2

--- a/solution.py
+++ b/solution.py
@@ -17,13 +17,14 @@
 INV_FOUR_PI = 0.07957747154594767
 
 VMEM_LIMIT = 12 * 1024 * 1024
-BATCH = 8
+BATCH = 24
 FEATURES = 32
 CHUNKS = (1, 1)
 LOCAL_PARTS = 1
 
 SMEM = pl.BlockSpec(memory_space=pltpu.SMEM)
 VMEM = pl.BlockSpec(memory_space=pltpu.VMEM)
+HBM = pl.BlockSpec(memory_space=pltpu.HBM)
 
 
 def leaf_range(leaf):
@@ -80,8 +81,11 @@
 
 
 def local_body(
-    first, offset_ref, near_ref, target_ref, source_ref, omega_ref, out_ref, even_ref, odd_ref
+    first, offset_ref, near_ref, target_ref, source_ref, probes_ref, out_ref,
+    even_ref, odd_ref, omega_ref, sem,
 ):
+    fetch = pltpu.make_async_copy(probes_ref, omega_ref, sem)
+    fetch.start()
     entries = near_ref.shape[1]
     leaves = out_ref.shape[1] // LEAF_PTS
     offset = offset_ref[0]
@@ -103,6 +107,7 @@
         )
 
     make(0, even_ref)
+    fetch.wait()
 
     def step(k, carry):
         make(2 * k + 1, odd_ref)
@@ -116,43 +121,42 @@
 
 def far_body(first, count_ref, table_ref, source_ref, target_ref, *refs):
     omegas = refs[:4]
-    own_ref, rest_ref, even_ref, odd_ref, total_ref, omega_ref = refs[4:]
+    own_ref, rest_ref, block_ref, total_ref, omega_ref, sems = refs[4:]
     size, points = own_ref.shape
+    fetches = []
+    for k in range(4):
+        rows = pl.ds(first if k < 3 else 0, size)
+        fetches.append(
+            pltpu.make_async_copy(
+                omegas[k].at[rows, :],
+                omega_ref.at[:, k * points : (k + 1) * points],
+                sems.at[k],
+            )
+        )
+        fetches[-1].start()
     count = count_ref[0]
     total_ref[...] = jnp.zeros_like(total_ref)
-    for k in range(4):
-        cut = slice(k * points, (k + 1) * points)
-        rows = slice(first, first + size) if k < 3 else slice(0, size)
-        omega_ref[:, cut] = omegas[k][rows, :]
-
-    def make(base, block_ref):
+    for fetch in fetches:
+        fetch.wait()
+
+    def step(k, carry):
         for u in range(BATCH):
+            item = k * BATCH + u
             block_ref[u] = turned_block(
-                source_ref[:, leaf_range(table_ref[0, base + u])],
-                target_ref[:, leaf_range(table_ref[1, base + u])],
+                source_ref[:, leaf_range(table_ref[0, item])],
+                target_ref[:, leaf_range(table_ref[1, item])],
             )
-
-    def use(base, block_ref):
         for u in range(BATCH):
+            item = k * BATCH + u
             product = jnp.dot(
-                omega_ref[:, leaf_range(table_ref[0, base + u])],
+                omega_ref[:, leaf_range(table_ref[0, item])],
                 block_ref[u],
                 preferred_element_type=jnp.float32,
             )
-            total_ref[:, leaf_range(table_ref[1, base + u])] += jnp.where(
-                base + u < count, product, 0.0
-            )
-
-    make(0, even_ref)
-
-    def step(k, carry):
-        make((2 * k + 1) * BATCH, odd_ref)
-        use(2 * k * BATCH, even_ref)
-        make((2 * k + 2) * BATCH, even_ref)
-        use((2 * k + 1) * BATCH, odd_ref)
+            total_ref[:, leaf_range(table_ref[1, item])] += jnp.where(item < count, product, 0.0)
         return carry
 
-    lax.fori_loop(0, lax.div(count + 2 * BATCH - 1, 2 * BATCH), step, 0)
+    lax.fori_loop(0, lax.div(count + BATCH - 1, BATCH), step, 0)
     own_ref[...] = total_ref[:, :points]
     for r in range(1, rest_ref.shape[0] + 1):
         rest_ref[r - 1] = total_ref[:, r * points : (r + 1) * points].astype(jnp.bfloat16)
@@ -203,10 +207,11 @@
         )
 
 
-def scale_body(count, merged_ref, energy_ref, out_ref):
-    parents = energy_ref.shape[0]
-    for p in range(parents):
-        factor = lax.rsqrt(energy_ref[p : p + 1, 0:SK2] / count + 1e-06)
+def scale_body(count, merged_ref, *refs):
+    energies, out_ref = refs[:-1], refs[-1]
+    energy = sum(ref[...] for ref in energies[1:]) + energies[0][...]
+    for p in range(energy.shape[0]):
+        factor = lax.rsqrt(energy[p : p + 1, 0:SK2] / count + 1e-06)
         out_ref[:, p * SK2 : (p + 1) * SK2] = merged_ref[:, p * SK2 : (p + 1) * SK2] * factor
 
 
@@ -247,9 +252,9 @@
 
 
 def far_table(pairs, me, masks, outer, leaf_dev, length):
-    owners = me ^ jnp.array(masks, jnp.int32)
-    source = pairs[:, 0] - owners[:, None] * leaf_dev
-    source += jnp.arange(4, dtype=jnp.int32)[:, None] * leaf_dev
+    member = jnp.arange(4, dtype=jnp.int32)
+    owners = me ^ (member % 2 * masks[0] + member // 2 * masks[1])
+    source = pairs[:, 0] - ((owners - member) * leaf_dev)[:, None]
     relation = (pairs[:, 1] // leaf_dev) ^ me
     inside = ((relation & outer) == 0).reshape(-1)
     target = (relation // 2) * leaf_dev + pairs[:, 1] % leaf_dev
@@ -289,6 +294,7 @@
         axis=1,
     )
     across = exchange(sent, "leaf", top)
+    both = exchange(sent, "leaf", top | low)
 
     source, target = features_of(points, [sent], [sent])
     part_points = points // LOCAL_PARTS
@@ -298,17 +304,18 @@
         return call(
             functools.partial(local_body, i * part_points // LEAF_PTS),
             jax.ShapeDtypeStruct((probe_dev, part_points), jnp.float32),
-            [SMEM, SMEM, VMEM, VMEM, VMEM],
-            [pltpu.VMEM((entries * LEAF_PTS, LEAF_PTS), jnp.bfloat16)] * 2,
+            [SMEM, SMEM, VMEM, VMEM, HBM],
+            [pltpu.VMEM((entries * LEAF_PTS, LEAF_PTS), jnp.bfloat16)] * 2
+            + [pltpu.VMEM((probe_dev, points), jnp.bfloat16), pltpu.SemaphoreType.DMA],
             micros=16.0 / LOCAL_PARTS,
         )((me * leaf_dev).reshape(1), table, target, source, omega)
 
     omega_beside = exchange(omega, "leaf", low)
-    beside = exchange(sent, "leaf", low)
-    partners = [exchange(sent, "leaf", 2 * r) for r in range(1, dests)]
-    both = exchange(across, "leaf", low)
     local = [local_part(i, near_local) for i in range(LOCAL_PARTS)]
-    omega_across = after(omega_across, *local)
+    omega_across = after(omega_across, omega_beside, *local)
+    late = after(sent, omega_across)
+    beside = exchange(late, "leaf", low)
+    partners = [exchange(late, "leaf", 2 * r) for r in range(1, dests)]
     relayed = []
     for first, size in chunks:
         part = omega_across[first : first + size]
@@ -317,13 +324,13 @@
         relayed.append(exchange(part, "leaf", low))
 
     bundles = [sent, across, beside, both]
+    bundles = list(lax.optimization_barrier((*bundles, relayed[0]))[:-1])
     pairs = jnp.stack([b[:, points:].astype(jnp.int32).reshape(2, pair_dev) for b in bundles])
-    pairs = after(pairs, omega_across)
-    rounds = (dests * 4 * CAP + 2 * BATCH - 1) // (2 * BATCH)
+    slots = (dests * 4 * CAP + BATCH - 1) // BATCH * BATCH
     far_count, codes = far_table(
-        pairs, me, [0, top, low, top | low], top | low, leaf_dev, (2 * rounds + 1) * BATCH
-    )
-    far_source, far_target = features_of(points, bundles, [sent, *partners])
+        pairs, me, (top, low), top | low, leaf_dev, slots
+    )
+    far_source, far_target = features_of(points, bundles, [bundles[0], *partners])
     owns, arrived = [], []
     for (first, size), omega_both in zip(chunks, relayed):
         own, rest = call(
@@ -332,12 +339,12 @@
                 jax.ShapeDtypeStruct((size, points), jnp.float32),
                 jax.ShapeDtypeStruct((dests - 1, size, points), jnp.bfloat16),
             ],
-            [SMEM, SMEM] + [VMEM] * 6,
+            [SMEM, SMEM, VMEM, VMEM] + [HBM] * 4,
             [
-                pltpu.VMEM((BATCH, LEAF_PTS, LEAF_PTS), jnp.bfloat16),
                 pltpu.VMEM((BATCH, LEAF_PTS, LEAF_PTS), jnp.bfloat16),
                 pltpu.VMEM((size, dests * points), jnp.float32),
                 pltpu.VMEM((size, 4 * points), jnp.bfloat16),
+                pltpu.SemaphoreType.DMA((4,)),
             ],
             micros=4.0,
         )(
@@ -366,12 +373,16 @@
         [VMEM] * (LOCAL_PARTS + 2 * len(chunks) + 1),
         micros=2.0,
     )(*local, *owns, *arrived, pick)
-    energy = lax.psum(energy, "probe")
+    n_probe = lax.axis_size("probe")
+    if n_probe & (n_probe - 1):
+        energies = [lax.psum(energy, "probe")]
+    else:
+        energies = [energy] + [exchange(energy, "probe", k) for k in range(1, n_probe)]
     parent = call(
-        functools.partial(scale_body, float(SK2 * probe_dev * lax.axis_size("probe"))),
+        functools.partial(scale_body, float(SK2 * probe_dev * n_probe)),
         jax.ShapeDtypeStruct((probe_dev, parent_dev * SK2), jnp.float32),
-        [VMEM] * 2,
-    )(merged, energy)
+        [VMEM] * (1 + len(energies)),
+    )(merged, *energies)
     return near, parent
 
 

time: 70.7 us -> 67 us (0.948)
  blocking collectives: 5.63 us -> 0 us
  starting transfers between devices: 12.3 us -> 17.7 us
  waiting for transfers between devices: 16.4 us -> 14.3 us
  Pallas kernels: 28.4 us -> 27.1 us
    psum x1 -> x0, blocking collectives: 5.63 us -> none  [per_device(): energy = lax.psum(energy, 'probe')]
    ppermute x10 -> x13, starting transfers between devices: 12.3 us -> 17.7 us  [exchange(): return lax.ppermute(array, axis, [(i, i ^ bit) for i in range(size)])]
    ppermute x10 -> x13, waiting for transfers between devices: 16.4 us -> 14.3 us  [exchange(): return lax.ppermute(array, axis, [(i, i ^ bit) for i in range(size)])]
    pallas_call x2, Pallas kernels: 8.09 us -> 6.74 us  [per_device(): call(functools.partial(far_body, first), [jax.ShapeDtypeStruct((size, poi...]
    slice x1, local copies, waits for them, and re-layouts: 0.73 us -> 0.02 us  [per_device(): part = omega_across[first:first + size]]
    unnamed x17 -> x16, local copies, waits for them, and re-layouts: 1.93 us -> 1.79 us
  transfers between devices with their start and end apart: 10 -> 13, of which waited for: 4 -> 7; matrix products, arithmetic and copies ran while one was open for 4% -> 6% of each run, Pallas kernels for 38% -> 38%
where the time goes in v3:
time: 67 us; the launch traced here: 65.8 us
  Pallas kernels  27.1 us (40%)
  starting transfers between devices  17.7 us (26%)
  waiting for transfers between devices  14.3 us (21%)
  local copies, waits for them, and re-layouts  3.35 us (5%)
  other arithmetic  2.59 us (4%)
  between operations  0.78 us (1%)
    ppermute x13, starting transfers between devices, exchange(): return lax.ppermute(array, axis, [(i, i ^ bit) for i in range(size)])  17.7 us
    pallas_call x1, Pallas kernels, local_part(): call(functools.partial(local_body, i * part_points // LEAF_PTS), jax.Shap...  16.1 us
    ppermute x13, waiting for transfers between devices, exchange(): return lax.ppermute(array, axis, [(i, i ^ bit) for i in range(size)])  14.3 us
    pallas_call x2, Pallas kernels, per_device(): call(functools.partial(far_body, first), [jax.ShapeDtypeStruct((size, poi...  6.74 us
    unnamed x16, local copies, waits for them, and re-layouts  1.79 us
    pallas_call x2, Pallas kernels, features_of(): call(functools.partial(feature_body, len(sources), len(targets)), [jax.Sh...  1.73 us
  transfers between devices with their start and end apart: 13, of which 7 were waited for; matrix products, arithmetic and copies ran while one was open for 6% of the time, Pallas kernels for 38%

profile of v3, /device:TPU:0, one launch (start us, length us, event | category | flops | bytes accessed | tf_op | source)
XLA Modules:
  0.0 65.8 jit_solution(5591058161065217152)
XLA Ops:
  0.6 3.0 %collective-permute-start.2 = (bf16[64,4096]{1,0:T(8,128)(2,1)}, bf16[64,4096]{1,0:T(8,128)(2,1)S(1)}, u32[]{:S(2)}, u32[]{:S(2)}) collective-permute-start(bf16[64,4096]{1,0:T(8,128)(2,1)} %refs_0_.3), channel_id=1, source_target_pairs={{0,4},{4,0},{8,12},{12,8},{16,20},{20,16},{24,28},{28,24},{1,5},{5... | collective-permute-start | bytes 1572872 | tf_op jit(solution)/shard_map/ppermute | solution.py:247
  3.7 2.6 %collective-permute-start.1 = (bf16[64,4096]{1,0:T(8,128)(2,1)}, bf16[64,4096]{1,0:T(8,128)(2,1)S(1)}, u32[]{:S(2)}, u32[]{:S(2)}) collective-permute-start(bf16[64,4096]{1,0:T(8,128)(2,1)} %refs_0_.3), channel_id=1, source_target_pairs={{0,16},{4,20},{8,24},{12,28},{16,0},{20,4},{24,8},{28,12},{1,17},{... | collective-permute-start | bytes 1572872 | tf_op jit(solution)/shard_map/ppermute | solution.py:247
  6.3 0.7 %convert_element_type.25 = f32[2,64]{1,0:T(2,128)S(1)} convert(s32[2,64]{1,0:T(2,128)} %param.11) | non-fusion elementwise | flops 128 | bytes 1024 | tf_op jit(solution)/shard_map/convert_element_type | solution.py:292
  7.7 0.9 %pad_maximum_fusion.refs_0_.refs_1_.refs_4_ = f32[4,4128]{1,0:T(4,128)S(1)} fusion(f32[4,32]{1,0:T(4,128)S(1)} %convert_element_type.26, f32[1,4096]{1,0:T(1,128)S(1)} %bitcast.10, f32[3,4096]{1,0:T(4,128)} %param.7), kind=kLoop, calls=%fused_computation.5 | loop fusion | flops 33024 | bytes 132096 | tf_op jit(solution)/shard_map/concatenate | solution.py:289
  9.1 1.0 %copy-done = bf16[64,4096]{1,0:T(8,128)(2,1)S(1)} copy-done((bf16[64,4096]{1,0:T(8,128)(2,1)S(1)}, bf16[64,4096]{1,0:T(8,128)(2,1)}, u32[]{:S(2)}) %copy-start) | copy-done | bytes 524312
  10.1 16.1 %shard_map.87.refs_0_ = f32[64,4096]{1,0:T(8,128)S(1)} custom-call(s32[1]{0:T(128)} %bitcast.offset_ref, s32[32,24]{1,0:T(8,128)S(1)} %copy.10.near_ref, bf16[32,4096]{1,0:T(8,128)(2,1)S(1)} %get-tuple-element.20.target_ref, bf16[32,4096]{1,0:T(8,128)(2,1)S(1)} %get-tuple-element.21.source_ref, bf16[64,4096]{1,0:T(8,128)(2,1)S(1)} %copy-done), custom_call_target="tpu_custom_call" | custom-call | flops 160000000 | bytes 480000 | tf_op jit(solution)/shard_map/pallas_call | solution.py:304
  26.2 3.2 %collective-permute-done.1.refs_1_ = bf16[64,4096]{1,0:T(8,128)(2,1)S(1)} collective-permute-done((bf16[64,4096]{1,0:T(8,128)(2,1)}, bf16[64,4096]{1,0:T(8,128)(2,1)S(1)}, u32[]{:S(2)}, u32[]{:S(2)}) %collective-permute-start.1) | collective-permute-done | bytes 524320 | tf_op jit(solution)/shard_map/ppermute | solution.py:247
  30.0 3.9 %collective-permute-start.4 = (f32[4,4128]{1,0:T(4,128)S(1)}, f32[4,4128]{1,0:T(4,128)S(1)}, u32[]{:S(2)}, u32[]{:S(2)}) collective-permute-start(f32[4,4128]{1,0:T(4,128)S(1)} %pad_maximum_fusion.refs_0_.refs_1_.refs_4_), channel_id=1, source_target_pairs={{0,20},{4,16},{8,28},{12,24},{16,4},{20,0},{24,12},{28,8},{1,21},{... | collective-permute-start | bytes 198152 | tf_op jit(solution)/shard_map/ppermute | solution.py:247
  34.5 1.2 %collective-permute-start.6 = (f32[4,4128]{1,0:T(4,128)S(1)}, f32[4,4128]{1,0:T(4,128)S(1)}, u32[]{:S(2)}, u32[]{:S(2)}) collective-permute-start(f32[4,4128]{1,0:T(4,128)S(1)} %pad_maximum_fusion.refs_0_.refs_1_.refs_4_), channel_id=1, source_target_pairs={{0,8},{4,12},{8,0},{12,4},{16,24},{20,28},{24,16},{28,20},{1,9},{5... | collective-permute-start | bytes 198152 | tf_op jit(solution)/shard_map/ppermute | solution.py:247
  36.3 2.5 %collective-permute-done.4.refs_3_ = f32[4,4128]{1,0:T(4,128)S(1)} collective-permute-done((f32[4,4128]{1,0:T(4,128)S(1)}, f32[4,4128]{1,0:T(4,128)S(1)}, u32[]{:S(2)}, u32[]{:S(2)}) %collective-permute-start.4) | collective-permute-done | bytes 66080 | tf_op jit(solution)/shard_map/ppermute | solution.py:247
  38.8 0.8 %collective-permute-done.3.refs_2_ = f32[4,4128]{1,0:T(4,128)S(1)} collective-permute-done((f32[4,4128]{1,0:T(4,128)S(1)}, f32[4,4128]{1,0:T(4,128)S(1)}, u32[]{:S(2)}, u32[]{:S(2)}) %collective-permute-start.3) | collective-permute-done | bytes 66080 | tf_op jit(solution)/shard_map/ppermute | solution.py:247
  39.9 0.7 slice_reduce_fusion.1
  40.9 0.7 %slice.32 = bf16[32,4096]{1,0:T(8,128)(2,1)} slice(bf16[64,4096]{1,0:T(8,128)(2,1)S(1)} %collective-permute-done.1.refs_1_), slice={[32:64], [0:4096]} | slice | bytes 524288 | tf_op jit(solution)/shard_map/slice | solution.py:323
  42.3 1.3 %shard_map.88 = (bf16[32,16384]{1,0:T(8,128)(2,1)S(1)}, bf16[32,8192]{1,0:T(8,128)(2,1)S(1)}) custom-call(f32[4,4128]{1,0:T(4,128)S(1)} %pad_maximum_fusion.refs_0_.refs_1_.refs_4_, f32[4,4128]{1,0:T(4,128)S(1)} %collective-permute-done.refs_1_, f32[4,4128]{1,0:T(4,128)S(1)} %collective-permute-done.3.refs_2_, f32[4,4128]{1,0:T(4,128)S(1)} %collective-permute-done.4.refs_3_, ...), custom_call_target="tpu_custom_call" | custom-call | flops 10000000 | bytes 30000 | tf_op jit(solution)/shard_map/pallas_call | solution.py:234
  43.8 3.4 %shard_map.89 = (f32[32,4096]{1,0:T(8,128)S(1)}, bf16[1,32,4096]{2,1,0:T(8,128)(2,1)S(1)}) custom-call(s32[1]{0:T(128)} %bitcast.2.count_ref, s32[2,144]{1,0:T(2,128)S(1)} %select_reduce_fusion.table_ref, bf16[32,16384]{1,0:T(8,128)(2,1)S(1)} %get-tuple-element.28.source_ref, bf16[32,8192]{1,0:T(8,128)(2,1)S(1)} %get-tuple-element.29.target_ref, ...), custom_call_target="tpu_custom_call" | custom-call | flops 40000000 | bytes 120000 | tf_op jit(solution)/shard_map/pallas_call | solution.py:336
  47.1 1.9 %collective-permute-start.8 = (bf16[32,4096]{1,0:T(8,128)(2,1)S(1)}, bf16[32,4096]{1,0:T(8,128)(2,1)S(1)}, u32[]{:S(2)}, u32[]{:S(2)}) collective-permute-start(bf16[32,4096]{1,0:T(8,128)(2,1)S(1)} %bitcast.8), channel_id=1, source_target_pairs={{0,8},{4,12},{8,0},{12,4},{16,24},{20,28},{24,16},{28,20},{1,9},{5... | collective-permute-start | bytes 786440 | tf_op jit(solution)/shard_map/ppermute | solution.py:247
  49.1 3.4 %shard_map.90 = (f32[32,4096]{1,0:T(8,128)S(1)}, bf16[1,32,4096]{2,1,0:T(8,128)(2,1)S(1)}) custom-call(s32[1]{0:T(128)} %bitcast.2.count_ref, s32[2,144]{1,0:T(2,128)S(1)} %select_reduce_fusion.table_ref, bf16[32,16384]{1,0:T(8,128)(2,1)S(1)} %get-tuple-element.28.source_ref, bf16[32,8192]{1,0:T(8,128)(2,1)S(1)} %get-tuple-element.29.target_ref, ...), custom_call_target="tpu_custom_call" | custom-call | flops 40000000 | bytes 120000 | tf_op jit(solution)/shard_map/pallas_call | solution.py:336
  52.5 1.7 %collective-permute-start.9 = (bf16[32,4096]{1,0:T(8,128)(2,1)S(1)}, bf16[32,4096]{1,0:T(8,128)(2,1)S(1)}, u32[]{:S(2)}, u32[]{:S(2)}) collective-permute-start(bf16[32,4096]{1,0:T(8,128)(2,1)S(1)} %bitcast.9), channel_id=1, source_target_pairs={{0,8},{4,12},{8,0},{12,4},{16,24},{20,28},{24,16},{28,20},{1,9},{5... | collective-permute-start | bytes 786440 | tf_op jit(solution)/shard_map/ppermute | solution.py:247
  54.8 4.6 %collective-permute-done.9.refs_4_ = bf16[32,4096]{1,0:T(8,128)(2,1)S(1)} collective-permute-done((bf16[32,4096]{1,0:T(8,128)(2,1)S(1)}, bf16[32,4096]{1,0:T(8,128)(2,1)S(1)}, u32[]{:S(2)}, u32[]{:S(2)}) %collective-permute-start.9) | collective-permute-done | bytes 262176 | tf_op jit(solution)/shard_map/ppermute | solution.py:247
  59.4 1.2 %shard_map.92 = (f32[64,4096]{1,0:T(8,128)}, f32[64,256]{1,0:T(8,128)S(1)}, f32[4,128]{1,0:T(4,128)S(1)}) custom-call(f32[64,4096]{1,0:T(8,128)S(1)} %shard_map.87.refs_0_, f32[32,4096]{1,0:T(8,128)S(1)} %get-tuple-element.30.refs_1_, f32[32,4096]{1,0:T(8,128)S(1)} %get-tuple-element.32.refs_2_, bf16[32,4096]{1,0:T(8,128)(2,1)S(1)} %collective-permute-done.8.refs_3_, ...), custom_call_target="tpu_custom_call" | custom-call | flops 20000000 | bytes 60000 | tf_op jit(solution)/shard_map/pallas_call | solution.py:366
  60.6 1.5 %collective-permute-start.11 = (f32[4,128]{1,0:T(4,128)S(1)}, f32[4,128]{1,0:T(4,128)S(1)}, u32[]{:S(2)}, u32[]{:S(2)}) collective-permute-start(f32[4,128]{1,0:T(4,128)S(1)} %get-tuple-element.37.refs_0_), channel_id=1, source_target_pairs={{0,2},{1,3},{2,0},{3,1},{4,6},{5,7},{6,4},{7,5},{8,10},{9,11},{10,... | collective-permute-start | bytes 6152 | tf_op jit(solution)/shard_map/ppermute | solution.py:247
  62.5 1.7 %collective-permute-done.11.refs_2_ = f32[4,128]{1,0:T(4,128)S(1)} collective-permute-done((f32[4,128]{1,0:T(4,128)S(1)}, f32[4,128]{1,0:T(4,128)S(1)}, u32[]{:S(2)}, u32[]{:S(2)}) %collective-permute-start.11) | collective-permute-done | bytes 2080 | tf_op jit(solution)/shard_map/ppermute | solution.py:247
  64.2 0.9 %collective-permute-done.12.refs_3_ = f32[4,128]{1,0:T(4,128)S(1)} collective-permute-done((f32[4,128]{1,0:T(4,128)S(1)}, f32[4,128]{1,0:T(4,128)S(1)}, u32[]{:S(2)}, u32[]{:S(2)}) %collective-permute-start.12) | collective-permute-done | bytes 2080 | tf_op jit(solution)/shard_map/ppermute | solution.py:247
  65.1 0.7 %shard_map.93 = f32[64,256]{1,0:T(8,128)} custom-call(f32[64,256]{1,0:T(8,128)S(1)} %get-tuple-element.36.merged_ref, f32[4,128]{1,0:T(4,128)S(1)} %get-tuple-element.37.refs_0_, f32[4,128]{1,0:T(4,128)S(1)} %collective-permute-done.10.refs_1_, f32[4,128]{1,0:T(4,128)S(1)} %collective-permute-done.11.refs_2_, f32[4,128]{1,0:T(4,128)S(1)} %collective-permute-done.12.refs_3_), custom_call_target="tpu_custom_call" | custom-call | flops 10000000 | bytes 30000 | tf_op jit(solution)/shard_map/pallas_call | solution.py:381
  (53 shorter events, 5.5 us)
Async XLA Ops:
  0.6 6.4 %copy-start.5 = (s32[32,24]{0,1:T(8,128)S(1)}, s32[32,24]{0,1:T(8,128)}, u32[]{:S(2)}) copy-start(s32[32,24]{0,1:T(8,128)} %param.10) | copy-start | bytes 9220
  0.6 25.5 %collective-permute-start.2 = (bf16[64,4096]{1,0:T(8,128)(2,1)}, bf16[64,4096]{1,0:T(8,128)(2,1)S(1)}, u32[]{:S(2)}, u32[]{:S(2)}) collective-permute-start(bf16[64,4096]{1,0:T(8,128)(2,1)} %refs_0_.3), channel_id=1, source_target_pairs={{0,4},{4,0},{8,12},{12,8},{16,20},{20,16},{24,28},{28,24},{1,5},{5... | collective-permute-start | bytes 1572872 | tf_op jit(solution)/shard_map/ppermute | solution.py:247
  3.7 25.7 %collective-permute-start.1 = (bf16[64,4096]{1,0:T(8,128)(2,1)}, bf16[64,4096]{1,0:T(8,128)(2,1)S(1)}, u32[]{:S(2)}, u32[]{:S(2)}) collective-permute-start(bf16[64,4096]{1,0:T(8,128)(2,1)} %refs_0_.3), channel_id=1, source_target_pairs={{0,16},{4,20},{8,24},{12,28},{16,0},{20,4},{24,8},{28,12},{1,17},{... | collective-permute-start | bytes 1572872 | tf_op jit(solution)/shard_map/ppermute | solution.py:247
  7.0 0.7 %copy-start.4 = (f32[4096]{0:T(1024)S(1)}, f32[4096]{0:T(1024)}, u32[]{:S(2)}) copy-start(f32[4096]{0:T(1024)} %param.8) | copy-start | bytes 49156
  9.1 1.0 %copy-start = (bf16[64,4096]{1,0:T(8,128)(2,1)S(1)}, bf16[64,4096]{1,0:T(8,128)(2,1)}, u32[]{:S(2)}) copy-start(bf16[64,4096]{1,0:T(8,128)(2,1)} %refs_0_.3) | copy-start | bytes 1572868
  29.4 10.1 %collective-permute-start.5 = (bf16[32,4096]{1,0:T(8,128)(2,1)S(1)}, bf16[32,4096]{1,0:T(8,128)(2,1)S(1)}, u32[]{:S(2)}, u32[]{:S(2)}) collective-permute-start(bf16[32,4096]{1,0:T(8,128)(2,1)S(1)} %slice.25), channel_id=1, source_target_pairs={{0,4},{4,0},{8,12},{12,8},{16,20},{20,16},{24,28},{28,24},{1,5},{5... | collective-permute-start | bytes 786440 | tf_op jit(solution)/shard_map/ppermute | solution.py:247
  30.0 6.3 %collective-permute-start = (f32[4,4128]{1,0:T(4,128)S(1)}, f32[4,4128]{1,0:T(4,128)S(1)}, u32[]{:S(2)}, u32[]{:S(2)}) collective-permute-start(f32[4,4128]{1,0:T(4,128)S(1)} %pad_maximum_fusion.refs_0_.refs_1_.refs_4_), channel_id=1, source_target_pairs={{0,16},{4,20},{8,24},{12,28},{16,0},{20,4},{24,8},{28,12},{1,17},{... | collective-permute-start | bytes 198152 | tf_op jit(solution)/shard_map/ppermute | solution.py:247
  30.0 8.8 %collective-permute-start.4 = (f32[4,4128]{1,0:T(4,128)S(1)}, f32[4,4128]{1,0:T(4,128)S(1)}, u32[]{:S(2)}, u32[]{:S(2)}) collective-permute-start(f32[4,4128]{1,0:T(4,128)S(1)} %pad_maximum_fusion.refs_0_.refs_1_.refs_4_), channel_id=1, source_target_pairs={{0,20},{4,16},{8,28},{12,24},{16,4},{20,0},{24,12},{28,8},{1,21},{... | collective-permute-start | bytes 198152 | tf_op jit(solution)/shard_map/ppermute | solution.py:247
  33.9 5.7 %collective-permute-start.3 = (f32[4,4128]{1,0:T(4,128)S(1)}, f32[4,4128]{1,0:T(4,128)S(1)}, u32[]{:S(2)}, u32[]{:S(2)}) collective-permute-start(f32[4,4128]{1,0:T(4,128)S(1)} %pad_maximum_fusion.refs_0_.refs_1_.refs_4_), channel_id=1, source_target_pairs={{0,4},{4,0},{8,12},{12,8},{16,20},{20,16},{24,28},{28,24},{1,5},{5... | collective-permute-start | bytes 198152 | tf_op jit(solution)/shard_map/ppermute | solution.py:247
  34.5 7.7 %collective-permute-start.6 = (f32[4,4128]{1,0:T(4,128)S(1)}, f32[4,4128]{1,0:T(4,128)S(1)}, u32[]{:S(2)}, u32[]{:S(2)}) collective-permute-start(f32[4,4128]{1,0:T(4,128)S(1)} %pad_maximum_fusion.refs_0_.refs_1_.refs_4_), channel_id=1, source_target_pairs={{0,8},{4,12},{8,0},{12,4},{16,24},{20,28},{24,16},{28,20},{1,9},{5... | collective-permute-start | bytes 198152 | tf_op jit(solution)/shard_map/ppermute | solution.py:247
  40.6 3.2 %copy-start.1 = (bf16[64,4096]{1,0:T(8,128)(2,1)S(1)}, bf16[64,4096]{1,0:T(8,128)(2,1)}, u32[]{:S(2)}) copy-start(bf16[64,4096]{1,0:T(8,128)(2,1)} %refs_0_.3) | copy-start | bytes 1572868
  41.7 7.4 %collective-permute-start.7 = (bf16[32,4096]{1,0:T(8,128)(2,1)}, bf16[32,4096]{1,0:T(8,128)(2,1)S(1)}, u32[]{:S(2)}, u32[]{:S(2)}) collective-permute-start(bf16[32,4096]{1,0:T(8,128)(2,1)} %slice.32), channel_id=1, source_target_pairs={{0,4},{4,0},{8,12},{12,8},{16,20},{20,16},{24,28},{28,24},{1,5},{5... | collective-permute-start | bytes 786440 | tf_op jit(solution)/shard_map/ppermute | solution.py:247
  47.1 7.0 %copy-start.2 = (bf16[4,256,64]{1,2,0:T(8,128)(2,1)S(1)}, bf16[4,256,64]{1,2,0:T(8,128)(2,1)}, u32[]{:S(2)}) copy-start(bf16[4,256,64]{1,2,0:T(8,128)(2,1)} %param.13) | copy-start | bytes 393220
  47.1 7.6 %collective-permute-start.8 = (bf16[32,4096]{1,0:T(8,128)(2,1)S(1)}, bf16[32,4096]{1,0:T(8,128)(2,1)S(1)}, u32[]{:S(2)}, u32[]{:S(2)}) collective-permute-start(bf16[32,4096]{1,0:T(8,128)(2,1)S(1)} %bitcast.8), channel_id=1, source_target_pairs={{0,8},{4,12},{8,0},{12,4},{16,24},{20,28},{24,16},{28,20},{1,9},{5... | collective-permute-start | bytes 786440 | tf_op jit(solution)/shard_map/ppermute | solution.py:247
  49.1 5.1 %copy-start.3 = (s32[32,32]{1,0:T(8,128)S(1)}, s32[32,32]{1,0:T(8,128)}, u32[]{:S(2)}) copy-start(s32[32,32]{1,0:T(8,128)} %skel_ref.1) | copy-start | bytes 12292
  52.5 7.0 %collective-permute-start.9 = (bf16[32,4096]{1,0:T(8,128)(2,1)S(1)}, bf16[32,4096]{1,0:T(8,128)(2,1)S(1)}, u32[]{:S(2)}, u32[]{:S(2)}) collective-permute-start(bf16[32,4096]{1,0:T(8,128)(2,1)S(1)} %bitcast.9), channel_id=1, source_target_pairs={{0,8},{4,12},{8,0},{12,4},{16,24},{20,28},{24,16},{28,20},{1,9},{5... | collective-permute-start | bytes 786440 | tf_op jit(solution)/shard_map/ppermute | solution.py:247
  60.6 1.9 %collective-permute-start.10 = (f32[4,128]{1,0:T(4,128)S(1)}, f32[4,128]{1,0:T(4,128)S(1)}, u32[]{:S(2)}, u32[]{:S(2)}) collective-permute-start(f32[4,128]{1,0:T(4,128)S(1)} %get-tuple-element.37.refs_0_), channel_id=1, source_target_pairs={{0,1},{1,0},{2,3},{3,2},{4,5},{5,4},{6,7},{7,6},{8,9},{9,8},{10,11... | collective-permute-start | bytes 6152 | tf_op jit(solution)/shard_map/ppermute | solution.py:247
  60.6 3.6 %collective-permute-start.11 = (f32[4,128]{1,0:T(4,128)S(1)}, f32[4,128]{1,0:T(4,128)S(1)}, u32[]{:S(2)}, u32[]{:S(2)}) collective-permute-start(f32[4,128]{1,0:T(4,128)S(1)} %get-tuple-element.37.refs_0_), channel_id=1, source_target_pairs={{0,2},{1,3},{2,0},{3,1},{4,6},{5,7},{6,4},{7,5},{8,10},{9,11},{10,... | collective-permute-start | bytes 6152 | tf_op jit(solution)/shard_map/ppermute | solution.py:247
  62.1 3.0 %collective-permute-start.12 = (f32[4,128]{1,0:T(4,128)S(1)}, f32[4,128]{1,0:T(4,128)S(1)}, u32[]{:S(2)}, u32[]{:S(2)}) collective-permute-start(f32[4,128]{1,0:T(4,128)S(1)} %get-tuple-element.37.refs_0_), channel_id=1, source_target_pairs={{0,3},{1,2},{2,1},{3,0},{4,7},{5,6},{6,5},{7,4},{8,11},{9,10},{10,... | collective-permute-start | bytes 6152 | tf_op jit(solution)/shard_map/ppermute | solution.py:247

commit v4 on v3

--- a/solution.py
+++ b/solution.py
@@ -44,33 +44,46 @@
     return (a, a, b, b, a, c), (p, q, p, q, r, p)
 
 
-def feature_body(n_source, n_target, *refs):
-    source_ref, target_ref, rows = refs[n_source + n_target :]
+def write_features(points_ref, rows, out, is_source):
     points = rows.shape[1]
+    centred = points_ref[0:3, :points] - 0.5
+    square = centred * centred
+    norm = square[0:1] + square[1:2] + square[2:3]
+    if is_source:
+        root = 1.0 / (points_ref[3:4, :points] * INV_FOUR_PI)
+        scale = root * root
+        side, shared, last = 1, (centred * scale, scale), scale * (norm + DELTA_SQ)
+    else:
+        side, shared, last = 0, (-2.0 * centred, norm), None
+    first = 0
+    for values in shared:
+        for part in six_products(values, values)[side]:
+            rows[first : first + values.shape[0], :] = part
+            first += values.shape[0]
+    parts = [jnp.ones_like(norm)] * 3 if last is None else split_three(last)
+    for part in parts:
+        rows[first : first + 1, :] = part
+        first += 1
+    out[...] = rows[...].astype(jnp.bfloat16)
+
+
+def feature_body(n_bundle, place_ref, *refs):
+    source_ref, target_ref, rows = refs[-3:]
+    points = rows.shape[1]
+    if len(refs) > n_bundle + 3:
+        own_source_ref, own_target_ref = refs[n_bundle:-3]
+        source_ref[:, :points] = own_source_ref[...]
+        target_ref[:, :points] = own_target_ref[:, :points]
+    target_ref[:, target_ref.shape[1] - LEAF_PTS :] = jnp.ones((FEATURES, LEAF_PTS), jnp.bfloat16)
     rows[27:FEATURES, :] = jnp.zeros((FEATURES - 27, points), jnp.float32)
-    for i in range(n_source + n_target):
-        points_ref = refs[i]
-        centred = points_ref[0:3, :points] - 0.5
-        square = centred * centred
-        norm = square[0:1] + square[1:2] + square[2:3]
-        if i < n_source:
-            root = 1.0 / (points_ref[3:4, :points] * INV_FOUR_PI)
-            scale = root * root
-            side, shared, last = 1, (centred * scale, scale), scale * (norm + DELTA_SQ)
-            out = source_ref.at[:, i * points : (i + 1) * points]
-        else:
-            side, shared, last = 0, (-2.0 * centred, norm), None
-            out = target_ref.at[:, (i - n_source) * points : (i - n_source + 1) * points]
-        first = 0
-        for values in shared:
-            for part in six_products(values, values)[side]:
-                rows[first : first + values.shape[0], :] = part
-                first += values.shape[0]
-        parts = [jnp.ones_like(norm)] * 3 if last is None else split_three(last)
-        for part in parts:
-            rows[first : first + 1, :] = part
-            first += 1
-        out[...] = rows[...].astype(jnp.bfloat16)
+    for i in range(n_bundle):
+        for kind, out_ref in enumerate((source_ref, target_ref)):
+            place = place_ref[kind, i]
+
+            @pl.when(place >= 0)
+            def _(points_ref=refs[i], place=place, out_ref=out_ref, kind=kind):
+                lanes = pl.ds(pl.multiple_of(place * points, LEAF_PTS), points)
+                write_features(points_ref, rows, out_ref.at[:, lanes], kind == 0)
 
 
 def turned_block(source, target):
@@ -119,23 +132,26 @@
     lax.fori_loop(0, leaves // 2, step, 0)
 
 
-def far_body(first, count_ref, table_ref, source_ref, target_ref, *refs):
+def far_body(first, table_ref, source_ref, target_ref, *refs):
     omegas = refs[:4]
     own_ref, rest_ref, block_ref, total_ref, omega_ref, sems = refs[4:]
     size, points = own_ref.shape
     fetches = []
-    for k in range(4):
-        rows = pl.ds(first if k < 3 else 0, size)
+    for k, slot in enumerate((0, 2, 1, 3)):
+        rows = pl.ds(first if k < 2 else 0, size)
         fetches.append(
             pltpu.make_async_copy(
                 omegas[k].at[rows, :],
-                omega_ref.at[:, k * points : (k + 1) * points],
+                omega_ref.at[:, slot * points : (slot + 1) * points],
                 sems.at[k],
             )
         )
         fetches[-1].start()
-    count = count_ref[0]
     total_ref[...] = jnp.zeros_like(total_ref)
+    spare = total_ref.shape[1] // LEAF_PTS - 1
+    rounds = sum(
+        (table_ref[1, k] < spare).astype(jnp.int32) for k in range(0, table_ref.shape[1], BATCH)
+    )
     for fetch in fetches:
         fetch.wait()
 
@@ -153,10 +169,10 @@
                 block_ref[u],
                 preferred_element_type=jnp.float32,
             )
-            total_ref[:, leaf_range(table_ref[1, item])] += jnp.where(item < count, product, 0.0)
+            total_ref[:, leaf_range(table_ref[1, item])] += product
         return carry
 
-    lax.fori_loop(0, lax.div(count + BATCH - 1, BATCH), step, 0)
+    lax.fori_loop(0, rounds, step, 0)
     own_ref[...] = total_ref[:, :points]
     for r in range(1, rest_ref.shape[0] + 1):
         rest_ref[r - 1] = total_ref[:, r * points : (r + 1) * points].astype(jnp.bfloat16)
@@ -230,16 +246,16 @@
     )
 
 
-def features_of(points, sources, targets):
+def features_of(points, senders, dests, places, bundles, own=()):
     return call(
-        functools.partial(feature_body, len(sources), len(targets)),
+        functools.partial(feature_body, len(bundles)),
         [
-            jax.ShapeDtypeStruct((FEATURES, len(sources) * points), jnp.bfloat16),
-            jax.ShapeDtypeStruct((FEATURES, len(targets) * points), jnp.bfloat16),
+            jax.ShapeDtypeStruct((FEATURES, senders * points), jnp.bfloat16),
+            jax.ShapeDtypeStruct((FEATURES, dests * points + LEAF_PTS), jnp.bfloat16),
         ],
-        [VMEM] * (len(sources) + len(targets)),
+        [SMEM] + [VMEM] * (len(bundles) + len(own)),
         [pltpu.VMEM((FEATURES, points), jnp.float32)],
-    )(*sources, *targets)
+    )(places, *bundles, *own)
 
 
 def exchange(array, axis, bit):
@@ -251,12 +267,43 @@
     return lax.optimization_barrier((array, *others))[0]
 
 
-def far_table(pairs, me, masks, outer, leaf_dev, length):
-    member = jnp.arange(4, dtype=jnp.int32)
-    owners = me ^ (member % 2 * masks[0] + member // 2 * masks[1])
-    source = pairs[:, 0] - ((owners - member) * leaf_dev)[:, None]
+def gather_bundles(sent, top, low, dests, wait):
+    masks = [top, low, top | low] + [2 * r for r in range(1, dests)]
+    n_leaf, n_probe = lax.axis_size("leaf"), lax.axis_size("probe")
+    if len(masks) != 4 or n_probe % 2:
+        rank = jnp.arange(len(masks), dtype=jnp.int32)
+        bundles = [exchange(sent, "leaf", mask) for mask in masks]
+    else:
+        core = lax.axis_index("probe") % 2
+        rank = jnp.stack([core, 2 + core, 1 - core, 3 - core])
+        bundles = []
+        for half in (0, 2):
+            pairs = [
+                (i * n_probe + q, (i ^ masks[half + q % 2]) * n_probe + q)
+                for i in range(n_leaf)
+                for q in range(n_probe)
+            ]
+            bundles.append(lax.ppermute(sent, ("leaf", "probe"), pairs))
+        bundles = list(lax.optimization_barrier((*bundles, *wait))[:2])
+        bundles += [exchange(bundle, "probe", 1) for bundle in bundles]
+    distance = jnp.where(
+        rank < 3, (rank + 1) % 2 * top + (rank + 1) // 2 % 2 * low, 2 * (rank - 2)
+    )
+    distance = jnp.where(rank == 2, top | low, distance)
+    sender = jnp.where(rank < 3, rank + 1, -1)
+    member = jnp.where(rank < 3, -1, rank - 2)
+    zero = jnp.zeros((1,), jnp.int32)
+    return (
+        [sent, *bundles],
+        jnp.concatenate([zero, distance]),
+        jnp.stack([jnp.concatenate([zero, sender]), jnp.concatenate([zero, member])]),
+    )
+
+
+def far_table(pairs, me, distance, sender, outer, leaf_dev, length, spare):
+    source = pairs[:, 0] - (((me ^ distance) - sender) * leaf_dev)[:, None]
     relation = (pairs[:, 1] // leaf_dev) ^ me
-    inside = ((relation & outer) == 0).reshape(-1)
+    inside = (((relation & outer) == 0) & (sender >= 0)[:, None]).reshape(-1)
     target = (relation // 2) * leaf_dev + pairs[:, 1] % leaf_dev
     iota = jnp.arange(inside.shape[0], dtype=jnp.int32)
     place = jnp.sum(
@@ -264,11 +311,8 @@
     )
     place = jnp.where(inside, place, -1)
     hit = place[None, None, :] == jnp.arange(length, dtype=jnp.int32)[None, :, None]
-    codes = jnp.stack([source.reshape(-1), target.reshape(-1)])
-    return (
-        jnp.sum(inside.astype(jnp.int32)).reshape(1),
-        jnp.sum(jnp.where(hit, codes[:, None, :], 0), axis=2),
-    )
+    codes = jnp.stack([source.reshape(-1), target.reshape(-1) - spare])
+    return jnp.sum(jnp.where(hit, codes[:, None, :], 0), axis=2) + jnp.array([[0], [spare]])
 
 
 def per_device(coords, weights, omega, near_local, far_pairs, skel_rows, parent_interp):
@@ -284,7 +328,9 @@
     unit = probe_dev // sum(CHUNKS)
     chunks = [(unit * sum(CHUNKS[:i]), unit * c) for i, c in enumerate(CHUNKS)]
 
-    omega_across = exchange(omega, "leaf", top)
+    parts = lax.optimization_barrier([omega[first : first + size] for first, size in chunks])
+    crossed = [exchange(part, "leaf", top) for part in parts]
+    omega_beside = exchange(after(omega, *parts), "leaf", low)
     pair_columns = 2 * pair_dev // 4
     sent = jnp.concatenate(
         [
@@ -293,10 +339,7 @@
         ],
         axis=1,
     )
-    across = exchange(sent, "leaf", top)
-    both = exchange(sent, "leaf", top | low)
-
-    source, target = features_of(points, [sent], [sent])
+    source, target = features_of(points, 1, 1, jnp.zeros((2, 1), jnp.int32), [sent])
     part_points = points // LOCAL_PARTS
     entries = near_local.shape[1]
 
@@ -310,45 +353,40 @@
             micros=16.0 / LOCAL_PARTS,
         )((me * leaf_dev).reshape(1), table, target, source, omega)
 
-    omega_beside = exchange(omega, "leaf", low)
     local = [local_part(i, near_local) for i in range(LOCAL_PARTS)]
-    omega_across = after(omega_across, omega_beside, *local)
-    late = after(sent, omega_across)
-    beside = exchange(late, "leaf", low)
-    partners = [exchange(late, "leaf", 2 * r) for r in range(1, dests)]
+    bundles, distance, places = gather_bundles(sent, top, low, dests, [crossed[0], *local])
     relayed = []
-    for first, size in chunks:
-        part = omega_across[first : first + size]
-        if relayed:
-            part = after(omega_across, relayed[-1])[first : first + size]
-        relayed.append(exchange(part, "leaf", low))
-
-    bundles = [sent, across, beside, both]
+    for i, part in enumerate(crossed):
+        crossed[i] = after(part, relayed[-1]) if relayed else after(part, omega_beside, *local)
+        relayed.append(exchange(crossed[i], "leaf", low))
+
     bundles = list(lax.optimization_barrier((*bundles, relayed[0]))[:-1])
     pairs = jnp.stack([b[:, points:].astype(jnp.int32).reshape(2, pair_dev) for b in bundles])
     slots = (dests * 4 * CAP + BATCH - 1) // BATCH * BATCH
-    far_count, codes = far_table(
-        pairs, me, (top, low), top | low, leaf_dev, slots
-    )
-    far_source, far_target = features_of(points, bundles, [bundles[0], *partners])
+    codes = far_table(
+        pairs, me, distance, places[0], top | low, leaf_dev, slots, dests * leaf_dev
+    )
+    far_source, far_target = features_of(
+        points, 4, dests, places, bundles
+    )
     owns, arrived = [], []
-    for (first, size), omega_both in zip(chunks, relayed):
+    for (first, size), from_across, from_both in zip(chunks, crossed, relayed):
         own, rest = call(
             functools.partial(far_body, first),
             [
                 jax.ShapeDtypeStruct((size, points), jnp.float32),
                 jax.ShapeDtypeStruct((dests - 1, size, points), jnp.bfloat16),
             ],
-            [SMEM, SMEM, VMEM, VMEM] + [HBM] * 4,
+            [SMEM, VMEM, VMEM] + [HBM] * 4,
             [
                 pltpu.VMEM((BATCH, LEAF_PTS, LEAF_PTS), jnp.bfloat16),
-                pltpu.VMEM((size, dests * points), jnp.float32),
+                pltpu.VMEM((size, dests * points + LEAF_PTS), jnp.float32),
                 pltpu.VMEM((size, 4 * points), jnp.bfloat16),
                 pltpu.SemaphoreType.DMA((4,)),
             ],
             micros=4.0,
         )(
-            far_count, codes, far_source, far_target, omega, omega_across, omega_beside, omega_both
+            codes, far_source, far_target, omega, omega_beside, from_across, from_both
         )
         half = dests // 2
         while half > 1:

time: 67 us -> 62.9 us (0.939); the launches traced: 65.8 us -> 62.5 us
  waiting for transfers between devices: 14.3 us -> 12.3 us
  starting transfers between devices: 17.7 us -> 16.5 us
    ppermute x13 -> x12, starting transfers between devices: 17.7 us -> 11.1 us  [exchange(): return lax.ppermute(array, axis, [(i, i ^ bit) for i in range(size)])]
    ppermute x0 -> x2, starting transfers between devices: none -> 5.39 us  [gather_bundles(): bundles.append(lax.ppermute(sent, ('leaf', 'probe'), pairs))]
    ppermute x13 -> x12, waiting for transfers between devices: 14.3 us -> 12.3 us  [exchange(): return lax.ppermute(array, axis, [(i, i ^ bit) for i in range(size)])]
    pallas_call x2, Pallas kernels: 6.74 us -> 5.37 us  [per_device(): call(functools.partial(far_body, first), [jax.ShapeDtypeStruct((size, poi...]
    pallas_call x2, Pallas kernels: 1.73 us -> 2.93 us  [features_of(): call(functools.partial(feature_body, len(bundles)), [jax.ShapeDtypeStruct...]
    unnamed x16 -> x13, local copies, waits for them, and re-layouts: 1.79 us -> 0.72 us
    slice x2, local copies, waits for them, and re-layouts: 0.74 us -> 1.79 us  [the longest x1 1.76 us: per_device(): omega[first:first + size]]
  transfers between devices with their start and end apart: 13 -> 14, of which waited for: 7 -> 7; matrix products, arithmetic and copies ran while one was open for 6% -> 6% of each run, Pallas kernels for 38% -> 40%
where the time goes in v4:
time: 62.9 us; the launch traced here: 62.5 us
  Pallas kernels  27 us (43%)
  starting transfers between devices  16.5 us (26%)
  waiting for transfers between devices  12.3 us (20%)
  local copies, waits for them, and re-layouts  3.55 us (6%)
  other arithmetic  2.38 us (4%)
  between operations  0.78 us (1%)
    pallas_call x1, Pallas kernels, local_part(): call(functools.partial(local_body, i * part_points // LEAF_PTS), jax.Shap...  16.1 us
    ppermute x12, waiting for transfers between devices, exchange(): return lax.ppermute(array, axis, [(i, i ^ bit) for i in range(size)])  12.3 us
    ppermute x12, starting transfers between devices, exchange(): return lax.ppermute(array, axis, [(i, i ^ bit) for i in range(size)])  11.1 us
    ppermute x2, starting transfers between devices, gather_bundles(): bundles.append(lax.ppermute(sent, ('leaf', 'probe'), pairs))  5.39 us
    pallas_call x2, Pallas kernels, per_device(): call(functools.partial(far_body, first), [jax.ShapeDtypeStruct((size, poi...  5.37 us
    pallas_call x2, Pallas kernels, features_of(): call(functools.partial(feature_body, len(bundles)), [jax.ShapeDtypeStruct...  2.93 us
    slice x1, local copies, waits for them, and re-layouts, per_device(): omega[first:first + size]  1.76 us
  transfers between devices with their start and end apart: 14, of which 7 were waited for; matrix products, arithmetic and copies ran while one was open for 6% of the time, Pallas kernels for 40%

profile of v4, /device:TPU:0, one launch (start us, length us, event | category | flops | bytes accessed | tf_op | source)
XLA Modules:
  0.0 62.5 jit_solution(7187719097192484544)
XLA Ops:
  0.6 0.7 %convert_element_type.24 = f32[2,64]{1,0:T(2,128)S(1)} convert(s32[2,64]{1,0:T(2,128)} %param.12) | non-fusion elementwise | flops 128 | bytes 1024 | tf_op jit(solution)/shard_map/convert_element_type | solution.py:338
  1.4 0.9 %pad_maximum_fusion.refs_0_ = f32[4,4128]{1,0:T(4,128)S(1)} fusion(f32[4,32]{1,0:T(4,128)S(1)} %convert_element_type.25, f32[1,4096]{1,0:T(1,128)} %bitcast.16, f32[3,4096]{1,0:T(4,128)} %param.8), kind=kLoop, calls=%fused_computation.5 | loop fusion | flops 33024 | bytes 132096 | tf_op jit(solution)/shard_map/concatenate | solution.py:335
  2.3 4.1 %collective-permute-start = (f32[4,4128]{1,0:T(4,128)S(1)}, f32[4,4128]{1,0:T(4,128)S(1)}, u32[]{:S(2)}, u32[]{:S(2)}) collective-permute-start(f32[4,4128]{1,0:T(4,128)S(1)} %pad_maximum_fusion.refs_0_), channel_id=1, source_target_pairs={{0,16},{1,5},{2,18},{3,7},{4,20},{5,1},{6,22},{7,3},{8,24},{9,13},... | collective-permute-start | bytes 198152 | tf_op jit(solution)/shard_map/ppermute | solution.py:286
  6.4 1.3 %collective-permute-start.1 = (f32[4,4128]{1,0:T(4,128)S(1)}, f32[4,4128]{1,0:T(4,128)S(1)}, u32[]{:S(2)}, u32[]{:S(2)}) collective-permute-start(f32[4,4128]{1,0:T(4,128)S(1)} %pad_maximum_fusion.refs_0_), channel_id=1, source_target_pairs={{0,20},{1,9},{2,22},{3,11},{4,16},{5,13},{6,18},{7,15},{8,28},{9,1... | collective-permute-start | bytes 198152 | tf_op jit(solution)/shard_map/ppermute | solution.py:286
  7.7 1.8 %fusion.18 = (bf16[32,4096]{1,0:T(8,128)(2,1)S(1)}, bf16[32,4096]{1,0:T(8,128)(2,1)}) fusion(bf16[64,4096]{1,0:T(8,128)(2,1)} %refs_0_.3), kind=kLoop, calls=%fused_computation.71 | loop fusion | bytes 1048576 | tf_op jit(solution)/shard_map/slice | solution.py:331
  9.5 2.6 %collective-permute-start.2 = (bf16[32,4096]{1,0:T(8,128)(2,1)}, bf16[32,4096]{1,0:T(8,128)(2,1)S(1)}, u32[]{:S(2)}, u32[]{:S(2)}) collective-permute-start(bf16[32,4096]{1,0:T(8,128)(2,1)} %get-tuple-element.27), channel_id=1, source_target_pairs={{0,16},{4,20},{8,24},{12,28},{16,0},{20,4},{24,8},{28,12},{1,17},{... | collective-permute-start | bytes 786440 | tf_op jit(solution)/shard_map/ppermute | solution.py:263
  13.4 1.0 %shard_map.95 = (bf16[32,4096]{1,0:T(8,128)(2,1)S(1)}, bf16[32,4224]{1,0:T(8,128)(2,1)S(1)}) custom-call(s32[2,1]{1,0:T(2,128)S(1)} %broadcast_21_place_ref.2.place_ref, f32[4,4128]{1,0:T(4,128)S(1)} %pad_maximum_fusion.refs_0_), custom_call_target="tpu_custom_call" | custom-call | flops 10000000 | bytes 30000 | tf_op jit(solution)/shard_map/pallas_call | solution.py:250
  14.4 16.1 %shard_map.96.refs_0_ = f32[64,4096]{1,0:T(8,128)S(1)} custom-call(s32[1]{0:T(128)} %bitcast.offset_ref, s32[32,24]{1,0:T(8,128)S(1)} %copy.11.near_ref, bf16[32,4224]{1,0:T(8,128)(2,1)S(1)} %get-tuple-element.25.target_ref, bf16[32,4096]{1,0:T(8,128)(2,1)S(1)} %get-tuple-element.26.source_ref, bf16[64,4096]{1,0:T(8,128)(2,1)S(1)} %copy-done), custom_call_target="tpu_custom_call" | custom-call | flops 160000000 | bytes 480000 | tf_op jit(solution)/shard_map/pallas_call | solution.py:347
  30.7 1.8 %collective-permute-start.6 = (bf16[32,4096]{1,0:T(8,128)(2,1)S(1)}, bf16[32,4096]{1,0:T(8,128)(2,1)S(1)}, u32[]{:S(2)}, u32[]{:S(2)}) collective-permute-start(bf16[32,4096]{1,0:T(8,128)(2,1)S(1)} %collective-permute-done.2.refs_2_), channel_id=1, source_target_pairs={{0,4},{4,0},{8,12},{12,8},{16,20},{20,16},{24,28},{28,24},{1,5},{5... | collective-permute-start | bytes 786440 | tf_op jit(solution)/shard_map/ppermute | solution.py:263
  33.5 0.7 %collective-permute-done.3.refs_3_ = f32[4,4128]{1,0:T(4,128)S(1)} collective-permute-done((f32[4,4128]{1,0:T(4,128)S(1)}, f32[4,4128]{1,0:T(4,128)S(1)}, u32[]{:S(2)}, u32[]{:S(2)}) %collective-permute-start.3) | collective-permute-done | bytes 66080 | tf_op jit(solution)/shard_map/ppermute | solution.py:263
  34.4 3.0 %collective-permute-done.6.refs_3_ = bf16[32,4096]{1,0:T(8,128)(2,1)S(1)} collective-permute-done((bf16[32,4096]{1,0:T(8,128)(2,1)S(1)}, bf16[32,4096]{1,0:T(8,128)(2,1)S(1)}, u32[]{:S(2)}, u32[]{:S(2)}) %collective-permute-start.6) | collective-permute-done | bytes 262176 | tf_op jit(solution)/shard_map/ppermute | solution.py:263
  38.4 1.5 %collective-permute-start.8 = (bf16[32,4096]{1,0:T(8,128)(2,1)S(1)}, bf16[32,4096]{1,0:T(8,128)(2,1)S(1)}, u32[]{:S(2)}, u32[]{:S(2)}) collective-permute-start(bf16[32,4096]{1,0:T(8,128)(2,1)S(1)} %collective-permute-done.7.refs_2_), channel_id=1, source_target_pairs={{0,4},{4,0},{8,12},{12,8},{16,20},{20,16},{24,28},{28,24},{1,5},{5... | collective-permute-start | bytes 786440 | tf_op jit(solution)/shard_map/ppermute | solution.py:263
  40.1 1.9 %shard_map.97 = (bf16[32,16384]{1,0:T(8,128)(2,1)S(1)}, bf16[32,8320]{1,0:T(8,128)(2,1)S(1)}) custom-call(s32[2,5]{1,0:T(2,128)S(1)} %pad_add_fusion.1.place_ref, f32[4,4128]{1,0:T(4,128)S(1)} %pad_maximum_fusion.refs_0_, f32[4,4128]{1,0:T(4,128)S(1)} %collective-permute-done.refs_1_, f32[4,4128]{1,0:T(4,128)S(1)} %collective-permute-done.1.refs_2_, ...), custom_call_target="tpu_custom_call" | custom-call | flops 10000000 | bytes 30000 | tf_op jit(solution)/shard_map/pallas_call | solution.py:250
  42.1 2.7 %shard_map.98 = (f32[32,4096]{1,0:T(8,128)S(1)}, bf16[1,32,4096]{2,1,0:T(8,128)(2,1)S(1)}) custom-call(s32[2,144]{1,0:T(2,128)S(1)} %broadcast_add_fusion.table_ref, bf16[32,16384]{1,0:T(8,128)(2,1)S(1)} %get-tuple-element.38.source_ref, bf16[32,8320]{1,0:T(8,128)(2,1)S(1)} %get-tuple-element.39.target_ref, bf16[64,4096]{1,0:T(8,128)(2,1)S(1)} %copy-done, ...), custom_call_target="tpu_custom_call" | custom-call | flops 40000000 | bytes 120000 | tf_op jit(solution)/shard_map/pallas_call | solution.py:374
  44.8 1.7 %collective-permute-start.9 = (bf16[32,4096]{1,0:T(8,128)(2,1)S(1)}, bf16[32,4096]{1,0:T(8,128)(2,1)S(1)}, u32[]{:S(2)}, u32[]{:S(2)}) collective-permute-start(bf16[32,4096]{1,0:T(8,128)(2,1)S(1)} %bitcast.14), channel_id=1, source_target_pairs={{0,8},{4,12},{8,0},{12,4},{16,24},{20,28},{24,16},{28,20},{1,9},{5... | collective-permute-start | bytes 786440 | tf_op jit(solution)/shard_map/ppermute | solution.py:263
  46.5 2.7 %shard_map.99 = (f32[32,4096]{1,0:T(8,128)S(1)}, bf16[1,32,4096]{2,1,0:T(8,128)(2,1)S(1)}) custom-call(s32[2,144]{1,0:T(2,128)S(1)} %broadcast_add_fusion.table_ref, bf16[32,16384]{1,0:T(8,128)(2,1)S(1)} %get-tuple-element.38.source_ref, bf16[32,8320]{1,0:T(8,128)(2,1)S(1)} %get-tuple-element.39.target_ref, bf16[64,4096]{1,0:T(8,128)(2,1)S(1)} %copy-done, ...), custom_call_target="tpu_custom_call" | custom-call | flops 40000000 | bytes 120000 | tf_op jit(solution)/shard_map/pallas_call | solution.py:374
  49.7 0.6 shard_map.100.refs_5_
  50.3 3.0 %collective-permute-done.9.refs_3_ = bf16[32,4096]{1,0:T(8,128)(2,1)S(1)} collective-permute-done((bf16[32,4096]{1,0:T(8,128)(2,1)S(1)}, bf16[32,4096]{1,0:T(8,128)(2,1)S(1)}, u32[]{:S(2)}, u32[]{:S(2)}) %collective-permute-start.9) | collective-permute-done | bytes 262176 | tf_op jit(solution)/shard_map/ppermute | solution.py:263
  53.3 2.8 %collective-permute-done.10.refs_4_ = bf16[32,4096]{1,0:T(8,128)(2,1)S(1)} collective-permute-done((bf16[32,4096]{1,0:T(8,128)(2,1)S(1)}, bf16[32,4096]{1,0:T(8,128)(2,1)S(1)}, u32[]{:S(2)}, u32[]{:S(2)}) %collective-permute-start.10) | collective-permute-done | bytes 262176 | tf_op jit(solution)/shard_map/ppermute | solution.py:263
  56.1 1.2 %shard_map.101 = (f32[64,4096]{1,0:T(8,128)}, f32[64,256]{1,0:T(8,128)S(1)}, f32[4,128]{1,0:T(4,128)S(1)}) custom-call(f32[64,4096]{1,0:T(8,128)S(1)} %shard_map.96.refs_0_, f32[32,4096]{1,0:T(8,128)S(1)} %get-tuple-element.40.refs_1_, f32[32,4096]{1,0:T(8,128)S(1)} %get-tuple-element.42.refs_2_, bf16[32,4096]{1,0:T(8,128)(2,1)S(1)} %collective-permute-done.9.refs_3_, ...), custom_call_target="tpu_custom_call" | custom-call | flops 20000000 | bytes 60000 | tf_op jit(solution)/shard_map/pallas_call | solution.py:404
  57.3 1.5 %collective-permute-start.12 = (f32[4,128]{1,0:T(4,128)S(1)}, f32[4,128]{1,0:T(4,128)S(1)}, u32[]{:S(2)}, u32[]{:S(2)}) collective-permute-start(f32[4,128]{1,0:T(4,128)S(1)} %get-tuple-element.47.refs_0_), channel_id=1, source_target_pairs={{0,2},{1,3},{2,0},{3,1},{4,6},{5,7},{6,4},{7,5},{8,10},{9,11},{10,... | collective-permute-start | bytes 6152 | tf_op jit(solution)/shard_map/ppermute | solution.py:263
  59.1 1.7 %collective-permute-done.12.refs_2_ = f32[4,128]{1,0:T(4,128)S(1)} collective-permute-done((f32[4,128]{1,0:T(4,128)S(1)}, f32[4,128]{1,0:T(4,128)S(1)}, u32[]{:S(2)}, u32[]{:S(2)}) %collective-permute-start.12) | collective-permute-done | bytes 2080 | tf_op jit(solution)/shard_map/ppermute | solution.py:263
  60.9 0.9 %collective-permute-done.13.refs_3_ = f32[4,128]{1,0:T(4,128)S(1)} collective-permute-done((f32[4,128]{1,0:T(4,128)S(1)}, f32[4,128]{1,0:T(4,128)S(1)}, u32[]{:S(2)}, u32[]{:S(2)}) %collective-permute-start.13) | collective-permute-done | bytes 2080 | tf_op jit(solution)/shard_map/ppermute | solution.py:263
  61.8 0.7 %shard_map.102 = f32[64,256]{1,0:T(8,128)} custom-call(f32[64,256]{1,0:T(8,128)S(1)} %get-tuple-element.46.merged_ref, f32[4,128]{1,0:T(4,128)S(1)} %get-tuple-element.47.refs_0_, f32[4,128]{1,0:T(4,128)S(1)} %collective-permute-done.11.refs_1_, f32[4,128]{1,0:T(4,128)S(1)} %collective-permute-done.12.refs_2_, f32[4,128]{1,0:T(4,128)S(1)} %collective-permute-done.13.refs_3_), custom_call_target="tpu_custom_call" | custom-call | flops 10000000 | bytes 30000 | tf_op jit(solution)/shard_map/pallas_call | solution.py:419
  (63 shorter events, 4.7 us)
Async XLA Ops:
  2.3 10.1 %copy-start = (bf16[64,4096]{1,0:T(8,128)(2,1)S(1)}, bf16[64,4096]{1,0:T(8,128)(2,1)}, u32[]{:S(2)}) copy-start(bf16[64,4096]{1,0:T(8,128)(2,1)} %refs_0_.3) | copy-start | bytes 1572868
  2.3 30.6 %collective-permute-start = (f32[4,4128]{1,0:T(4,128)S(1)}, f32[4,4128]{1,0:T(4,128)S(1)}, u32[]{:S(2)}, u32[]{:S(2)}) collective-permute-start(f32[4,4128]{1,0:T(4,128)S(1)} %pad_maximum_fusion.refs_0_), channel_id=1, source_target_pairs={{0,16},{1,5},{2,18},{3,7},{4,20},{5,1},{6,22},{7,3},{8,24},{9,13},... | collective-permute-start | bytes 198152 | tf_op jit(solution)/shard_map/ppermute | solution.py:286
  6.4 26.5 %collective-permute-start.1 = (f32[4,4128]{1,0:T(4,128)S(1)}, f32[4,4128]{1,0:T(4,128)S(1)}, u32[]{:S(2)}, u32[]{:S(2)}) collective-permute-start(f32[4,4128]{1,0:T(4,128)S(1)} %pad_maximum_fusion.refs_0_), channel_id=1, source_target_pairs={{0,20},{1,9},{2,22},{3,11},{4,16},{5,13},{6,18},{7,15},{8,28},{9,1... | collective-permute-start | bytes 198152 | tf_op jit(solution)/shard_map/ppermute | solution.py:286
  9.5 21.3 %collective-permute-start.2 = (bf16[32,4096]{1,0:T(8,128)(2,1)}, bf16[32,4096]{1,0:T(8,128)(2,1)S(1)}, u32[]{:S(2)}, u32[]{:S(2)}) collective-permute-start(bf16[32,4096]{1,0:T(8,128)(2,1)} %get-tuple-element.27), channel_id=1, source_target_pairs={{0,16},{4,20},{8,24},{12,28},{16,0},{20,4},{24,8},{28,12},{1,17},{... | collective-permute-start | bytes 786440 | tf_op jit(solution)/shard_map/ppermute | solution.py:263
  12.0 26.3 %collective-permute-start.7 = (bf16[32,4096]{1,0:T(8,128)(2,1)S(1)}, bf16[32,4096]{1,0:T(8,128)(2,1)S(1)}, u32[]{:S(2)}, u32[]{:S(2)}) collective-permute-start(bf16[32,4096]{1,0:T(8,128)(2,1)S(1)} %get-tuple-element.30), channel_id=1, source_target_pairs={{0,16},{4,20},{8,24},{12,28},{16,0},{20,4},{24,8},{28,12},{1,17},{... | collective-permute-start | bytes 786440 | tf_op jit(solution)/shard_map/ppermute | solution.py:263
  12.4 18.3 %collective-permute-start.5 = (bf16[64,4096]{1,0:T(8,128)(2,1)S(1)}, bf16[64,4096]{1,0:T(8,128)(2,1)S(1)}, u32[]{:S(2)}, u32[]{:S(2)}) collective-permute-start(bf16[64,4096]{1,0:T(8,128)(2,1)S(1)} %copy-done), channel_id=1, source_target_pairs={{0,4},{4,0},{8,12},{12,8},{16,20},{20,16},{24,28},{28,24},{1,5},{5... | collective-permute-start | bytes 1572872 | tf_op jit(solution)/shard_map/ppermute | solution.py:263
  12.6 0.7 %copy-start.3 = (s32[32,24]{0,1:T(8,128)S(1)}, s32[32,24]{0,1:T(8,128)}, u32[]{:S(2)}) copy-start(s32[32,24]{0,1:T(8,128)} %param.11) | copy-start | bytes 9220
  30.7 6.7 %collective-permute-start.6 = (bf16[32,4096]{1,0:T(8,128)(2,1)S(1)}, bf16[32,4096]{1,0:T(8,128)(2,1)S(1)}, u32[]{:S(2)}, u32[]{:S(2)}) collective-permute-start(bf16[32,4096]{1,0:T(8,128)(2,1)S(1)} %collective-permute-done.2.refs_2_), channel_id=1, source_target_pairs={{0,4},{4,0},{8,12},{12,8},{16,20},{20,16},{24,28},{28,24},{1,5},{5... | collective-permute-start | bytes 786440 | tf_op jit(solution)/shard_map/ppermute | solution.py:263
  32.9 1.3 %collective-permute-start.3 = (f32[4,4128]{1,0:T(4,128)S(1)}, f32[4,4128]{1,0:T(4,128)S(1)}, u32[]{:S(2)}, u32[]{:S(2)}) collective-permute-start(f32[4,4128]{1,0:T(4,128)S(1)} %collective-permute-done.refs_1_), channel_id=1, source_target_pairs={{0,1},{1,0},{2,3},{3,2},{4,5},{5,4},{6,7},{7,6},{8,9},{9,8},{10,11... | collective-permute-start | bytes 198152 | tf_op jit(solution)/shard_map/ppermute | solution.py:263
  33.0 1.4 %collective-permute-start.4 = (f32[4,4128]{1,0:T(4,128)S(1)}, f32[4,4128]{1,0:T(4,128)S(1)}, u32[]{:S(2)}, u32[]{:S(2)}) collective-permute-start(f32[4,4128]{1,0:T(4,128)S(1)} %collective-permute-done.1.refs_2_), channel_id=1, source_target_pairs={{0,1},{1,0},{2,3},{3,2},{4,5},{5,4},{6,7},{7,6},{8,9},{9,8},{10,11... | collective-permute-start | bytes 198152 | tf_op jit(solution)/shard_map/ppermute | solution.py:263
  38.4 8.1 %collective-permute-start.8 = (bf16[32,4096]{1,0:T(8,128)(2,1)S(1)}, bf16[32,4096]{1,0:T(8,128)(2,1)S(1)}, u32[]{:S(2)}, u32[]{:S(2)}) collective-permute-start(bf16[32,4096]{1,0:T(8,128)(2,1)S(1)} %collective-permute-done.7.refs_2_), channel_id=1, source_target_pairs={{0,4},{4,0},{8,12},{12,8},{16,20},{20,16},{24,28},{28,24},{1,5},{5... | collective-permute-start | bytes 786440 | tf_op jit(solution)/shard_map/ppermute | solution.py:263
  44.8 4.9 %copy-start.1 = (bf16[4,256,64]{1,2,0:T(8,128)(2,1)S(1)}, bf16[4,256,64]{1,2,0:T(8,128)(2,1)}, u32[]{:S(2)}) copy-start(bf16[4,256,64]{1,2,0:T(8,128)(2,1)} %param.14) | copy-start | bytes 393220
  44.8 8.5 %collective-permute-start.9 = (bf16[32,4096]{1,0:T(8,128)(2,1)S(1)}, bf16[32,4096]{1,0:T(8,128)(2,1)S(1)}, u32[]{:S(2)}, u32[]{:S(2)}) collective-permute-start(bf16[32,4096]{1,0:T(8,128)(2,1)S(1)} %bitcast.14), channel_id=1, source_target_pairs={{0,8},{4,12},{8,0},{12,4},{16,24},{20,28},{24,16},{28,20},{1,9},{5... | collective-permute-start | bytes 786440 | tf_op jit(solution)/shard_map/ppermute | solution.py:263
  46.5 3.2 %copy-start.2 = (s32[32,32]{1,0:T(8,128)S(1)}, s32[32,32]{1,0:T(8,128)}, u32[]{:S(2)}) copy-start(s32[32,32]{1,0:T(8,128)} %skel_ref.1) | copy-start | bytes 12292
  49.2 6.9 %collective-permute-start.10 = (bf16[32,4096]{1,0:T(8,128)(2,1)S(1)}, bf16[32,4096]{1,0:T(8,128)(2,1)S(1)}, u32[]{:S(2)}, u32[]{:S(2)}) collective-permute-start(bf16[32,4096]{1,0:T(8,128)(2,1)S(1)} %bitcast.15), channel_id=1, source_target_pairs={{0,8},{4,12},{8,0},{12,4},{16,24},{20,28},{24,16},{28,20},{1,9},{5... | collective-permute-start | bytes 786440 | tf_op jit(solution)/shard_map/ppermute | solution.py:263
  57.3 1.9 %collective-permute-start.11 = (f32[4,128]{1,0:T(4,128)S(1)}, f32[4,128]{1,0:T(4,128)S(1)}, u32[]{:S(2)}, u32[]{:S(2)}) collective-permute-start(f32[4,128]{1,0:T(4,128)S(1)} %get-tuple-element.47.refs_0_), channel_id=1, source_target_pairs={{0,1},{1,0},{2,3},{3,2},{4,5},{5,4},{6,7},{7,6},{8,9},{9,8},{10,11... | collective-permute-start | bytes 6152 | tf_op jit(solution)/shard_map/ppermute | solution.py:263
  57.3 3.6 %collective-permute-start.12 = (f32[4,128]{1,0:T(4,128)S(1)}, f32[4,128]{1,0:T(4,128)S(1)}, u32[]{:S(2)}, u32[]{:S(2)}) collective-permute-start(f32[4,128]{1,0:T(4,128)S(1)} %get-tuple-element.47.refs_0_), channel_id=1, source_target_pairs={{0,2},{1,3},{2,0},{3,1},{4,6},{5,7},{6,4},{7,5},{8,10},{9,11},{10,... | collective-permute-start | bytes 6152 | tf_op jit(solution)/shard_map/ppermute | solution.py:263
  58.8 3.0 %collective-permute-start.13 = (f32[4,128]{1,0:T(4,128)S(1)}, f32[4,128]{1,0:T(4,128)S(1)}, u32[]{:S(2)}, u32[]{:S(2)}) collective-permute-start(f32[4,128]{1,0:T(4,128)S(1)} %get-tuple-element.47.refs_0_), channel_id=1, source_target_pairs={{0,3},{1,2},{2,1},{3,0},{4,7},{5,6},{6,5},{7,4},{8,11},{9,10},{10,... | collective-permute-start | bytes 6152 | tf_op jit(solution)/shard_map/ppermute | solution.py:263

commit v5 on v4

--- a/solution.py
+++ b/solution.py
@@ -20,7 +20,7 @@
 BATCH = 24
 FEATURES = 32
 CHUNKS = (1, 1)
-LOCAL_PARTS = 1
+SHARE = 2
 
 SMEM = pl.BlockSpec(memory_space=pltpu.SMEM)
 VMEM = pl.BlockSpec(memory_space=pltpu.VMEM)
@@ -94,14 +94,21 @@
 
 
 def local_body(
-    first, offset_ref, near_ref, target_ref, source_ref, probes_ref, out_ref,
-    even_ref, odd_ref, omega_ref, sem,
+    place_ref, near_ref, target_ref, source_ref, own_probes_ref, other_probes_ref,
+    own_ref, other_ref, even_ref, odd_ref, omega_ref, sems,
 ):
-    fetch = pltpu.make_async_copy(probes_ref, omega_ref, sem)
-    fetch.start()
+    probe_dev = own_ref.shape[0]
+    fetches = [
+        pltpu.make_async_copy(
+            ref, omega_ref.at[i * probe_dev : (i + 1) * probe_dev, :], sems.at[i]
+        )
+        for i, ref in enumerate((own_probes_ref, other_probes_ref))
+    ]
+    for fetch in fetches:
+        fetch.start()
     entries = near_ref.shape[1]
-    leaves = out_ref.shape[1] // LEAF_PTS
-    offset = offset_ref[0]
+    leaves = own_ref.shape[1] // LEAF_PTS
+    offset, first = place_ref[0], place_ref[1]
 
     def source_of(t, e):
         return leaf_range(near_ref[first + t, e] - offset)
@@ -115,12 +122,13 @@
 
     def use(t, block_ref):
         probes = jnp.concatenate([omega_ref[:, source_of(t, e)] for e in range(entries)], axis=1)
-        out_ref[:, leaf_range(t)] = jnp.dot(
-            probes, block_ref[...], preferred_element_type=jnp.float32
-        )
+        total = jnp.dot(probes, block_ref[...], preferred_element_type=jnp.float32)
+        own_ref[:, leaf_range(t)] = total[:probe_dev]
+        other_ref[:, leaf_range(t)] = total[probe_dev:]
 
     make(0, even_ref)
-    fetch.wait()
+    for fetch in fetches:
+        fetch.wait()
 
     def step(k, carry):
         make(2 * k + 1, odd_ref)
@@ -191,22 +199,19 @@
         ).astype(jnp.bfloat16)
 
 
-def merge_body(n_local, n_chunk, *refs):
-    locals_ = refs[:n_local]
-    owns = refs[n_local : n_local + n_chunk]
-    arrived = refs[n_local + n_chunk : n_local + 2 * n_chunk]
-    pick_ref, near_ref, merged_ref, energy_ref = refs[n_local + 2 * n_chunk :]
-    width = locals_[0].shape[1]
-    for i in range(n_local):
-        columns = slice(i * width, (i + 1) * width)
+def merge_body(n_chunk, side_ref, mine_ref, theirs_ref, *refs):
+    owns, arrived = refs[:n_chunk], refs[n_chunk : 2 * n_chunk]
+    pick_ref, near_ref, merged_ref, energy_ref = refs[2 * n_chunk :]
+    width = mine_ref.shape[1]
+    for half in range(SHARE):
+        columns = slice(half * width, (half + 1) * width)
         first = 0
         for own_ref, arrived_ref in zip(owns, arrived):
             rows = slice(first, first + own_ref.shape[0])
             first += own_ref.shape[0]
+            local = jnp.where(side_ref[0] == half, mine_ref[rows, :], theirs_ref[rows, :])
             near_ref[rows, columns] = (
-                locals_[i][rows, :]
-                + own_ref[:, columns]
-                + arrived_ref[:, columns].astype(jnp.float32)
+                local + own_ref[:, columns] + arrived_ref[:, columns].astype(jnp.float32)
             )
     parents, _, width = pick_ref.shape
     for p in range(parents):
@@ -328,8 +333,10 @@
     unit = probe_dev // sum(CHUNKS)
     chunks = [(unit * sum(CHUNKS[:i]), unit * c) for i, c in enumerate(CHUNKS)]
 
+    omega_other = exchange(omega, "probe", 1)
     parts = lax.optimization_barrier([omega[first : first + size] for first, size in chunks])
     crossed = [exchange(part, "leaf", top) for part in parts]
+    coords = after(coords, *parts)
     omega_beside = exchange(after(omega, *parts), "leaf", low)
     pair_columns = 2 * pair_dev // 4
     sent = jnp.concatenate(
@@ -340,27 +347,26 @@
         axis=1,
     )
     source, target = features_of(points, 1, 1, jnp.zeros((2, 1), jnp.int32), [sent])
-    part_points = points // LOCAL_PARTS
-    entries = near_local.shape[1]
-
-    def local_part(i, table):
-        return call(
-            functools.partial(local_body, i * part_points // LEAF_PTS),
-            jax.ShapeDtypeStruct((probe_dev, part_points), jnp.float32),
-            [SMEM, SMEM, VMEM, VMEM, HBM],
-            [pltpu.VMEM((entries * LEAF_PTS, LEAF_PTS), jnp.bfloat16)] * 2
-            + [pltpu.VMEM((probe_dev, points), jnp.bfloat16), pltpu.SemaphoreType.DMA],
-            micros=16.0 / LOCAL_PARTS,
-        )((me * leaf_dev).reshape(1), table, target, source, omega)
-
-    local = [local_part(i, near_local) for i in range(LOCAL_PARTS)]
-    bundles, distance, places = gather_bundles(sent, top, low, dests, [crossed[0], *local])
-    relayed = []
+    side = (lax.axis_index("probe") % SHARE).reshape(1)
+    share_points = points // SHARE
+    mine, other = call(
+        local_body,
+        [jax.ShapeDtypeStruct((probe_dev, share_points), jnp.float32)] * 2,
+        [SMEM, SMEM, VMEM, VMEM, HBM, HBM],
+        [pltpu.VMEM((near_local.shape[1] * LEAF_PTS, LEAF_PTS), jnp.bfloat16)] * 2
+        + [pltpu.VMEM((2 * probe_dev, points), jnp.bfloat16), pltpu.SemaphoreType.DMA((2,))],
+        micros=10.0,
+    )(
+        jnp.concatenate([(me * leaf_dev).reshape(1), side * (leaf_dev // SHARE)]),
+        near_local, target, source, omega, omega_other,
+    )
+    bundles, distance, places = gather_bundles(sent, top, low, dests, [crossed[0], mine])
+    relayed, raw = [], list(crossed)
     for i, part in enumerate(crossed):
-        crossed[i] = after(part, relayed[-1]) if relayed else after(part, omega_beside, *local)
+        crossed[i] = after(part, relayed[-1]) if relayed else after(part, omega_beside, mine)
         relayed.append(exchange(crossed[i], "leaf", low))
 
-    bundles = list(lax.optimization_barrier((*bundles, relayed[0]))[:-1])
+    bundles = lax.optimization_barrier((*bundles, relayed[0], *raw[1:]))[: len(bundles)]
     pairs = jnp.stack([b[:, points:].astype(jnp.int32).reshape(2, pair_dev) for b in bundles])
     slots = (dests * 4 * CAP + BATCH - 1) // BATCH * BATCH
     codes = far_table(
@@ -396,21 +402,22 @@
             half //= 2
         owns.append(own)
         arrived.append(exchange(rest[0], "leaf", 2))
+    theirs = exchange(other, "probe", 1)
     pick = call(
         pick_body,
         jax.ShapeDtypeStruct((parent_dev, SK2, CHILD * LEAF_PTS), jnp.bfloat16),
         [VMEM] * 2,
     )(skel_rows, parent_interp.transpose(0, 2, 1))
     near, merged, energy = call(
-        functools.partial(merge_body, LOCAL_PARTS, len(chunks)),
+        functools.partial(merge_body, len(chunks)),
         [
             jax.ShapeDtypeStruct((probe_dev, points), jnp.float32),
             jax.ShapeDtypeStruct((probe_dev, parent_dev * SK2), jnp.float32),
             jax.ShapeDtypeStruct((parent_dev, LEAF_PTS), jnp.float32),
         ],
-        [VMEM] * (LOCAL_PARTS + 2 * len(chunks) + 1),
+        [SMEM] + [VMEM] * (2 * len(chunks) + 3),
         micros=2.0,
-    )(*local, *owns, *arrived, pick)
+    )(side, mine, theirs, *owns, *arrived, pick)
     n_probe = lax.axis_size("probe")
     if n_probe & (n_probe - 1):
         energies = [lax.psum(energy, "probe")]

time: 62.9 us -> 61 us (0.970)
  Pallas kernels: 27 us -> 21.3 us
  waiting for transfers between devices: 12.3 us -> 17.5 us
  other arithmetic: 2.38 us -> 0.92 us
  local copies, waits for them, and re-layouts: 3.55 us -> 4.25 us
    pallas_call x2, Pallas kernels: 17.3 us -> 11.7 us  [the longest x1 10.4 us: per_device(): call(local_body, [jax.ShapeDtypeStruct((probe_dev, share_points), jnp.flo...]
    ppermute x12 -> x14, waiting for transfers between devices: 12.3 us -> 17.5 us  [exchange(): return lax.ppermute(array, axis, [(i, i ^ bit) for i in range(size)])]
    unnamed x13 -> x21, local copies, waits for them, and re-layouts: 0.72 us -> 2.11 us
    concatenate x1, other arithmetic: 0.89 us -> 0.03 us  [per_device(): jnp.concatenate([jnp.concatenate([coords, weights[None]], axis=0), far_pa...]
    slice x1, local copies, waits for them, and re-layouts: 1.76 us -> 1.08 us  [per_device(): omega[first:first + size]]
    convert_element_type x1, other arithmetic: 0.68 us -> 0.01 us  [per_device(): far_pairs.reshape(4, pair_columns).astype(jnp.float32)]
    ppermute x12 -> x14, starting transfers between devices: 11.1 us -> 10.9 us  [exchange(): return lax.ppermute(array, axis, [(i, i ^ bit) for i in range(size)])]
  transfers between devices with their start and end apart: 14 -> 16, of which waited for: 7 -> 7; matrix products, arithmetic and copies ran while one was open for 6% -> 5% of each run, Pallas kernels for 40% -> 32%
where the time goes in v5:
time: 61 us; the launch traced here: 60.7 us
  Pallas kernels  21.3 us (35%)
  waiting for transfers between devices  17.5 us (29%)
  starting transfers between devices  15.9 us (26%)
  local copies, waits for them, and re-layouts  4.25 us (7%)
  other arithmetic  0.92 us (2%)
  between operations  0.8 us (1%)
    ppermute x14, waiting for transfers between devices, exchange(): return lax.ppermute(array, axis, [(i, i ^ bit) for i in range(size)])  17.5 us
    ppermute x14, starting transfers between devices, exchange(): return lax.ppermute(array, axis, [(i, i ^ bit) for i in range(size)])  10.9 us
    pallas_call x1, Pallas kernels, per_device(): call(local_body, [jax.ShapeDtypeStruct((probe_dev, share_points), jnp.flo...  10.4 us
    pallas_call x2, Pallas kernels, per_device(): call(functools.partial(far_body, first), [jax.ShapeDtypeStruct((size, poi...  5.39 us
    ppermute x2, starting transfers between devices, gather_bundles(): bundles.append(lax.ppermute(sent, ('leaf', 'probe'), pairs))  5 us
    pallas_call x2, Pallas kernels, features_of(): call(functools.partial(feature_body, len(bundles)), [jax.ShapeDtypeStruct...  2.93 us
    unnamed x21, local copies, waits for them, and re-layouts  2.11 us
    pallas_call x1, Pallas kernels, per_device(): call(functools.partial(merge_body, len(chunks)), [jax.ShapeDtypeStruct((p...  1.29 us
  transfers between devices with their start and end apart: 16, of which 7 were waited for; matrix products, arithmetic and copies ran while one was open for 5% of the time, Pallas kernels for 32%

profile of v5, /device:TPU:0, one launch (start us, length us, event | category | flops | bytes accessed | tf_op | source)
XLA Modules:
  0.0 60.7 jit_solution(16836177782605009590)
XLA Ops:
  1.2 1.1 %fusion.18 = (bf16[32,4096]{1,0:T(8,128)(2,1)S(1)}, bf16[32,4096]{1,0:T(8,128)(2,1)S(1)}) fusion(bf16[64,4096]{1,0:T(8,128)(2,1)} %refs_0_.3), kind=kLoop, calls=%fused_computation.72 | loop fusion | bytes 1048576 | tf_op jit(solution)/shard_map/slice | solution.py:337
  2.3 0.7 %copy-done.7 = s32[2,64]{1,0:T(2,128)S(1)} copy-done((s32[2,64]{1,0:T(2,128)S(1)}, s32[2,64]{1,0:T(2,128)}, u32[]{:S(2)}) %copy-start.7) | copy-done | bytes 536
  3.1 3.7 %collective-permute-start.2 = (f32[4,4128]{1,0:T(4,128)S(1)}, f32[4,4128]{1,0:T(4,128)S(1)}, u32[]{:S(2)}, u32[]{:S(2)}) collective-permute-start(f32[4,4128]{1,0:T(4,128)S(1)} %pad_maximum_fusion.refs_0_), channel_id=1, source_target_pairs={{0,16},{1,5},{2,18},{3,7},{4,20},{5,1},{6,22},{7,3},{8,24},{9,13},... | collective-permute-start | bytes 198152 | tf_op jit(solution)/shard_map/ppermute | solution.py:291
  6.8 1.3 %collective-permute-start.3 = (f32[4,4128]{1,0:T(4,128)S(1)}, f32[4,4128]{1,0:T(4,128)S(1)}, u32[]{:S(2)}, u32[]{:S(2)}) collective-permute-start(f32[4,4128]{1,0:T(4,128)S(1)} %pad_maximum_fusion.refs_0_), channel_id=1, source_target_pairs={{0,20},{1,9},{2,22},{3,11},{4,16},{5,13},{6,18},{7,15},{8,28},{9,1... | collective-permute-start | bytes 198152 | tf_op jit(solution)/shard_map/ppermute | solution.py:291
  8.1 2.6 %collective-permute-start.4 = (bf16[32,4096]{1,0:T(8,128)(2,1)S(1)}, bf16[32,4096]{1,0:T(8,128)(2,1)S(1)}, u32[]{:S(2)}, u32[]{:S(2)}) collective-permute-start(bf16[32,4096]{1,0:T(8,128)(2,1)S(1)} %get-tuple-element.28), channel_id=1, source_target_pairs={{0,16},{4,20},{8,24},{12,28},{16,0},{20,4},{24,8},{28,12},{1,17},{... | collective-permute-start | bytes 786440 | tf_op jit(solution)/shard_map/ppermute | solution.py:268
  11.9 1.0 %shard_map.95 = (bf16[32,4096]{1,0:T(8,128)(2,1)S(1)}, bf16[32,4224]{1,0:T(8,128)(2,1)S(1)}) custom-call(s32[2,1]{1,0:T(2,128)S(1)} %broadcast_21_place_ref.2.place_ref, f32[4,4128]{1,0:T(4,128)S(1)} %pad_maximum_fusion.refs_0_), custom_call_target="tpu_custom_call" | custom-call | flops 10000000 | bytes 30000 | tf_op jit(solution)/shard_map/pallas_call | solution.py:255
  13.2 10.4 %shard_map.96 = (f32[64,2048]{1,0:T(8,128)S(1)}, f32[64,2048]{1,0:T(8,128)S(1)}) custom-call(s32[2]{0:T(128)S(1)} %pad_add_fusion.5.place_ref, s32[32,24]{1,0:T(8,128)S(1)} %copy.11.near_ref, bf16[32,4224]{1,0:T(8,128)(2,1)S(1)} %get-tuple-element.31.target_ref, bf16[32,4096]{1,0:T(8,128)(2,1)S(1)} %get-tuple-element.32.source_ref, ...), custom_call_target="tpu_custom_call" | custom-call | flops 100000000 | bytes 300000 | tf_op jit(solution)/shard_map/pallas_call | solution.py:352
  23.6 0.8 %copy-done.3 = f32[64,2048]{1,0:T(8,128)} copy-done((f32[64,2048]{1,0:T(8,128)}, f32[64,2048]{1,0:T(8,128)S(1)}, u32[]{:S(2)}) %copy-start.3) | copy-done | bytes 524312
  24.4 6.0 %collective-permute-done.4.refs_2_ = bf16[32,4096]{1,0:T(8,128)(2,1)S(1)} collective-permute-done((bf16[32,4096]{1,0:T(8,128)(2,1)S(1)}, bf16[32,4096]{1,0:T(8,128)(2,1)S(1)}, u32[]{:S(2)}, u32[]{:S(2)}) %collective-permute-start.4) | collective-permute-done | bytes 262176 | tf_op jit(solution)/shard_map/ppermute | solution.py:268
  30.4 1.2 %collective-permute-start.8 = (bf16[32,4096]{1,0:T(8,128)(2,1)S(1)}, bf16[32,4096]{1,0:T(8,128)(2,1)S(1)}, u32[]{:S(2)}, u32[]{:S(2)}) collective-permute-start(bf16[32,4096]{1,0:T(8,128)(2,1)S(1)} %collective-permute-done.4.refs_2_), channel_id=1, source_target_pairs={{0,4},{4,0},{8,12},{12,8},{16,20},{20,16},{24,28},{28,24},{1,5},{5... | collective-permute-start | bytes 786440 | tf_op jit(solution)/shard_map/ppermute | solution.py:268
  32.7 1.9 %collective-permute-done.9.refs_2_ = bf16[32,4096]{1,0:T(8,128)(2,1)S(1)} collective-permute-done((bf16[32,4096]{1,0:T(8,128)(2,1)S(1)}, bf16[32,4096]{1,0:T(8,128)(2,1)S(1)}, u32[]{:S(2)}, u32[]{:S(2)}) %collective-permute-start.9) | collective-permute-done | bytes 262176 | tf_op jit(solution)/shard_map/ppermute | solution.py:268
  34.6 2.2 %collective-permute-done.8.refs_3_ = bf16[32,4096]{1,0:T(8,128)(2,1)S(1)} collective-permute-done((bf16[32,4096]{1,0:T(8,128)(2,1)S(1)}, bf16[32,4096]{1,0:T(8,128)(2,1)S(1)}, u32[]{:S(2)}, u32[]{:S(2)}) %collective-permute-start.8) | collective-permute-done | bytes 262176 | tf_op jit(solution)/shard_map/ppermute | solution.py:268
  37.7 1.3 %collective-permute-start.10 = (bf16[32,4096]{1,0:T(8,128)(2,1)S(1)}, bf16[32,4096]{1,0:T(8,128)(2,1)S(1)}, u32[]{:S(2)}, u32[]{:S(2)}) collective-permute-start(bf16[32,4096]{1,0:T(8,128)(2,1)S(1)} %collective-permute-done.9.refs_2_), channel_id=1, source_target_pairs={{0,4},{4,0},{8,12},{12,8},{16,20},{20,16},{24,28},{28,24},{1,5},{5... | collective-permute-start | bytes 786440 | tf_op jit(solution)/shard_map/ppermute | solution.py:268
  39.2 1.9 %shard_map.97 = (bf16[32,16384]{1,0:T(8,128)(2,1)S(1)}, bf16[32,8320]{1,0:T(8,128)(2,1)S(1)}) custom-call(s32[2,5]{1,0:T(2,128)S(1)} %pad_add_fusion.1.place_ref, f32[4,4128]{1,0:T(4,128)S(1)} %pad_maximum_fusion.refs_0_, f32[4,4128]{1,0:T(4,128)S(1)} %collective-permute-done.2.refs_1_, f32[4,4128]{1,0:T(4,128)S(1)} %collective-permute-done.3.refs_2_, ...), custom_call_target="tpu_custom_call" | custom-call | flops 10000000 | bytes 30000 | tf_op jit(solution)/shard_map/pallas_call | solution.py:255
  41.2 2.7 %shard_map.98 = (f32[32,4096]{1,0:T(8,128)S(1)}, bf16[1,32,4096]{2,1,0:T(8,128)(2,1)S(1)}) custom-call(s32[2,144]{1,0:T(2,128)S(1)} %broadcast_add_fusion.table_ref, bf16[32,16384]{1,0:T(8,128)(2,1)S(1)} %get-tuple-element.44.source_ref, bf16[32,8320]{1,0:T(8,128)(2,1)S(1)} %get-tuple-element.45.target_ref, bf16[64,4096]{1,0:T(8,128)(2,1)S(1)} %copy-done, ...), custom_call_target="tpu_custom_call" | custom-call | flops 40000000 | bytes 120000 | tf_op jit(solution)/shard_map/pallas_call | solution.py:380
  44.5 2.7 %shard_map.99 = (f32[32,4096]{1,0:T(8,128)S(1)}, bf16[1,32,4096]{2,1,0:T(8,128)(2,1)S(1)}) custom-call(s32[2,144]{1,0:T(2,128)S(1)} %broadcast_add_fusion.table_ref, bf16[32,16384]{1,0:T(8,128)(2,1)S(1)} %get-tuple-element.44.source_ref, bf16[32,8320]{1,0:T(8,128)(2,1)S(1)} %get-tuple-element.45.target_ref, bf16[64,4096]{1,0:T(8,128)(2,1)S(1)} %copy-done, ...), custom_call_target="tpu_custom_call" | custom-call | flops 40000000 | bytes 120000 | tf_op jit(solution)/shard_map/pallas_call | solution.py:380
  47.2 1.5 %collective-permute-start.12 = (bf16[32,4096]{1,0:T(8,128)(2,1)S(1)}, bf16[32,4096]{1,0:T(8,128)(2,1)S(1)}, u32[]{:S(2)}, u32[]{:S(2)}) collective-permute-start(bf16[32,4096]{1,0:T(8,128)(2,1)S(1)} %bitcast.15), channel_id=1, source_target_pairs={{0,8},{4,12},{8,0},{12,4},{16,24},{20,28},{24,16},{28,20},{1,9},{5... | collective-permute-start | bytes 786440 | tf_op jit(solution)/shard_map/ppermute | solution.py:268
  49.4 2.0 %collective-permute-done.11.refs_2_ = bf16[32,4096]{1,0:T(8,128)(2,1)S(1)} collective-permute-done((bf16[32,4096]{1,0:T(8,128)(2,1)S(1)}, bf16[32,4096]{1,0:T(8,128)(2,1)S(1)}, u32[]{:S(2)}, u32[]{:S(2)}) %collective-permute-start.11) | collective-permute-done | bytes 262176 | tf_op jit(solution)/shard_map/ppermute | solution.py:268
  51.4 2.8 %collective-permute-done.12.refs_3_ = bf16[32,4096]{1,0:T(8,128)(2,1)S(1)} collective-permute-done((bf16[32,4096]{1,0:T(8,128)(2,1)S(1)}, bf16[32,4096]{1,0:T(8,128)(2,1)S(1)}, u32[]{:S(2)}, u32[]{:S(2)}) %collective-permute-start.12) | collective-permute-done | bytes 262176 | tf_op jit(solution)/shard_map/ppermute | solution.py:268
  54.2 1.3 %shard_map.101 = (f32[64,4096]{1,0:T(8,128)}, f32[64,256]{1,0:T(8,128)S(1)}, f32[4,128]{1,0:T(4,128)S(1)}) custom-call(s32[1]{0:T(128)} %bitcast.side_ref, f32[64,2048]{1,0:T(8,128)S(1)} %get-tuple-element.33.mine_ref, f32[64,2048]{1,0:T(8,128)S(1)} %collective-permute-done.1.theirs_ref, f32[32,4096]{1,0:T(8,128)S(1)} %get-tuple-element.46.refs_0_, ...), custom_call_target="tpu_custom_call" | custom-call | flops 20000000 | bytes 60000 | tf_op jit(solution)/shard_map/pallas_call | solution.py:411
  55.5 1.5 %collective-permute-start.14 = (f32[4,128]{1,0:T(4,128)S(1)}, f32[4,128]{1,0:T(4,128)S(1)}, u32[]{:S(2)}, u32[]{:S(2)}) collective-permute-start(f32[4,128]{1,0:T(4,128)S(1)} %get-tuple-element.53.refs_0_), channel_id=1, source_target_pairs={{0,2},{1,3},{2,0},{3,1},{4,6},{5,7},{6,4},{7,5},{8,10},{9,11},{10,... | collective-permute-start | bytes 6152 | tf_op jit(solution)/shard_map/ppermute | solution.py:268
  57.4 1.7 %collective-permute-done.14.refs_2_ = f32[4,128]{1,0:T(4,128)S(1)} collective-permute-done((f32[4,128]{1,0:T(4,128)S(1)}, f32[4,128]{1,0:T(4,128)S(1)}, u32[]{:S(2)}, u32[]{:S(2)}) %collective-permute-start.14) | collective-permute-done | bytes 2080 | tf_op jit(solution)/shard_map/ppermute | solution.py:268
  59.1 0.9 %collective-permute-done.15.refs_3_ = f32[4,128]{1,0:T(4,128)S(1)} collective-permute-done((f32[4,128]{1,0:T(4,128)S(1)}, f32[4,128]{1,0:T(4,128)S(1)}, u32[]{:S(2)}, u32[]{:S(2)}) %collective-permute-start.15) | collective-permute-done | bytes 2080 | tf_op jit(solution)/shard_map/ppermute | solution.py:268
  60.0 0.7 %shard_map.102 = f32[64,256]{1,0:T(8,128)} custom-call(f32[64,256]{1,0:T(8,128)S(1)} %get-tuple-element.52.merged_ref, f32[4,128]{1,0:T(4,128)S(1)} %get-tuple-element.53.refs_0_, f32[4,128]{1,0:T(4,128)S(1)} %collective-permute-done.13.refs_1_, f32[4,128]{1,0:T(4,128)S(1)} %collective-permute-done.14.refs_2_, f32[4,128]{1,0:T(4,128)S(1)} %collective-permute-done.15.refs_3_), custom_call_target="tpu_custom_call" | custom-call | flops 10000000 | bytes 30000 | tf_op jit(solution)/shard_map/pallas_call | solution.py:426
  (76 shorter events, 6.0 us)
Async XLA Ops:
  0.6 10.0 %copy-start = (bf16[64,4096]{1,0:T(8,128)(2,1)S(1)}, bf16[64,4096]{1,0:T(8,128)(2,1)}, u32[]{:S(2)}) copy-start(bf16[64,4096]{1,0:T(8,128)(2,1)} %refs_0_.3) | copy-start | bytes 1572868
  0.6 2.4 %copy-start.4 = (f32[3,4096]{1,0:T(4,128)S(1)}, f32[3,4096]{1,0:T(4,128)}, u32[]{:S(2)}) copy-start(f32[3,4096]{1,0:T(4,128)} %param.8) | copy-start | bytes 147460
  0.6 12.4 %collective-permute-start = (bf16[64,4096]{1,0:T(8,128)(2,1)}, bf16[64,4096]{1,0:T(8,128)(2,1)S(1)}, u32[]{:S(2)}, u32[]{:S(2)}) collective-permute-start(bf16[64,4096]{1,0:T(8,128)(2,1)} %refs_0_.3), channel_id=1, source_target_pairs={{0,1},{1,0},{2,3},{3,2},{4,5},{5,4},{6,7},{7,6},{8,9},{9,8},{10,11... | collective-permute-start | bytes 1572872 | tf_op jit(solution)/shard_map/ppermute | solution.py:268
  1.2 1.9 %copy-start.5 = (f32[4096]{0:T(1024)S(1)}, f32[4096]{0:T(1024)}, u32[]{:S(2)}) copy-start(f32[4096]{0:T(1024)} %param.9) | copy-start | bytes 49156
  2.3 0.7 %copy-start.7 = (s32[2,64]{1,0:T(2,128)S(1)}, s32[2,64]{1,0:T(2,128)}, u32[]{:S(2)}) copy-start(s32[2,64]{1,0:T(2,128)} %param.12) | copy-start | bytes 1540
  3.1 29.0 %collective-permute-start.2 = (f32[4,4128]{1,0:T(4,128)S(1)}, f32[4,4128]{1,0:T(4,128)S(1)}, u32[]{:S(2)}, u32[]{:S(2)}) collective-permute-start(f32[4,4128]{1,0:T(4,128)S(1)} %pad_maximum_fusion.refs_0_), channel_id=1, source_target_pairs={{0,16},{1,5},{2,18},{3,7},{4,20},{5,1},{6,22},{7,3},{8,24},{9,13},... | collective-permute-start | bytes 198152 | tf_op jit(solution)/shard_map/ppermute | solution.py:291
  6.8 25.3 %collective-permute-start.3 = (f32[4,4128]{1,0:T(4,128)S(1)}, f32[4,4128]{1,0:T(4,128)S(1)}, u32[]{:S(2)}, u32[]{:S(2)}) collective-permute-start(f32[4,4128]{1,0:T(4,128)S(1)} %pad_maximum_fusion.refs_0_), channel_id=1, source_target_pairs={{0,20},{1,9},{2,22},{3,11},{4,16},{5,13},{6,18},{7,15},{8,28},{9,1... | collective-permute-start | bytes 198152 | tf_op jit(solution)/shard_map/ppermute | solution.py:291
  8.1 22.3 %collective-permute-start.4 = (bf16[32,4096]{1,0:T(8,128)(2,1)S(1)}, bf16[32,4096]{1,0:T(8,128)(2,1)S(1)}, u32[]{:S(2)}, u32[]{:S(2)}) collective-permute-start(bf16[32,4096]{1,0:T(8,128)(2,1)S(1)} %get-tuple-element.28), channel_id=1, source_target_pairs={{0,16},{4,20},{8,24},{12,28},{16,0},{20,4},{24,8},{28,12},{1,17},{... | collective-permute-start | bytes 786440 | tf_op jit(solution)/shard_map/ppermute | solution.py:268
  10.7 19.8 %collective-permute-start.7 = (bf16[64,4096]{1,0:T(8,128)(2,1)S(1)}, bf16[64,4096]{1,0:T(8,128)(2,1)S(1)}, u32[]{:S(2)}, u32[]{:S(2)}) collective-permute-start(bf16[64,4096]{1,0:T(8,128)(2,1)S(1)} %copy-done), channel_id=1, source_target_pairs={{0,4},{4,0},{8,12},{12,8},{16,20},{20,16},{24,28},{28,24},{1,5},{5... | collective-permute-start | bytes 1572872 | tf_op jit(solution)/shard_map/ppermute | solution.py:268
  11.2 0.7 %copy-start.6 = (s32[32,24]{0,1:T(8,128)S(1)}, s32[32,24]{0,1:T(8,128)}, u32[]{:S(2)}) copy-start(s32[32,24]{0,1:T(8,128)} %param.11) | copy-start | bytes 9220
  13.1 21.5 %collective-permute-start.9 = (bf16[32,4096]{1,0:T(8,128)(2,1)S(1)}, bf16[32,4096]{1,0:T(8,128)(2,1)S(1)}, u32[]{:S(2)}, u32[]{:S(2)}) collective-permute-start(bf16[32,4096]{1,0:T(8,128)(2,1)S(1)} %get-tuple-element.29), channel_id=1, source_target_pairs={{0,16},{4,20},{8,24},{12,28},{16,0},{20,4},{24,8},{28,12},{1,17},{... | collective-permute-start | bytes 786440 | tf_op jit(solution)/shard_map/ppermute | solution.py:268
  23.6 0.8 %copy-start.3 = (f32[64,2048]{1,0:T(8,128)}, f32[64,2048]{1,0:T(8,128)S(1)}, u32[]{:S(2)}) copy-start(f32[64,2048]{1,0:T(8,128)S(1)} %get-tuple-element.34) | copy-start | bytes 1572868
  30.4 6.4 %collective-permute-start.8 = (bf16[32,4096]{1,0:T(8,128)(2,1)S(1)}, bf16[32,4096]{1,0:T(8,128)(2,1)S(1)}, u32[]{:S(2)}, u32[]{:S(2)}) collective-permute-start(bf16[32,4096]{1,0:T(8,128)(2,1)S(1)} %collective-permute-done.4.refs_2_), channel_id=1, source_target_pairs={{0,4},{4,0},{8,12},{12,8},{16,20},{20,16},{24,28},{28,24},{1,5},{5... | collective-permute-start | bytes 786440 | tf_op jit(solution)/shard_map/ppermute | solution.py:268
  32.0 2.5 %collective-permute-start.5 = (f32[4,4128]{1,0:T(4,128)S(1)}, f32[4,4128]{1,0:T(4,128)S(1)}, u32[]{:S(2)}, u32[]{:S(2)}) collective-permute-start(f32[4,4128]{1,0:T(4,128)S(1)} %collective-permute-done.2.refs_1_), channel_id=1, source_target_pairs={{0,1},{1,0},{2,3},{3,2},{4,5},{5,4},{6,7},{7,6},{8,9},{9,8},{10,11... | collective-permute-start | bytes 198152 | tf_op jit(solution)/shard_map/ppermute | solution.py:268
  32.1 2.5 %collective-permute-start.6 = (f32[4,4128]{1,0:T(4,128)S(1)}, f32[4,4128]{1,0:T(4,128)S(1)}, u32[]{:S(2)}, u32[]{:S(2)}) collective-permute-start(f32[4,4128]{1,0:T(4,128)S(1)} %collective-permute-done.3.refs_2_), channel_id=1, source_target_pairs={{0,1},{1,0},{2,3},{3,2},{4,5},{5,4},{6,7},{7,6},{8,9},{9,8},{10,11... | collective-permute-start | bytes 198152 | tf_op jit(solution)/shard_map/ppermute | solution.py:268
  32.6 18.8 %collective-permute-start.1 = (f32[64,2048]{1,0:T(8,128)}, f32[64,2048]{1,0:T(8,128)S(1)}, u32[]{:S(2)}, u32[]{:S(2)}) collective-permute-start(f32[64,2048]{1,0:T(8,128)} %copy-done.3), channel_id=1, source_target_pairs={{0,1},{1,0},{2,3},{3,2},{4,5},{5,4},{6,7},{7,6},{8,9},{9,8},{10,11... | collective-permute-start | bytes 1572872 | tf_op jit(solution)/shard_map/ppermute | solution.py:268
  37.7 6.8 %collective-permute-start.10 = (bf16[32,4096]{1,0:T(8,128)(2,1)S(1)}, bf16[32,4096]{1,0:T(8,128)(2,1)S(1)}, u32[]{:S(2)}, u32[]{:S(2)}) collective-permute-start(bf16[32,4096]{1,0:T(8,128)(2,1)S(1)} %collective-permute-done.9.refs_2_), channel_id=1, source_target_pairs={{0,4},{4,0},{8,12},{12,8},{16,20},{20,16},{24,28},{28,24},{1,5},{5... | collective-permute-start | bytes 786440 | tf_op jit(solution)/shard_map/ppermute | solution.py:268
  43.9 4.9 %copy-start.1 = (bf16[4,256,64]{1,2,0:T(8,128)(2,1)S(1)}, bf16[4,256,64]{1,2,0:T(8,128)(2,1)}, u32[]{:S(2)}) copy-start(bf16[4,256,64]{1,2,0:T(8,128)(2,1)} %param.14) | copy-start | bytes 393220
  43.9 7.5 %collective-permute-start.11 = (bf16[32,4096]{1,0:T(8,128)(2,1)S(1)}, bf16[32,4096]{1,0:T(8,128)(2,1)S(1)}, u32[]{:S(2)}, u32[]{:S(2)}) collective-permute-start(bf16[32,4096]{1,0:T(8,128)(2,1)S(1)} %bitcast.14), channel_id=1, source_target_pairs={{0,8},{4,12},{8,0},{12,4},{16,24},{20,28},{24,16},{28,20},{1,9},{5... | collective-permute-start | bytes 786440 | tf_op jit(solution)/shard_map/ppermute | solution.py:268
  44.5 4.2 %copy-start.2 = (s32[32,32]{1,0:T(8,128)S(1)}, s32[32,32]{1,0:T(8,128)}, u32[]{:S(2)}) copy-start(s32[32,32]{1,0:T(8,128)} %skel_ref.1) | copy-start | bytes 12292
  47.2 7.0 %collective-permute-start.12 = (bf16[32,4096]{1,0:T(8,128)(2,1)S(1)}, bf16[32,4096]{1,0:T(8,128)(2,1)S(1)}, u32[]{:S(2)}, u32[]{:S(2)}) collective-permute-start(bf16[32,4096]{1,0:T(8,128)(2,1)S(1)} %bitcast.15), channel_id=1, source_target_pairs={{0,8},{4,12},{8,0},{12,4},{16,24},{20,28},{24,16},{28,20},{1,9},{5... | collective-permute-start | bytes 786440 | tf_op jit(solution)/shard_map/ppermute | solution.py:268
  55.5 1.9 %collective-permute-start.13 = (f32[4,128]{1,0:T(4,128)S(1)}, f32[4,128]{1,0:T(4,128)S(1)}, u32[]{:S(2)}, u32[]{:S(2)}) collective-permute-start(f32[4,128]{1,0:T(4,128)S(1)} %get-tuple-element.53.refs_0_), channel_id=1, source_target_pairs={{0,1},{1,0},{2,3},{3,2},{4,5},{5,4},{6,7},{7,6},{8,9},{9,8},{10,11... | collective-permute-start | bytes 6152 | tf_op jit(solution)/shard_map/ppermute | solution.py:268
  55.5 3.6 %collective-permute-start.14 = (f32[4,128]{1,0:T(4,128)S(1)}, f32[4,128]{1,0:T(4,128)S(1)}, u32[]{:S(2)}, u32[]{:S(2)}) collective-permute-start(f32[4,128]{1,0:T(4,128)S(1)} %get-tuple-element.53.refs_0_), channel_id=1, source_target_pairs={{0,2},{1,3},{2,0},{3,1},{4,6},{5,7},{6,4},{7,5},{8,10},{9,11},{10,... | collective-permute-start | bytes 6152 | tf_op jit(solution)/shard_map/ppermute | solution.py:268
  57.0 3.0 %collective-permute-start.15 = (f32[4,128]{1,0:T(4,128)S(1)}, f32[4,128]{1,0:T(4,128)S(1)}, u32[]{:S(2)}, u32[]{:S(2)}) collective-permute-start(f32[4,128]{1,0:T(4,128)S(1)} %get-tuple-element.53.refs_0_), channel_id=1, source_target_pairs={{0,3},{1,2},{2,1},{3,0},{4,7},{5,6},{6,5},{7,4},{8,11},{9,10},{10,... | collective-permute-start | bytes 6152 | tf_op jit(solution)/shard_map/ppermute | solution.py:268

commit v6 on v5

--- a/solution.py
+++ b/solution.py
@@ -68,12 +68,8 @@
 
 
 def feature_body(n_bundle, place_ref, *refs):
-    source_ref, target_ref, rows = refs[-3:]
+    source_ref, target_ref, rows = refs[n_bundle:]
     points = rows.shape[1]
-    if len(refs) > n_bundle + 3:
-        own_source_ref, own_target_ref = refs[n_bundle:-3]
-        source_ref[:, :points] = own_source_ref[...]
-        target_ref[:, :points] = own_target_ref[:, :points]
     target_ref[:, target_ref.shape[1] - LEAF_PTS :] = jnp.ones((FEATURES, LEAF_PTS), jnp.bfloat16)
     rows[27:FEATURES, :] = jnp.zeros((FEATURES - 27, points), jnp.float32)
     for i in range(n_bundle):
@@ -84,6 +80,60 @@
             def _(points_ref=refs[i], place=place, out_ref=out_ref, kind=kind):
                 lanes = pl.ds(pl.multiple_of(place * points, LEAF_PTS), points)
                 write_features(points_ref, rows, out_ref.at[:, lanes], kind == 0)
+
+
+def far_prepare_body(n_bundle, outer, place_ref, *refs):
+    source_ref, target_ref, table_ref, rows, inside_ref, values_ref, turned_ref = refs[n_bundle:]
+    feature_body(n_bundle, place_ref, *refs[:n_bundle], source_ref, target_ref, rows)
+    points = rows.shape[1]
+    leaf_dev = points // LEAF_PTS
+    shift = leaf_dev.bit_length() - 1
+    spare = target_ref.shape[1] // LEAF_PTS - 1
+    columns = refs[0].shape[1] - points
+    inside_ref[...] = jnp.zeros_like(inside_ref)
+    values_ref[...] = jnp.zeros_like(values_ref)
+    me = place_ref[3, 0]
+    for i in range(n_bundle):
+        sender = place_ref[0, i]
+        pairs = refs[i][:, points:]
+        offset = ((me ^ place_ref[2, i]) - sender) * leaf_dev
+        source = pairs[0:2] - offset.astype(jnp.float32)
+        target = pairs[2:4].astype(jnp.int32)
+        relation = lax.shift_right_logical(target, shift) ^ me
+        owned = ((relation & outer) == 0) & (sender >= 0)
+        member = lax.shift_right_logical(relation, 1) * leaf_dev + (target & (leaf_dev - 1))
+        inside_ref[2 * i : 2 * i + 2, :columns] = owned.astype(jnp.float32)
+        for h in range(2):
+            values_ref[2 * i + h, 0:1, :columns] = source[h : h + 1]
+            values_ref[2 * i + h, 1:2, :columns] = (member - spare)[h : h + 1].astype(jnp.float32)
+    inside = inside_ref[...]
+    count = inside.shape[0]
+
+    def iota(shape, axis):
+        return lax.broadcasted_iota(jnp.int32, shape, axis)
+
+    def product(left, right):
+        return jnp.dot(
+            left.astype(jnp.bfloat16),
+            right.astype(jnp.bfloat16),
+            preferred_element_type=jnp.float32,
+        )
+
+    square, low = (LEAF_PTS, LEAF_PTS), (count, count)
+    earlier = (iota(square, 0) < iota(square, 1)).astype(jnp.float32)
+    above = (iota(low, 1) < iota(low, 0)).astype(jnp.float32)
+    place = product(inside, earlier) + product(above, product(inside, jnp.ones(square)))
+    turned_ref[...] = jnp.full(square, -1.0)
+    turned_ref[:count, :] = jnp.where(inside > 0, place, -1.0)
+    turned = jnp.transpose(turned_ref[...])
+    length = table_ref.shape[1]
+    wide = (length + LEAF_PTS - 1) // LEAF_PTS * LEAF_PTS
+    slot = iota((LEAF_PTS, wide), 1).astype(jnp.float32)
+    table = jnp.zeros((8, wide), jnp.float32)
+    for r in range(2 * n_bundle):
+        hit = (turned[:, r : r + 1] == slot).astype(jnp.float32)
+        table = table + product(values_ref[r], hit)
+    table_ref[...] = table[0:2, :length].astype(jnp.int32) + iota((2, length), 0) * spare
 
 
 def turned_block(source, target):
@@ -305,21 +355,6 @@
     )
 
 
-def far_table(pairs, me, distance, sender, outer, leaf_dev, length, spare):
-    source = pairs[:, 0] - (((me ^ distance) - sender) * leaf_dev)[:, None]
-    relation = (pairs[:, 1] // leaf_dev) ^ me
-    inside = (((relation & outer) == 0) & (sender >= 0)[:, None]).reshape(-1)
-    target = (relation // 2) * leaf_dev + pairs[:, 1] % leaf_dev
-    iota = jnp.arange(inside.shape[0], dtype=jnp.int32)
-    place = jnp.sum(
-        (inside[:, None] & (iota[:, None] < iota[None, :])).astype(jnp.int32), axis=0
-    )
-    place = jnp.where(inside, place, -1)
-    hit = place[None, None, :] == jnp.arange(length, dtype=jnp.int32)[None, :, None]
-    codes = jnp.stack([source.reshape(-1), target.reshape(-1) - spare])
-    return jnp.sum(jnp.where(hit, codes[:, None, :], 0), axis=2) + jnp.array([[0], [spare]])
-
-
 def per_device(coords, weights, omega, near_local, far_pairs, skel_rows, parent_interp):
     n_leaf = lax.axis_size("leaf")
     points = coords.shape[1]
@@ -361,20 +396,31 @@
         near_local, target, source, omega, omega_other,
     )
     bundles, distance, places = gather_bundles(sent, top, low, dests, [crossed[0], mine])
-    relayed, raw = [], list(crossed)
-    for i, part in enumerate(crossed):
-        crossed[i] = after(part, relayed[-1]) if relayed else after(part, omega_beside, mine)
+    crossed[0] = after(crossed[0], omega_beside, mine)
+    relayed = [exchange(crossed[0], "leaf", low)]
+    slots = (dests * 4 * CAP + BATCH - 1) // BATCH * BATCH
+    n_rows = (2 * len(bundles) + 7) // 8 * 8
+    far_source, far_target, codes = call(
+        functools.partial(far_prepare_body, len(bundles), top | low),
+        [
+            jax.ShapeDtypeStruct((FEATURES, 4 * points), jnp.bfloat16),
+            jax.ShapeDtypeStruct((FEATURES, dests * points + LEAF_PTS), jnp.bfloat16),
+            jax.ShapeDtypeStruct((2, slots), jnp.int32),
+        ],
+        [SMEM] + [VMEM] * len(bundles),
+        [
+            pltpu.VMEM((FEATURES, points), jnp.float32),
+            pltpu.VMEM((n_rows, LEAF_PTS), jnp.float32),
+            pltpu.VMEM((n_rows, 8, LEAF_PTS), jnp.float32),
+            pltpu.VMEM((LEAF_PTS, LEAF_PTS), jnp.float32),
+        ],
+    )(
+        jnp.concatenate([places, distance[None], jnp.broadcast_to(me, (1, len(bundles)))]),
+        *bundles,
+    )
+    for i, part in enumerate(crossed[1:], 1):
+        crossed[i] = after(part, relayed[-1], codes)
         relayed.append(exchange(crossed[i], "leaf", low))
-
-    bundles = lax.optimization_barrier((*bundles, relayed[0], *raw[1:]))[: len(bundles)]
-    pairs = jnp.stack([b[:, points:].astype(jnp.int32).reshape(2, pair_dev) for b in bundles])
-    slots = (dests * 4 * CAP + BATCH - 1) // BATCH * BATCH
-    codes = far_table(
-        pairs, me, distance, places[0], top | low, leaf_dev, slots, dests * leaf_dev
-    )
-    far_source, far_target = features_of(
-        points, 4, dests, places, bundles
-    )
     owns, arrived = [], []
     for (first, size), from_across, from_both in zip(chunks, crossed, relayed):
         own, rest = call(

time: 61 us -> 60.5 us (level)
  local copies, waits for them, and re-layouts: 4.25 us -> 1.94 us
  Pallas kernels: 21.3 us -> 23.3 us
  waiting for transfers between devices: 17.5 us -> 18.5 us
    pallas_call x0 -> x1, Pallas kernels: none -> 2.71 us  [per_device(): call(functools.partial(far_prepare_body, len(bundles), top | low), [jax.S...]
    ppermute x2, waiting for transfers between devices: 0.01 us -> 2.18 us  [gather_bundles(): bundles.append(lax.ppermute(sent, ('leaf', 'probe'), pairs))]
    pallas_call x2 -> x1, Pallas kernels: 2.93 us -> 0.99 us  [features_of(): call(functools.partial(feature_body, len(bundles)), [jax.ShapeDtypeStruct...]
    unnamed x21 -> x15, local copies, waits for them, and re-layouts: 2.11 us -> 0.7 us
    pallas_call x2, Pallas kernels: 5.39 us -> 6.61 us  [per_device(): call(functools.partial(far_body, first), [jax.ShapeDtypeStruct((size, poi...]
    ppermute x14, waiting for transfers between devices: 17.5 us -> 16.3 us  [exchange(): return lax.ppermute(array, axis, [(i, i ^ bit) for i in range(size)])]
    ppermute x2, starting transfers between devices: 5 us -> 3.95 us  [gather_bundles(): bundles.append(lax.ppermute(sent, ('leaf', 'probe'), pairs))]
  transfers between devices with their start and end apart: 16 -> 16, of which waited for: 7 -> 10; matrix products, arithmetic and copies ran while one was open for 5% -> 3% of each run, Pallas kernels for 32% -> 35%
where the time goes in v6:
time: 60.5 us; the launch traced here: 60.2 us
  Pallas kernels  23.3 us (39%)
  waiting for transfers between devices  18.5 us (31%)
  starting transfers between devices  15.3 us (25%)
  local copies, waits for them, and re-layouts  1.94 us (3%)
  between operations  0.77 us (1%)
    ppermute x14, waiting for transfers between devices, exchange(): return lax.ppermute(array, axis, [(i, i ^ bit) for i in range(size)])  16.3 us
    ppermute x14, starting transfers between devices, exchange(): return lax.ppermute(array, axis, [(i, i ^ bit) for i in range(size)])  11.3 us
    pallas_call x1, Pallas kernels, per_device(): call(local_body, [jax.ShapeDtypeStruct((probe_dev, share_points), jnp.flo...  10.4 us
    pallas_call x2, Pallas kernels, per_device(): call(functools.partial(far_body, first), [jax.ShapeDtypeStruct((size, poi...  6.61 us
    ppermute x2, starting transfers between devices, gather_bundles(): bundles.append(lax.ppermute(sent, ('leaf', 'probe'), pairs))  3.95 us
    pallas_call x1, Pallas kernels, per_device(): call(functools.partial(far_prepare_body, len(bundles), top | low), [jax.S...  2.71 us
    ppermute x2, waiting for transfers between devices, gather_bundles(): bundles.append(lax.ppermute(sent, ('leaf', 'probe'), pairs))  2.18 us
    pallas_call x1, Pallas kernels, per_device(): call(functools.partial(merge_body, len(chunks)), [jax.ShapeDtypeStruct((p...  1.29 us
  transfers between devices with their start and end apart: 16, of which 10 were waited for; matrix products, arithmetic and copies ran while one was open for 3% of the time, Pallas kernels for 35%

profile of v6, /device:TPU:0, one launch (start us, length us, event | category | flops | bytes accessed | tf_op | source)
XLA Modules:
  0.0 60.2 jit_solution(1137599329241104296)
XLA Ops:
  1.2 1.1 %fusion.7 = (bf16[32,4096]{1,0:T(8,128)(2,1)S(1)}, bf16[32,4096]{1,0:T(8,128)(2,1)S(1)}) fusion(bf16[64,4096]{1,0:T(8,128)(2,1)} %refs_0_.3), kind=kLoop, calls=%fused_computation.26 | loop fusion | bytes 1048576 | tf_op jit(solution)/shard_map/slice | solution.py:372
  2.3 3.7 %collective-permute-start.4 = (bf16[32,4096]{1,0:T(8,128)(2,1)S(1)}, bf16[32,4096]{1,0:T(8,128)(2,1)S(1)}, u32[]{:S(2)}, u32[]{:S(2)}) collective-permute-start(bf16[32,4096]{1,0:T(8,128)(2,1)S(1)} %get-tuple-element.24), channel_id=1, source_target_pairs={{0,16},{4,20},{8,24},{12,28},{16,0},{20,4},{24,8},{28,12},{1,17},{... | collective-permute-start | bytes 786440 | tf_op jit(solution)/shard_map/ppermute | solution.py:318
  6.1 0.7 %collective-permute-start.2 = (f32[4,4128]{1,0:T(4,128)S(1)}, f32[4,4128]{1,0:T(4,128)S(1)}, u32[]{:S(2)}, u32[]{:S(2)}) collective-permute-start(f32[4,4128]{1,0:T(4,128)S(1)} %pad_maximum_fusion.refs_0_), channel_id=1, source_target_pairs={{0,16},{1,5},{2,18},{3,7},{4,20},{5,1},{6,22},{7,3},{8,24},{9,13},... | collective-permute-start | bytes 198152 | tf_op jit(solution)/shard_map/ppermute | solution.py:341
  6.8 3.3 %collective-permute-start.3 = (f32[4,4128]{1,0:T(4,128)S(1)}, f32[4,4128]{1,0:T(4,128)S(1)}, u32[]{:S(2)}, u32[]{:S(2)}) collective-permute-start(f32[4,4128]{1,0:T(4,128)S(1)} %pad_maximum_fusion.refs_0_), channel_id=1, source_target_pairs={{0,20},{1,9},{2,22},{3,11},{4,16},{5,13},{6,18},{7,15},{8,28},{9,1... | collective-permute-start | bytes 198152 | tf_op jit(solution)/shard_map/ppermute | solution.py:341
  11.3 1.0 %shard_map.86 = (bf16[32,4096]{1,0:T(8,128)(2,1)S(1)}, bf16[32,4224]{1,0:T(8,128)(2,1)S(1)}) custom-call(s32[2,1]{1,0:T(2,128)S(1)} %broadcast_15_place_ref.2.place_ref, f32[4,4128]{1,0:T(4,128)S(1)} %pad_maximum_fusion.refs_0_), custom_call_target="tpu_custom_call" | custom-call | flops 10000000 | bytes 30000 | tf_op jit(solution)/shard_map/pallas_call | solution.py:305
  13.1 10.4 %shard_map.87 = (f32[64,2048]{1,0:T(8,128)S(1)}, f32[64,2048]{1,0:T(8,128)S(1)}) custom-call(s32[2]{0:T(128)S(1)} %pad_add_fusion.3.place_ref, s32[32,24]{1,0:T(8,128)S(1)} %copy.9.near_ref, bf16[32,4224]{1,0:T(8,128)(2,1)S(1)} %get-tuple-element.27.target_ref, bf16[32,4096]{1,0:T(8,128)(2,1)S(1)} %get-tuple-element.28.source_ref, ...), custom_call_target="tpu_custom_call" | custom-call | flops 100000000 | bytes 300000 | tf_op jit(solution)/shard_map/pallas_call | solution.py:387
  23.5 2.3 %collective-permute-done.4.refs_2_ = bf16[32,4096]{1,0:T(8,128)(2,1)S(1)} collective-permute-done((bf16[32,4096]{1,0:T(8,128)(2,1)S(1)}, bf16[32,4096]{1,0:T(8,128)(2,1)S(1)}, u32[]{:S(2)}, u32[]{:S(2)}) %collective-permute-start.4) | collective-permute-done | bytes 262176 | tf_op jit(solution)/shard_map/ppermute | solution.py:318
  25.8 1.8 %collective-permute-start.8 = (bf16[32,4096]{1,0:T(8,128)(2,1)S(1)}, bf16[32,4096]{1,0:T(8,128)(2,1)S(1)}, u32[]{:S(2)}, u32[]{:S(2)}) collective-permute-start(bf16[32,4096]{1,0:T(8,128)(2,1)S(1)} %collective-permute-done.4.refs_2_), channel_id=1, source_target_pairs={{0,4},{4,0},{8,12},{12,8},{16,20},{20,16},{24,28},{28,24},{1,5},{5... | collective-permute-start | bytes 786440 | tf_op jit(solution)/shard_map/ppermute | solution.py:318
  27.7 2.2 %collective-permute-done.3.refs_2_ = f32[4,4128]{1,0:T(4,128)S(1)} collective-permute-done((f32[4,4128]{1,0:T(4,128)S(1)}, f32[4,4128]{1,0:T(4,128)S(1)}, u32[]{:S(2)}, u32[]{:S(2)}) %collective-permute-start.3) | collective-permute-done | bytes 66080 | tf_op jit(solution)/shard_map/ppermute | solution.py:341
  30.5 0.7 %collective-permute-done.5.refs_3_ = f32[4,4128]{1,0:T(4,128)S(1)} collective-permute-done((f32[4,4128]{1,0:T(4,128)S(1)}, f32[4,4128]{1,0:T(4,128)S(1)}, u32[]{:S(2)}, u32[]{:S(2)}) %collective-permute-start.5) | collective-permute-done | bytes 66080 | tf_op jit(solution)/shard_map/ppermute | solution.py:318
  31.3 2.7 %shard_map.88 = (bf16[32,16384]{1,0:T(8,128)(2,1)S(1)}, bf16[32,8320]{1,0:T(8,128)(2,1)S(1)}, s32[2,144]{1,0:T(2,128)S(1)}) custom-call(s32[4,5]{1,0:T(4,128)S(1)} %add_add_fusion.place_ref, f32[4,4128]{1,0:T(4,128)S(1)} %pad_maximum_fusion.refs_0_, f32[4,4128]{1,0:T(4,128)S(1)} %collective-permute-done.2.refs_1_, ...), custom_call_target="tpu_custom_call" | custom-call | flops 10000000 | bytes 30000 | tf_op jit(solution)/shard_map/pallas_call | solution.py:403
  34.4 1.0 %collective-permute-start.10 = (bf16[32,4096]{1,0:T(8,128)(2,1)S(1)}, bf16[32,4096]{1,0:T(8,128)(2,1)S(1)}, u32[]{:S(2)}, u32[]{:S(2)}) collective-permute-start(bf16[32,4096]{1,0:T(8,128)(2,1)S(1)} %collective-permute-done.9.refs_2_), channel_id=1, source_target_pairs={{0,4},{4,0},{8,12},{12,8},{16,20},{20,16},{24,28},{28,24},{1,5},{5... | collective-permute-start | bytes 786440 | tf_op jit(solution)/shard_map/ppermute | solution.py:318
  35.4 3.3 %shard_map.89 = (f32[32,4096]{1,0:T(8,128)S(1)}, bf16[1,32,4096]{2,1,0:T(8,128)(2,1)S(1)}) custom-call(s32[2,144]{1,0:T(2,128)S(1)} %get-tuple-element.33.table_ref, bf16[32,16384]{1,0:T(8,128)(2,1)S(1)} %get-tuple-element.34.source_ref, bf16[32,8320]{1,0:T(8,128)(2,1)S(1)} %get-tuple-element.35.target_ref, bf16[64,4096]{1,0:T(8,128)(2,1)S(1)} %copy-done, ...), custom_call_target="tpu_custom_call" | custom-call | flops 40000000 | bytes 120000 | tf_op jit(solution)/shard_map/pallas_call | solution.py:426
  38.7 0.8 %collective-permute-start.11 = (bf16[32,4096]{1,0:T(8,128)(2,1)S(1)}, bf16[32,4096]{1,0:T(8,128)(2,1)S(1)}, u32[]{:S(2)}, u32[]{:S(2)}) collective-permute-start(bf16[32,4096]{1,0:T(8,128)(2,1)S(1)} %bitcast.17), channel_id=1, source_target_pairs={{0,8},{4,12},{8,0},{12,4},{16,24},{20,28},{24,16},{28,20},{1,9},{5... | collective-permute-start | bytes 786440 | tf_op jit(solution)/shard_map/ppermute | solution.py:318
  39.5 3.2 %collective-permute-done.10.refs_3_ = bf16[32,4096]{1,0:T(8,128)(2,1)S(1)} collective-permute-done((bf16[32,4096]{1,0:T(8,128)(2,1)S(1)}, bf16[32,4096]{1,0:T(8,128)(2,1)S(1)}, u32[]{:S(2)}, u32[]{:S(2)}) %collective-permute-start.10) | collective-permute-done | bytes 262176 | tf_op jit(solution)/shard_map/ppermute | solution.py:318
  42.7 3.3 %shard_map.90 = (f32[32,4096]{1,0:T(8,128)S(1)}, bf16[1,32,4096]{2,1,0:T(8,128)(2,1)S(1)}) custom-call(s32[2,144]{1,0:T(2,128)S(1)} %get-tuple-element.33.table_ref, bf16[32,16384]{1,0:T(8,128)(2,1)S(1)} %get-tuple-element.34.source_ref, bf16[32,8320]{1,0:T(8,128)(2,1)S(1)} %get-tuple-element.35.target_ref, bf16[64,4096]{1,0:T(8,128)(2,1)S(1)} %copy-done, ...), custom_call_target="tpu_custom_call" | custom-call | flops 40000000 | bytes 120000 | tf_op jit(solution)/shard_map/pallas_call | solution.py:426
  46.1 0.6 %shard_map.91.refs_4_ = bf16[4,64,1024]{2,1,0:T(8,128)(2,1)S(1)} custom-call(s32[32,32]{1,0:T(8,128)S(1)} %copy-done.2, bf16[4,64,256]{2,1,0:T(8,128)(2,1)S(1)} %bitcast.16), custom_call_target="tpu_custom_call" | custom-call | flops 10000000 | bytes 30000 | tf_op jit(solution)/shard_map/pallas_call | solution.py:452
  46.7 0.8 %collective-permute-done.11.refs_2_ = bf16[32,4096]{1,0:T(8,128)(2,1)S(1)} collective-permute-done((bf16[32,4096]{1,0:T(8,128)(2,1)S(1)}, bf16[32,4096]{1,0:T(8,128)(2,1)S(1)}, u32[]{:S(2)}, u32[]{:S(2)}) %collective-permute-start.11) | collective-permute-done | bytes 262176 | tf_op jit(solution)/shard_map/ppermute | solution.py:318
  47.5 6.0 %collective-permute-done.12.refs_3_ = bf16[32,4096]{1,0:T(8,128)(2,1)S(1)} collective-permute-done((bf16[32,4096]{1,0:T(8,128)(2,1)S(1)}, bf16[32,4096]{1,0:T(8,128)(2,1)S(1)}, u32[]{:S(2)}, u32[]{:S(2)}) %collective-permute-start.12) | collective-permute-done | bytes 262176 | tf_op jit(solution)/shard_map/ppermute | solution.py:318
  53.5 1.3 %shard_map.92 = (f32[64,4096]{1,0:T(8,128)}, f32[64,256]{1,0:T(8,128)S(1)}, f32[4,128]{1,0:T(4,128)S(1)}) custom-call(s32[1]{0:T(128)} %bitcast.side_ref, f32[64,2048]{1,0:T(8,128)S(1)} %get-tuple-element.29.mine_ref, f32[64,2048]{1,0:T(8,128)S(1)} %collective-permute-done.1.theirs_ref, f32[32,4096]{1,0:T(8,128)S(1)} %get-tuple-element.38.refs_0_, ...), custom_call_target="tpu_custom_call" | custom-call | flops 20000000 | bytes 60000 | tf_op jit(solution)/shard_map/pallas_call | solution.py:457
  54.8 1.7 %collective-permute-start.14 = (f32[4,128]{1,0:T(4,128)S(1)}, f32[4,128]{1,0:T(4,128)S(1)}, u32[]{:S(2)}, u32[]{:S(2)}) collective-permute-start(f32[4,128]{1,0:T(4,128)S(1)} %get-tuple-element.45.refs_0_), channel_id=1, source_target_pairs={{0,2},{1,3},{2,0},{3,1},{4,6},{5,7},{6,4},{7,5},{8,10},{9,11},{10,... | collective-permute-start | bytes 6152 | tf_op jit(solution)/shard_map/ppermute | solution.py:318
  56.7 1.7 %collective-permute-done.14.refs_2_ = f32[4,128]{1,0:T(4,128)S(1)} collective-permute-done((f32[4,128]{1,0:T(4,128)S(1)}, f32[4,128]{1,0:T(4,128)S(1)}, u32[]{:S(2)}, u32[]{:S(2)}) %collective-permute-start.14) | collective-permute-done | bytes 2080 | tf_op jit(solution)/shard_map/ppermute | solution.py:318
  58.4 1.1 %collective-permute-done.15.refs_3_ = f32[4,128]{1,0:T(4,128)S(1)} collective-permute-done((f32[4,128]{1,0:T(4,128)S(1)}, f32[4,128]{1,0:T(4,128)S(1)}, u32[]{:S(2)}, u32[]{:S(2)}) %collective-permute-start.15) | collective-permute-done | bytes 2080 | tf_op jit(solution)/shard_map/ppermute | solution.py:318
  59.5 0.7 %shard_map.93 = f32[64,256]{1,0:T(8,128)} custom-call(f32[64,256]{1,0:T(8,128)S(1)} %get-tuple-element.44.merged_ref, f32[4,128]{1,0:T(4,128)S(1)} %get-tuple-element.45.refs_0_, f32[4,128]{1,0:T(4,128)S(1)} %collective-permute-done.13.refs_1_, f32[4,128]{1,0:T(4,128)S(1)} %collective-permute-done.14.refs_2_, f32[4,128]{1,0:T(4,128)S(1)} %collective-permute-done.15.refs_3_), custom_call_target="tpu_custom_call" | custom-call | flops 10000000 | bytes 30000 | tf_op jit(solution)/shard_map/pallas_call | solution.py:472
  (43 shorter events, 4.2 us)
Async XLA Ops:
  0.6 9.4 %copy-start = (bf16[64,4096]{1,0:T(8,128)(2,1)S(1)}, bf16[64,4096]{1,0:T(8,128)(2,1)}, u32[]{:S(2)}) copy-start(bf16[64,4096]{1,0:T(8,128)(2,1)} %refs_0_.3) | copy-start | bytes 1572868
  0.6 5.4 %copy-start.3 = (f32[3,4096]{1,0:T(4,128)S(1)}, f32[3,4096]{1,0:T(4,128)}, u32[]{:S(2)}) copy-start(f32[3,4096]{1,0:T(4,128)} %param.7) | copy-start | bytes 147460
  0.6 11.8 %collective-permute-start = (bf16[64,4096]{1,0:T(8,128)(2,1)}, bf16[64,4096]{1,0:T(8,128)(2,1)S(1)}, u32[]{:S(2)}, u32[]{:S(2)}) collective-permute-start(bf16[64,4096]{1,0:T(8,128)(2,1)} %refs_0_.3), channel_id=1, source_target_pairs={{0,1},{1,0},{2,3},{3,2},{4,5},{5,4},{6,7},{7,6},{8,9},{9,8},{10,11... | collective-permute-start | bytes 1572872 | tf_op jit(solution)/shard_map/ppermute | solution.py:318
  1.2 4.9 %copy-start.4 = (f32[4096]{0:T(1024)S(1)}, f32[4096]{0:T(1024)}, u32[]{:S(2)}) copy-start(f32[4096]{0:T(1024)} %param.8) | copy-start | bytes 49156
  2.3 3.7 %copy-start.6 = (s32[2,64]{1,0:T(2,128)S(1)}, s32[2,64]{1,0:T(2,128)}, u32[]{:S(2)}) copy-start(s32[2,64]{1,0:T(2,128)} %param.11) | copy-start | bytes 1540
  2.3 23.5 %collective-permute-start.4 = (bf16[32,4096]{1,0:T(8,128)(2,1)S(1)}, bf16[32,4096]{1,0:T(8,128)(2,1)S(1)}, u32[]{:S(2)}, u32[]{:S(2)}) collective-permute-start(bf16[32,4096]{1,0:T(8,128)(2,1)S(1)} %get-tuple-element.24), channel_id=1, source_target_pairs={{0,16},{4,20},{8,24},{12,28},{16,0},{20,4},{24,8},{28,12},{1,17},{... | collective-permute-start | bytes 786440 | tf_op jit(solution)/shard_map/ppermute | solution.py:318
  6.1 21.6 %collective-permute-start.2 = (f32[4,4128]{1,0:T(4,128)S(1)}, f32[4,4128]{1,0:T(4,128)S(1)}, u32[]{:S(2)}, u32[]{:S(2)}) collective-permute-start(f32[4,4128]{1,0:T(4,128)S(1)} %pad_maximum_fusion.refs_0_), channel_id=1, source_target_pairs={{0,16},{1,5},{2,18},{3,7},{4,20},{5,1},{6,22},{7,3},{8,24},{9,13},... | collective-permute-start | bytes 198152 | tf_op jit(solution)/shard_map/ppermute | solution.py:341
  6.8 23.2 %collective-permute-start.3 = (f32[4,4128]{1,0:T(4,128)S(1)}, f32[4,4128]{1,0:T(4,128)S(1)}, u32[]{:S(2)}, u32[]{:S(2)}) collective-permute-start(f32[4,4128]{1,0:T(4,128)S(1)} %pad_maximum_fusion.refs_0_), channel_id=1, source_target_pairs={{0,20},{1,9},{2,22},{3,11},{4,16},{5,13},{6,18},{7,15},{8,28},{9,1... | collective-permute-start | bytes 198152 | tf_op jit(solution)/shard_map/ppermute | solution.py:341
  10.1 15.8 %collective-permute-start.7 = (bf16[64,4096]{1,0:T(8,128)(2,1)S(1)}, bf16[64,4096]{1,0:T(8,128)(2,1)S(1)}, u32[]{:S(2)}, u32[]{:S(2)}) collective-permute-start(bf16[64,4096]{1,0:T(8,128)(2,1)S(1)} %copy-done), channel_id=1, source_target_pairs={{0,4},{4,0},{8,12},{12,8},{16,20},{20,16},{24,28},{28,24},{1,5},{5... | collective-permute-start | bytes 1572872 | tf_op jit(solution)/shard_map/ppermute | solution.py:318
  10.6 0.7 %copy-start.5 = (s32[32,24]{0,1:T(8,128)S(1)}, s32[32,24]{0,1:T(8,128)}, u32[]{:S(2)}) copy-start(s32[32,24]{0,1:T(8,128)} %param.10) | copy-start | bytes 9220
  12.5 21.6 %collective-permute-start.9 = (bf16[32,4096]{1,0:T(8,128)(2,1)S(1)}, bf16[32,4096]{1,0:T(8,128)(2,1)S(1)}, u32[]{:S(2)}, u32[]{:S(2)}) collective-permute-start(bf16[32,4096]{1,0:T(8,128)(2,1)S(1)} %get-tuple-element.25), channel_id=1, source_target_pairs={{0,16},{4,20},{8,24},{12,28},{16,0},{20,4},{24,8},{28,12},{1,17},{... | collective-permute-start | bytes 786440 | tf_op jit(solution)/shard_map/ppermute | solution.py:318
  25.8 8.6 %collective-permute-start.8 = (bf16[32,4096]{1,0:T(8,128)(2,1)S(1)}, bf16[32,4096]{1,0:T(8,128)(2,1)S(1)}, u32[]{:S(2)}, u32[]{:S(2)}) collective-permute-start(bf16[32,4096]{1,0:T(8,128)(2,1)S(1)} %collective-permute-done.4.refs_2_), channel_id=1, source_target_pairs={{0,4},{4,0},{8,12},{12,8},{16,20},{20,16},{24,28},{28,24},{1,5},{5... | collective-permute-start | bytes 786440 | tf_op jit(solution)/shard_map/ppermute | solution.py:318
  29.9 1.3 %collective-permute-start.5 = (f32[4,4128]{1,0:T(4,128)S(1)}, f32[4,4128]{1,0:T(4,128)S(1)}, u32[]{:S(2)}, u32[]{:S(2)}) collective-permute-start(f32[4,4128]{1,0:T(4,128)S(1)} %collective-permute-done.2.refs_1_), channel_id=1, source_target_pairs={{0,1},{1,0},{2,3},{3,2},{4,5},{5,4},{6,7},{7,6},{8,9},{9,8},{10,11... | collective-permute-start | bytes 198152 | tf_op jit(solution)/shard_map/ppermute | solution.py:318
  29.9 1.4 %collective-permute-start.6 = (f32[4,4128]{1,0:T(4,128)S(1)}, f32[4,4128]{1,0:T(4,128)S(1)}, u32[]{:S(2)}, u32[]{:S(2)}) collective-permute-start(f32[4,4128]{1,0:T(4,128)S(1)} %collective-permute-done.3.refs_2_), channel_id=1, source_target_pairs={{0,1},{1,0},{2,3},{3,2},{4,5},{5,4},{6,7},{7,6},{8,9},{9,8},{10,11... | collective-permute-start | bytes 198152 | tf_op jit(solution)/shard_map/ppermute | solution.py:318
  34.4 8.3 %collective-permute-start.10 = (bf16[32,4096]{1,0:T(8,128)(2,1)S(1)}, bf16[32,4096]{1,0:T(8,128)(2,1)S(1)}, u32[]{:S(2)}, u32[]{:S(2)}) collective-permute-start(bf16[32,4096]{1,0:T(8,128)(2,1)S(1)} %collective-permute-done.9.refs_2_), channel_id=1, source_target_pairs={{0,4},{4,0},{8,12},{12,8},{16,20},{20,16},{24,28},{28,24},{1,5},{5... | collective-permute-start | bytes 786440 | tf_op jit(solution)/shard_map/ppermute | solution.py:318
  35.4 12.1 %collective-permute-start.1 = (f32[64,2048]{1,0:T(8,128)S(1)}, f32[64,2048]{1,0:T(8,128)S(1)}, u32[]{:S(2)}, u32[]{:S(2)}) collective-permute-start(f32[64,2048]{1,0:T(8,128)S(1)} %get-tuple-element.30), channel_id=1, source_target_pairs={{0,1},{1,0},{2,3},{3,2},{4,5},{5,4},{6,7},{7,6},{8,9},{9,8},{10,11... | collective-permute-start | bytes 1572872 | tf_op jit(solution)/shard_map/ppermute | solution.py:318
  38.7 7.4 %copy-start.1 = (bf16[4,256,64]{1,2,0:T(8,128)(2,1)S(1)}, bf16[4,256,64]{1,2,0:T(8,128)(2,1)}, u32[]{:S(2)}) copy-start(bf16[4,256,64]{1,2,0:T(8,128)(2,1)} %param.13) | copy-start | bytes 393220
  38.7 8.8 %collective-permute-start.11 = (bf16[32,4096]{1,0:T(8,128)(2,1)S(1)}, bf16[32,4096]{1,0:T(8,128)(2,1)S(1)}, u32[]{:S(2)}, u32[]{:S(2)}) collective-permute-start(bf16[32,4096]{1,0:T(8,128)(2,1)S(1)} %bitcast.17), channel_id=1, source_target_pairs={{0,8},{4,12},{8,0},{12,4},{16,24},{20,28},{24,16},{28,20},{1,9},{5... | collective-permute-start | bytes 786440 | tf_op jit(solution)/shard_map/ppermute | solution.py:318
  42.7 3.4 %copy-start.2 = (s32[32,32]{1,0:T(8,128)S(1)}, s32[32,32]{1,0:T(8,128)}, u32[]{:S(2)}) copy-start(s32[32,32]{1,0:T(8,128)} %skel_ref.1) | copy-start | bytes 12292
  46.0 7.5 %collective-permute-start.12 = (bf16[32,4096]{1,0:T(8,128)(2,1)S(1)}, bf16[32,4096]{1,0:T(8,128)(2,1)S(1)}, u32[]{:S(2)}, u32[]{:S(2)}) collective-permute-start(bf16[32,4096]{1,0:T(8,128)(2,1)S(1)} %bitcast.18), channel_id=1, source_target_pairs={{0,8},{4,12},{8,0},{12,4},{16,24},{20,28},{24,16},{28,20},{1,9},{5... | collective-permute-start | bytes 786440 | tf_op jit(solution)/shard_map/ppermute | solution.py:318
  54.8 1.9 %collective-permute-start.13 = (f32[4,128]{1,0:T(4,128)S(1)}, f32[4,128]{1,0:T(4,128)S(1)}, u32[]{:S(2)}, u32[]{:S(2)}) collective-permute-start(f32[4,128]{1,0:T(4,128)S(1)} %get-tuple-element.45.refs_0_), channel_id=1, source_target_pairs={{0,1},{1,0},{2,3},{3,2},{4,5},{5,4},{6,7},{7,6},{8,9},{9,8},{10,11... | collective-permute-start | bytes 6152 | tf_op jit(solution)/shard_map/ppermute | solution.py:318
  54.8 3.6 %collective-permute-start.14 = (f32[4,128]{1,0:T(4,128)S(1)}, f32[4,128]{1,0:T(4,128)S(1)}, u32[]{:S(2)}, u32[]{:S(2)}) collective-permute-start(f32[4,128]{1,0:T(4,128)S(1)} %get-tuple-element.45.refs_0_), channel_id=1, source_target_pairs={{0,2},{1,3},{2,0},{3,1},{4,6},{5,7},{6,4},{7,5},{8,10},{9,11},{10,... | collective-permute-start | bytes 6152 | tf_op jit(solution)/shard_map/ppermute | solution.py:318
  56.5 3.0 %collective-permute-start.15 = (f32[4,128]{1,0:T(4,128)S(1)}, f32[4,128]{1,0:T(4,128)S(1)}, u32[]{:S(2)}, u32[]{:S(2)}) collective-permute-start(f32[4,128]{1,0:T(4,128)S(1)} %get-tuple-element.45.refs_0_), channel_id=1, source_target_pairs={{0,3},{1,2},{2,1},{3,0},{4,7},{5,6},{6,5},{7,4},{8,11},{9,10},{10,... | collective-permute-start | bytes 6152 | tf_op jit(solution)/shard_map/ppermute | solution.py:318

commit v7 on v6

--- a/solution.py
+++ b/solution.py
@@ -251,7 +251,7 @@
 
 def merge_body(n_chunk, side_ref, mine_ref, theirs_ref, *refs):
     owns, arrived = refs[:n_chunk], refs[n_chunk : 2 * n_chunk]
-    pick_ref, near_ref, merged_ref, energy_ref = refs[2 * n_chunk :]
+    pick_ref, merged_ref, energy_ref, near_ref = refs[2 * n_chunk :]
     width = mine_ref.shape[1]
     for half in range(SHARE):
         columns = slice(half * width, (half + 1) * width)
@@ -276,6 +276,26 @@
             jnp.sum(jnp.sum(merged * merged, axis=0, keepdims=True), axis=1, keepdims=True),
             (1, LEAF_PTS),
         )
+
+
+def near_rows(half, rows, side_ref, mine_ref, theirs_ref, own_ref, arrived_ref):
+    width = mine_ref.shape[1]
+    columns = slice(half * width, (half + 1) * width)
+    local = jnp.where(side_ref[0] == half, mine_ref[rows, :], theirs_ref[rows, :])
+    return local + own_ref[:, columns] + arrived_ref[:, columns].astype(jnp.float32)
+
+
+def near_body(n_chunk, side_ref, mine_ref, theirs_ref, *refs):
+    owns, arrived, near_ref = refs[:n_chunk], refs[n_chunk : 2 * n_chunk], refs[-1]
+    width = mine_ref.shape[1]
+    for half in range(SHARE):
+        first = 0
+        for own_ref, arrived_ref in zip(owns, arrived):
+            rows = slice(first, first + own_ref.shape[0])
+            first += own_ref.shape[0]
+            near_ref[rows, half * width : (half + 1) * width] = near_rows(
+                half, rows, side_ref, mine_ref, theirs_ref, own_ref, arrived_ref
+            )
 
 
 def scale_body(count, merged_ref, *refs):
@@ -454,21 +474,27 @@
         jax.ShapeDtypeStruct((parent_dev, SK2, CHILD * LEAF_PTS), jnp.bfloat16),
         [VMEM] * 2,
     )(skel_rows, parent_interp.transpose(0, 2, 1))
-    near, merged, energy = call(
+    merged, energy = call(
         functools.partial(merge_body, len(chunks)),
         [
-            jax.ShapeDtypeStruct((probe_dev, points), jnp.float32),
             jax.ShapeDtypeStruct((probe_dev, parent_dev * SK2), jnp.float32),
             jax.ShapeDtypeStruct((parent_dev, LEAF_PTS), jnp.float32),
         ],
         [SMEM] + [VMEM] * (2 * len(chunks) + 3),
+        [pltpu.VMEM((probe_dev, points), jnp.float32)],
         micros=2.0,
     )(side, mine, theirs, *owns, *arrived, pick)
+    near = call(
+        functools.partial(near_body, len(chunks)),
+        jax.ShapeDtypeStruct((probe_dev, points), jnp.float32),
+        [SMEM] + [VMEM] * (2 + 2 * len(chunks)),
+    )(side, mine, theirs, *owns, *arrived)
     n_probe = lax.axis_size("probe")
     if n_probe & (n_probe - 1):
         energies = [lax.psum(energy, "probe")]
     else:
         energies = [energy] + [exchange(energy, "probe", k) for k in range(1, n_probe)]
+    near, merged = lax.optimization_barrier((near, merged))
     parent = call(
         functools.partial(scale_body, float(SK2 * probe_dev * n_probe)),
         jax.ShapeDtypeStruct((probe_dev, parent_dev * SK2), jnp.float32),

time: 60.5 us -> 59.5 us (0.983)
  waiting for transfers between devices: 18.5 us -> 17.3 us
    pallas_call x0 -> x1, Pallas kernels: none -> 1.2 us  [per_device(): call(functools.partial(near_body, len(chunks)), jax.ShapeDtypeStruct((pro...]
    ppermute x14, waiting for transfers between devices: 16.3 us -> 15.2 us  [exchange(): return lax.ppermute(array, axis, [(i, i ^ bit) for i in range(size)])]
    pallas_call x1, Pallas kernels: 1.29 us -> 0.5 us  [per_device(): call(functools.partial(merge_body, len(chunks)), [jax.ShapeDtypeStruct((p...]
  transfers between devices with their start and end apart: 16 -> 16, of which waited for: 10 -> 10; matrix products, arithmetic and copies ran while one was open for 3% -> 3% of each run, Pallas kernels for 35% -> 38%
where the time goes in v7:
time: 59.5 us; the launch traced here: 59.6 us
  Pallas kernels  23.8 us (40%)
  waiting for transfers between devices  17.3 us (29%)
  starting transfers between devices  15.3 us (26%)
  local copies, waits for them, and re-layouts  1.94 us (3%)
  between operations  0.78 us (1%)
    ppermute x14, waiting for transfers between devices, exchange(): return lax.ppermute(array, axis, [(i, i ^ bit) for i in range(size)])  15.2 us
    ppermute x14, starting transfers between devices, exchange(): return lax.ppermute(array, axis, [(i, i ^ bit) for i in range(size)])  11.4 us
    pallas_call x1, Pallas kernels, per_device(): call(local_body, [jax.ShapeDtypeStruct((probe_dev, share_points), jnp.flo...  10.4 us
    pallas_call x2, Pallas kernels, per_device(): call(functools.partial(far_body, first), [jax.ShapeDtypeStruct((size, poi...  6.62 us
    ppermute x2, starting transfers between devices, gather_bundles(): bundles.append(lax.ppermute(sent, ('leaf', 'probe'), pairs))  3.95 us
    pallas_call x1, Pallas kernels, per_device(): call(functools.partial(far_prepare_body, len(bundles), top | low), [jax.S...  2.71 us
    ppermute x2, waiting for transfers between devices, gather_bundles(): bundles.append(lax.ppermute(sent, ('leaf', 'probe'), pairs))  2.18 us
    pallas_call x1, Pallas kernels, per_device(): call(functools.partial(near_body, len(chunks)), jax.ShapeDtypeStruct((pro...  1.2 us
  transfers between devices with their start and end apart: 16, of which 10 were waited for; matrix products, arithmetic and copies ran while one was open for 3% of the time, Pallas kernels for 38%

profile of v7, /device:TPU:0, one launch (start us, length us, event | category | flops | bytes accessed | tf_op | source)
XLA Modules:
  0.0 59.6 jit_solution(12958600170358921012)
XLA Ops:
  1.2 1.1 %fusion.7 = (bf16[32,4096]{1,0:T(8,128)(2,1)S(1)}, bf16[32,4096]{1,0:T(8,128)(2,1)S(1)}) fusion(bf16[64,4096]{1,0:T(8,128)(2,1)} %refs_0_.3), kind=kLoop, calls=%fused_computation.26 | loop fusion | bytes 1048576 | tf_op jit(solution)/shard_map/slice | solution.py:392
  2.3 3.7 %collective-permute-start.4 = (bf16[32,4096]{1,0:T(8,128)(2,1)S(1)}, bf16[32,4096]{1,0:T(8,128)(2,1)S(1)}, u32[]{:S(2)}, u32[]{:S(2)}) collective-permute-start(bf16[32,4096]{1,0:T(8,128)(2,1)S(1)} %get-tuple-element.25), channel_id=1, source_target_pairs={{0,16},{4,20},{8,24},{12,28},{16,0},{20,4},{24,8},{28,12},{1,17},{... | collective-permute-start | bytes 786440 | tf_op jit(solution)/shard_map/ppermute | solution.py:338
  6.1 0.7 %collective-permute-start.2 = (f32[4,4128]{1,0:T(4,128)S(1)}, f32[4,4128]{1,0:T(4,128)S(1)}, u32[]{:S(2)}, u32[]{:S(2)}) collective-permute-start(f32[4,4128]{1,0:T(4,128)S(1)} %pad_maximum_fusion.refs_0_), channel_id=1, source_target_pairs={{0,16},{1,5},{2,18},{3,7},{4,20},{5,1},{6,22},{7,3},{8,24},{9,13},... | collective-permute-start | bytes 198152 | tf_op jit(solution)/shard_map/ppermute | solution.py:361
  6.8 3.3 %collective-permute-start.3 = (f32[4,4128]{1,0:T(4,128)S(1)}, f32[4,4128]{1,0:T(4,128)S(1)}, u32[]{:S(2)}, u32[]{:S(2)}) collective-permute-start(f32[4,4128]{1,0:T(4,128)S(1)} %pad_maximum_fusion.refs_0_), channel_id=1, source_target_pairs={{0,20},{1,9},{2,22},{3,11},{4,16},{5,13},{6,18},{7,15},{8,28},{9,1... | collective-permute-start | bytes 198152 | tf_op jit(solution)/shard_map/ppermute | solution.py:361
  11.3 1.0 %shard_map.86 = (bf16[32,4096]{1,0:T(8,128)(2,1)S(1)}, bf16[32,4224]{1,0:T(8,128)(2,1)S(1)}) custom-call(s32[2,1]{1,0:T(2,128)S(1)} %broadcast_15_place_ref.2.place_ref, f32[4,4128]{1,0:T(4,128)S(1)} %pad_maximum_fusion.refs_0_), custom_call_target="tpu_custom_call" | custom-call | flops 10000000 | bytes 30000 | tf_op jit(solution)/shard_map/pallas_call | solution.py:325
  12.5 0.6 %collective-permute-start.9 = (bf16[32,4096]{1,0:T(8,128)(2,1)S(1)}, bf16[32,4096]{1,0:T(8,128)(2,1)S(1)}, u32[]{:S(2)}, u32[]{:S(2)}) collective-permute-start(bf16[32,4096]{1,0:T(8,128)(2,1)S(1)} %get-tuple-element.26), channel_id=1, source_target_pairs={{0,16},{4,20},{8,24},{12,28},{16,0},{20,4},{24,8},{28,12},{1,17},{... | collective-permute-start | bytes 786440 | tf_op jit(solution)/shard_map/ppermute | solution.py:338
  13.1 10.4 %shard_map.87 = (f32[64,2048]{1,0:T(8,128)S(1)}, f32[64,2048]{1,0:T(8,128)S(1)}) custom-call(s32[2]{0:T(128)S(1)} %pad_add_fusion.3.place_ref, s32[32,24]{1,0:T(8,128)S(1)} %copy.9.near_ref, bf16[32,4224]{1,0:T(8,128)(2,1)S(1)} %get-tuple-element.28.target_ref, bf16[32,4096]{1,0:T(8,128)(2,1)S(1)} %get-tuple-element.29.source_ref, ...), custom_call_target="tpu_custom_call" | custom-call | flops 100000000 | bytes 300000 | tf_op jit(solution)/shard_map/pallas_call | solution.py:407
  23.5 2.3 %collective-permute-done.4.refs_2_ = bf16[32,4096]{1,0:T(8,128)(2,1)S(1)} collective-permute-done((bf16[32,4096]{1,0:T(8,128)(2,1)S(1)}, bf16[32,4096]{1,0:T(8,128)(2,1)S(1)}, u32[]{:S(2)}, u32[]{:S(2)}) %collective-permute-start.4) | collective-permute-done | bytes 262176 | tf_op jit(solution)/shard_map/ppermute | solution.py:338
  25.8 1.8 %collective-permute-start.8 = (bf16[32,4096]{1,0:T(8,128)(2,1)S(1)}, bf16[32,4096]{1,0:T(8,128)(2,1)S(1)}, u32[]{:S(2)}, u32[]{:S(2)}) collective-permute-start(bf16[32,4096]{1,0:T(8,128)(2,1)S(1)} %collective-permute-done.4.refs_2_), channel_id=1, source_target_pairs={{0,4},{4,0},{8,12},{12,8},{16,20},{20,16},{24,28},{28,24},{1,5},{5... | collective-permute-start | bytes 786440 | tf_op jit(solution)/shard_map/ppermute | solution.py:338
  27.7 2.2 %collective-permute-done.3.refs_2_ = f32[4,4128]{1,0:T(4,128)S(1)} collective-permute-done((f32[4,4128]{1,0:T(4,128)S(1)}, f32[4,4128]{1,0:T(4,128)S(1)}, u32[]{:S(2)}, u32[]{:S(2)}) %collective-permute-start.3) | collective-permute-done | bytes 66080 | tf_op jit(solution)/shard_map/ppermute | solution.py:361
  30.5 0.7 %collective-permute-done.5.refs_3_ = f32[4,4128]{1,0:T(4,128)S(1)} collective-permute-done((f32[4,4128]{1,0:T(4,128)S(1)}, f32[4,4128]{1,0:T(4,128)S(1)}, u32[]{:S(2)}, u32[]{:S(2)}) %collective-permute-start.5) | collective-permute-done | bytes 66080 | tf_op jit(solution)/shard_map/ppermute | solution.py:338
  31.3 2.7 %shard_map.88 = (bf16[32,16384]{1,0:T(8,128)(2,1)S(1)}, bf16[32,8320]{1,0:T(8,128)(2,1)S(1)}, s32[2,144]{1,0:T(2,128)S(1)}) custom-call(s32[4,5]{1,0:T(4,128)S(1)} %add_add_fusion.place_ref, f32[4,4128]{1,0:T(4,128)S(1)} %pad_maximum_fusion.refs_0_, f32[4,4128]{1,0:T(4,128)S(1)} %collective-permute-done.2.refs_1_, ...), custom_call_target="tpu_custom_call" | custom-call | flops 10000000 | bytes 30000 | tf_op jit(solution)/shard_map/pallas_call | solution.py:423
  34.4 1.0 %collective-permute-start.10 = (bf16[32,4096]{1,0:T(8,128)(2,1)S(1)}, bf16[32,4096]{1,0:T(8,128)(2,1)S(1)}, u32[]{:S(2)}, u32[]{:S(2)}) collective-permute-start(bf16[32,4096]{1,0:T(8,128)(2,1)S(1)} %collective-permute-done.9.refs_2_), channel_id=1, source_target_pairs={{0,4},{4,0},{8,12},{12,8},{16,20},{20,16},{24,28},{28,24},{1,5},{5... | collective-permute-start | bytes 786440 | tf_op jit(solution)/shard_map/ppermute | solution.py:338
  35.4 3.3 %shard_map.89 = (f32[32,4096]{1,0:T(8,128)S(1)}, bf16[1,32,4096]{2,1,0:T(8,128)(2,1)S(1)}) custom-call(s32[2,144]{1,0:T(2,128)S(1)} %get-tuple-element.34.table_ref, bf16[32,16384]{1,0:T(8,128)(2,1)S(1)} %get-tuple-element.35.source_ref, bf16[32,8320]{1,0:T(8,128)(2,1)S(1)} %get-tuple-element.36.target_ref, bf16[64,4096]{1,0:T(8,128)(2,1)S(1)} %copy-done, ...), custom_call_target="tpu_custom_call" | custom-call | flops 40000000 | bytes 120000 | tf_op jit(solution)/shard_map/pallas_call | solution.py:446
  38.7 0.8 %collective-permute-start.11 = (bf16[32,4096]{1,0:T(8,128)(2,1)S(1)}, bf16[32,4096]{1,0:T(8,128)(2,1)S(1)}, u32[]{:S(2)}, u32[]{:S(2)}) collective-permute-start(bf16[32,4096]{1,0:T(8,128)(2,1)S(1)} %bitcast.17), channel_id=1, source_target_pairs={{0,8},{4,12},{8,0},{12,4},{16,24},{20,28},{24,16},{28,20},{1,9},{5... | collective-permute-start | bytes 786440 | tf_op jit(solution)/shard_map/ppermute | solution.py:338
  39.5 3.2 %collective-permute-done.10.refs_3_ = bf16[32,4096]{1,0:T(8,128)(2,1)S(1)} collective-permute-done((bf16[32,4096]{1,0:T(8,128)(2,1)S(1)}, bf16[32,4096]{1,0:T(8,128)(2,1)S(1)}, u32[]{:S(2)}, u32[]{:S(2)}) %collective-permute-start.10) | collective-permute-done | bytes 262176 | tf_op jit(solution)/shard_map/ppermute | solution.py:338
  42.7 3.3 %shard_map.90 = (f32[32,4096]{1,0:T(8,128)S(1)}, bf16[1,32,4096]{2,1,0:T(8,128)(2,1)S(1)}) custom-call(s32[2,144]{1,0:T(2,128)S(1)} %get-tuple-element.34.table_ref, bf16[32,16384]{1,0:T(8,128)(2,1)S(1)} %get-tuple-element.35.source_ref, bf16[32,8320]{1,0:T(8,128)(2,1)S(1)} %get-tuple-element.36.target_ref, bf16[64,4096]{1,0:T(8,128)(2,1)S(1)} %copy-done, ...), custom_call_target="tpu_custom_call" | custom-call | flops 40000000 | bytes 120000 | tf_op jit(solution)/shard_map/pallas_call | solution.py:446
  46.1 0.6 %shard_map.92.refs_4_ = bf16[4,64,1024]{2,1,0:T(8,128)(2,1)S(1)} custom-call(s32[32,32]{1,0:T(8,128)S(1)} %copy-done.2, bf16[4,64,256]{2,1,0:T(8,128)(2,1)S(1)} %bitcast.16), custom_call_target="tpu_custom_call" | custom-call | flops 10000000 | bytes 30000 | tf_op jit(solution)/shard_map/pallas_call | solution.py:472
  46.8 0.8 %collective-permute-done.11.refs_2_ = bf16[32,4096]{1,0:T(8,128)(2,1)S(1)} collective-permute-done((bf16[32,4096]{1,0:T(8,128)(2,1)S(1)}, bf16[32,4096]{1,0:T(8,128)(2,1)S(1)}, u32[]{:S(2)}, u32[]{:S(2)}) %collective-permute-start.11) | collective-permute-done | bytes 262176 | tf_op jit(solution)/shard_map/ppermute | solution.py:338
  47.5 6.0 %collective-permute-done.12.refs_3_ = bf16[32,4096]{1,0:T(8,128)(2,1)S(1)} collective-permute-done((bf16[32,4096]{1,0:T(8,128)(2,1)S(1)}, bf16[32,4096]{1,0:T(8,128)(2,1)S(1)}, u32[]{:S(2)}, u32[]{:S(2)}) %collective-permute-start.12) | collective-permute-done | bytes 262176 | tf_op jit(solution)/shard_map/ppermute | solution.py:338
  54.1 1.7 %collective-permute-start.14 = (f32[4,128]{1,0:T(4,128)S(1)}, f32[4,128]{1,0:T(4,128)S(1)}, u32[]{:S(2)}, u32[]{:S(2)}) collective-permute-start(f32[4,128]{1,0:T(4,128)S(1)} %get-tuple-element.47.refs_0_), channel_id=1, source_target_pairs={{0,2},{1,3},{2,0},{3,1},{4,6},{5,7},{6,4},{7,5},{8,10},{9,11},{10,... | collective-permute-start | bytes 6152 | tf_op jit(solution)/shard_map/ppermute | solution.py:338
  56.0 1.2 %shard_map.91 = f32[64,4096]{1,0:T(8,128)} custom-call(s32[1]{0:T(128)} %bitcast.side_ref, f32[64,2048]{1,0:T(8,128)S(1)} %get-tuple-element.30.mine_ref, f32[64,2048]{1,0:T(8,128)S(1)} %collective-permute-done.1.theirs_ref, f32[32,4096]{1,0:T(8,128)S(1)} %get-tuple-element.39.refs_0_, f32[32,4096]{1,0:T(8,128)S(1)} %get-tuple-element.41.refs_1_, ...), custom_call_target="tpu_custom_call" | custom-call | flops 10000000 | bytes 30000 | tf_op jit(solution)/shard_map/pallas_call | solution.py:487
  57.8 1.1 %collective-permute-done.15.refs_3_ = f32[4,128]{1,0:T(4,128)S(1)} collective-permute-done((f32[4,128]{1,0:T(4,128)S(1)}, f32[4,128]{1,0:T(4,128)S(1)}, u32[]{:S(2)}, u32[]{:S(2)}) %collective-permute-start.15) | collective-permute-done | bytes 2080 | tf_op jit(solution)/shard_map/ppermute | solution.py:338
  58.9 0.7 %shard_map.94 = f32[64,256]{1,0:T(8,128)} custom-call(f32[64,256]{1,0:T(8,128)S(1)} %get-tuple-element.46.merged_ref, f32[4,128]{1,0:T(4,128)S(1)} %get-tuple-element.47.refs_0_, f32[4,128]{1,0:T(4,128)S(1)} %collective-permute-done.13.refs_1_, f32[4,128]{1,0:T(4,128)S(1)} %collective-permute-done.14.refs_2_, f32[4,128]{1,0:T(4,128)S(1)} %collective-permute-done.15.refs_3_), custom_call_target="tpu_custom_call" | custom-call | flops 10000000 | bytes 30000 | tf_op jit(solution)/shard_map/pallas_call | solution.py:498
  (44 shorter events, 4.7 us)
Async XLA Ops:
  0.6 9.4 %copy-start = (bf16[64,4096]{1,0:T(8,128)(2,1)S(1)}, bf16[64,4096]{1,0:T(8,128)(2,1)}, u32[]{:S(2)}) copy-start(bf16[64,4096]{1,0:T(8,128)(2,1)} %refs_0_.3) | copy-start | bytes 1572868
  0.6 5.4 %copy-start.3 = (f32[3,4096]{1,0:T(4,128)S(1)}, f32[3,4096]{1,0:T(4,128)}, u32[]{:S(2)}) copy-start(f32[3,4096]{1,0:T(4,128)} %param.7) | copy-start | bytes 147460
  0.6 11.8 %collective-permute-start = (bf16[64,4096]{1,0:T(8,128)(2,1)}, bf16[64,4096]{1,0:T(8,128)(2,1)S(1)}, u32[]{:S(2)}, u32[]{:S(2)}) collective-permute-start(bf16[64,4096]{1,0:T(8,128)(2,1)} %refs_0_.3), channel_id=1, source_target_pairs={{0,1},{1,0},{2,3},{3,2},{4,5},{5,4},{6,7},{7,6},{8,9},{9,8},{10,11... | collective-permute-start | bytes 1572872 | tf_op jit(solution)/shard_map/ppermute | solution.py:338
  1.2 4.9 %copy-start.4 = (f32[4096]{0:T(1024)S(1)}, f32[4096]{0:T(1024)}, u32[]{:S(2)}) copy-start(f32[4096]{0:T(1024)} %param.8) | copy-start | bytes 49156
  2.3 3.7 %copy-start.6 = (s32[2,64]{1,0:T(2,128)S(1)}, s32[2,64]{1,0:T(2,128)}, u32[]{:S(2)}) copy-start(s32[2,64]{1,0:T(2,128)} %param.11) | copy-start | bytes 1540
  2.3 23.5 %collective-permute-start.4 = (bf16[32,4096]{1,0:T(8,128)(2,1)S(1)}, bf16[32,4096]{1,0:T(8,128)(2,1)S(1)}, u32[]{:S(2)}, u32[]{:S(2)}) collective-permute-start(bf16[32,4096]{1,0:T(8,128)(2,1)S(1)} %get-tuple-element.25), channel_id=1, source_target_pairs={{0,16},{4,20},{8,24},{12,28},{16,0},{20,4},{24,8},{28,12},{1,17},{... | collective-permute-start | bytes 786440 | tf_op jit(solution)/shard_map/ppermute | solution.py:338
  6.1 21.6 %collective-permute-start.2 = (f32[4,4128]{1,0:T(4,128)S(1)}, f32[4,4128]{1,0:T(4,128)S(1)}, u32[]{:S(2)}, u32[]{:S(2)}) collective-permute-start(f32[4,4128]{1,0:T(4,128)S(1)} %pad_maximum_fusion.refs_0_), channel_id=1, source_target_pairs={{0,16},{1,5},{2,18},{3,7},{4,20},{5,1},{6,22},{7,3},{8,24},{9,13},... | collective-permute-start | bytes 198152 | tf_op jit(solution)/shard_map/ppermute | solution.py:361
  6.8 23.2 %collective-permute-start.3 = (f32[4,4128]{1,0:T(4,128)S(1)}, f32[4,4128]{1,0:T(4,128)S(1)}, u32[]{:S(2)}, u32[]{:S(2)}) collective-permute-start(f32[4,4128]{1,0:T(4,128)S(1)} %pad_maximum_fusion.refs_0_), channel_id=1, source_target_pairs={{0,20},{1,9},{2,22},{3,11},{4,16},{5,13},{6,18},{7,15},{8,28},{9,1... | collective-permute-start | bytes 198152 | tf_op jit(solution)/shard_map/ppermute | solution.py:361
  10.1 15.8 %collective-permute-start.7 = (bf16[64,4096]{1,0:T(8,128)(2,1)S(1)}, bf16[64,4096]{1,0:T(8,128)(2,1)S(1)}, u32[]{:S(2)}, u32[]{:S(2)}) collective-permute-start(bf16[64,4096]{1,0:T(8,128)(2,1)S(1)} %copy-done), channel_id=1, source_target_pairs={{0,4},{4,0},{8,12},{12,8},{16,20},{20,16},{24,28},{28,24},{1,5},{5... | collective-permute-start | bytes 1572872 | tf_op jit(solution)/shard_map/ppermute | solution.py:338
  10.6 0.7 %copy-start.5 = (s32[32,24]{0,1:T(8,128)S(1)}, s32[32,24]{0,1:T(8,128)}, u32[]{:S(2)}) copy-start(s32[32,24]{0,1:T(8,128)} %param.10) | copy-start | bytes 9220
  12.5 21.6 %collective-permute-start.9 = (bf16[32,4096]{1,0:T(8,128)(2,1)S(1)}, bf16[32,4096]{1,0:T(8,128)(2,1)S(1)}, u32[]{:S(2)}, u32[]{:S(2)}) collective-permute-start(bf16[32,4096]{1,0:T(8,128)(2,1)S(1)} %get-tuple-element.26), channel_id=1, source_target_pairs={{0,16},{4,20},{8,24},{12,28},{16,0},{20,4},{24,8},{28,12},{1,17},{... | collective-permute-start | bytes 786440 | tf_op jit(solution)/shard_map/ppermute | solution.py:338
  25.8 8.6 %collective-permute-start.8 = (bf16[32,4096]{1,0:T(8,128)(2,1)S(1)}, bf16[32,4096]{1,0:T(8,128)(2,1)S(1)}, u32[]{:S(2)}, u32[]{:S(2)}) collective-permute-start(bf16[32,4096]{1,0:T(8,128)(2,1)S(1)} %collective-permute-done.4.refs_2_), channel_id=1, source_target_pairs={{0,4},{4,0},{8,12},{12,8},{16,20},{20,16},{24,28},{28,24},{1,5},{5... | collective-permute-start | bytes 786440 | tf_op jit(solution)/shard_map/ppermute | solution.py:338
  29.9 1.3 %collective-permute-start.5 = (f32[4,4128]{1,0:T(4,128)S(1)}, f32[4,4128]{1,0:T(4,128)S(1)}, u32[]{:S(2)}, u32[]{:S(2)}) collective-permute-start(f32[4,4128]{1,0:T(4,128)S(1)} %collective-permute-done.2.refs_1_), channel_id=1, source_target_pairs={{0,1},{1,0},{2,3},{3,2},{4,5},{5,4},{6,7},{7,6},{8,9},{9,8},{10,11... | collective-permute-start | bytes 198152 | tf_op jit(solution)/shard_map/ppermute | solution.py:338
  29.9 1.4 %collective-permute-start.6 = (f32[4,4128]{1,0:T(4,128)S(1)}, f32[4,4128]{1,0:T(4,128)S(1)}, u32[]{:S(2)}, u32[]{:S(2)}) collective-permute-start(f32[4,4128]{1,0:T(4,128)S(1)} %collective-permute-done.3.refs_2_), channel_id=1, source_target_pairs={{0,1},{1,0},{2,3},{3,2},{4,5},{5,4},{6,7},{7,6},{8,9},{9,8},{10,11... | collective-permute-start | bytes 198152 | tf_op jit(solution)/shard_map/ppermute | solution.py:338
  34.4 8.3 %collective-permute-start.10 = (bf16[32,4096]{1,0:T(8,128)(2,1)S(1)}, bf16[32,4096]{1,0:T(8,128)(2,1)S(1)}, u32[]{:S(2)}, u32[]{:S(2)}) collective-permute-start(bf16[32,4096]{1,0:T(8,128)(2,1)S(1)} %collective-permute-done.9.refs_2_), channel_id=1, source_target_pairs={{0,4},{4,0},{8,12},{12,8},{16,20},{20,16},{24,28},{28,24},{1,5},{5... | collective-permute-start | bytes 786440 | tf_op jit(solution)/shard_map/ppermute | solution.py:338
  35.4 12.1 %collective-permute-start.1 = (f32[64,2048]{1,0:T(8,128)S(1)}, f32[64,2048]{1,0:T(8,128)S(1)}, u32[]{:S(2)}, u32[]{:S(2)}) collective-permute-start(f32[64,2048]{1,0:T(8,128)S(1)} %get-tuple-element.31), channel_id=1, source_target_pairs={{0,1},{1,0},{2,3},{3,2},{4,5},{5,4},{6,7},{7,6},{8,9},{9,8},{10,11... | collective-permute-start | bytes 1572872 | tf_op jit(solution)/shard_map/ppermute | solution.py:338
  38.7 7.4 %copy-start.1 = (bf16[4,256,64]{1,2,0:T(8,128)(2,1)S(1)}, bf16[4,256,64]{1,2,0:T(8,128)(2,1)}, u32[]{:S(2)}) copy-start(bf16[4,256,64]{1,2,0:T(8,128)(2,1)} %param.13) | copy-start | bytes 393220
  38.7 8.8 %collective-permute-start.11 = (bf16[32,4096]{1,0:T(8,128)(2,1)S(1)}, bf16[32,4096]{1,0:T(8,128)(2,1)S(1)}, u32[]{:S(2)}, u32[]{:S(2)}) collective-permute-start(bf16[32,4096]{1,0:T(8,128)(2,1)S(1)} %bitcast.17), channel_id=1, source_target_pairs={{0,8},{4,12},{8,0},{12,4},{16,24},{20,28},{24,16},{28,20},{1,9},{5... | collective-permute-start | bytes 786440 | tf_op jit(solution)/shard_map/ppermute | solution.py:338
  42.7 3.4 %copy-start.2 = (s32[32,32]{1,0:T(8,128)S(1)}, s32[32,32]{1,0:T(8,128)}, u32[]{:S(2)}) copy-start(s32[32,32]{1,0:T(8,128)} %skel_ref.1) | copy-start | bytes 12292
  46.0 7.5 %collective-permute-start.12 = (bf16[32,4096]{1,0:T(8,128)(2,1)S(1)}, bf16[32,4096]{1,0:T(8,128)(2,1)S(1)}, u32[]{:S(2)}, u32[]{:S(2)}) collective-permute-start(bf16[32,4096]{1,0:T(8,128)(2,1)S(1)} %bitcast.18), channel_id=1, source_target_pairs={{0,8},{4,12},{8,0},{12,4},{16,24},{20,28},{24,16},{28,20},{1,9},{5... | collective-permute-start | bytes 786440 | tf_op jit(solution)/shard_map/ppermute | solution.py:338
  54.1 3.1 %collective-permute-start.13 = (f32[4,128]{1,0:T(4,128)S(1)}, f32[4,128]{1,0:T(4,128)S(1)}, u32[]{:S(2)}, u32[]{:S(2)}) collective-permute-start(f32[4,128]{1,0:T(4,128)S(1)} %get-tuple-element.47.refs_0_), channel_id=1, source_target_pairs={{0,1},{1,0},{2,3},{3,2},{4,5},{5,4},{6,7},{7,6},{8,9},{9,8},{10,11... | collective-permute-start | bytes 6152 | tf_op jit(solution)/shard_map/ppermute | solution.py:338
  54.1 3.7 %collective-permute-start.14 = (f32[4,128]{1,0:T(4,128)S(1)}, f32[4,128]{1,0:T(4,128)S(1)}, u32[]{:S(2)}, u32[]{:S(2)}) collective-permute-start(f32[4,128]{1,0:T(4,128)S(1)} %get-tuple-element.47.refs_0_), channel_id=1, source_target_pairs={{0,2},{1,3},{2,0},{3,1},{4,6},{5,7},{6,4},{7,5},{8,10},{9,11},{10,... | collective-permute-start | bytes 6152 | tf_op jit(solution)/shard_map/ppermute | solution.py:338
  55.9 3.0 %collective-permute-start.15 = (f32[4,128]{1,0:T(4,128)S(1)}, f32[4,128]{1,0:T(4,128)S(1)}, u32[]{:S(2)}, u32[]{:S(2)}) collective-permute-start(f32[4,128]{1,0:T(4,128)S(1)} %get-tuple-element.47.refs_0_), channel_id=1, source_target_pairs={{0,3},{1,2},{2,1},{3,0},{4,7},{5,6},{6,5},{7,4},{8,11},{9,10},{10,... | collective-permute-start | bytes 6152 | tf_op jit(solution)/shard_map/ppermute | solution.py:338
